TPU v7x, 256 devices: a whole 4x4x8 slice. The times are simulated.
256 devices in a mesh: dp: 32 (over x, y, core), tensor: 8 (over z).
Axes of the slice: x: 4, y: 4, z: 8, core: 2. Of those that a mesh axis runs over, the one named last changes fastest.
Arguments:
- inputs: bfloat16 [1024, 6144], P('dp'), may hold values from -6 to 6
- norm_gain: float32 [6144], replicated, may hold values from 0.1 to 1.9
- out_grad: bfloat16 [1024, 21504], P('dp', 'tensor'), may hold values from -0.59765625 to 0.59765625
- weight: bfloat16 [6144, 21504], P('dp', 'tensor'), may hold values from -0.078125 to 0.078125
- moment: float32 [6144, 21504], P('dp', 'tensor'), may hold values from -3 to 3
- right_basis: float32 [21504, 512], P(('tensor', 'dp')), may hold values from -0.0390625 to 0.0390625
Outputs:
- input_grad: bfloat16 [1024, 6144], P('dp', 'tensor')
- gain_grad: float32 [6144], P('tensor')
- moment_new: float32 [6144, 21504], P('dp', 'tensor')
- basis_new: float32 [21504, 512], P(('tensor', 'dp'))
- update: float32 [6144, 21504], P('dp', 'tensor')
All inputs are finite; a program needn't handle non-finite values.
Results may differ from a plain program's by a relative error of at most 0.0031.
Values may be sent and summed in bfloat16 or wider, within the bound.
A program may use at most 128 MiB of HBM per device.

v0:
```python
import math

import jax
import jax.numpy as jnp
from jax import lax
from jax.sharding import PartitionSpec as P

D = 6144
HEADS = 24
HEAD_DIM = 128
FF = 12288
RANK = 512


PRECISE = lax.Precision.HIGHEST
MOMENTUM = 0.8
NORM_EPSILON = 1e-06


def per_device(inputs, norm_gain, out_grad, weight, moment, right_basis):
    tensor_count = lax.axis_size("tensor")
    tensor_index = lax.axis_index("tensor")
    width = inputs.shape[1]
    group_cols = weight.shape[1]
    widened = inputs.astype(jnp.float32)
    row_mean = jnp.mean(widened, axis=1, keepdims=True)
    centered = widened - row_mean
    row_var = jnp.mean(centered * centered, axis=1, keepdims=True)
    inv_std = lax.rsqrt(row_var + NORM_EPSILON)
    standard = centered * inv_std
    normed = (standard * norm_gain).astype(jnp.bfloat16)
    feature_block = lax.all_to_all(normed, "dp", split_axis=1, concat_axis=0, tiled=True)
    shard_in = lax.all_gather(out_grad, "dp", axis=0, tiled=True)
    grad_acc = lax.dot_general(
        feature_block, shard_in, (((0,), (0,)), ((), ())), preferred_element_type=jnp.float32
    )
    back_rows = lax.dot_general(
        shard_in, weight, (((1,), (1,)), ((), ())), preferred_element_type=jnp.float32
    )
    back_mine = lax.all_to_all(back_rows, "dp", split_axis=0, concat_axis=1, tiled=True)
    share_cols = width // tensor_count
    offset = tensor_index * share_cols
    normed_grad = lax.psum(back_mine, "tensor")
    scaled_grad = normed_grad * norm_gain
    mean_grad = jnp.mean(scaled_grad, axis=1, keepdims=True)
    mean_proj = jnp.mean(scaled_grad * standard, axis=1, keepdims=True)
    full_grad = inv_std * (scaled_grad - mean_grad - standard * mean_proj)
    input_grad = lax.dynamic_slice_in_dim(full_grad, offset, share_cols, 1).astype(jnp.bfloat16)
    gain_part = lax.dynamic_slice_in_dim(
        jnp.sum(normed_grad * standard, axis=0), offset, share_cols, 0
    )
    gain_grad = lax.psum(gain_part, "dp")
    buffer = moment + grad_acc
    columns = buffer
    projected_part = jnp.dot(
        columns,
        lax.all_gather(right_basis, "dp", axis=0, tiled=True),
        precision=PRECISE,
        preferred_element_type=jnp.float32,
    )
    projected = lax.psum(projected_part, "tensor")
    gram = lax.psum(jnp.dot(projected.T, projected, precision=PRECISE), "dp")
    factor = jnp.linalg.cholesky(gram)
    orthonormal = lax.linalg.triangular_solve(
        factor, projected, left_side=False, lower=True, transpose_a=True
    )
    columns = buffer
    coeff_own = lax.psum_scatter(
        lax.dot_general(
            columns,
            orthonormal,
            (((0,), (0,)), ((), ())),
            precision=PRECISE,
            preferred_element_type=jnp.float32,
        ),
        "dp",
        scatter_dimension=0,
        tiled=True,
    )
    col_squares = lax.psum(jnp.sum(coeff_own * coeff_own, axis=0), ("dp", "tensor"))
    coeffs = lax.all_gather(coeff_own, "dp", axis=0, tiled=True)
    col_inverse = 1.0 / (jnp.sqrt(col_squares) + 1e-08)
    basis_new = coeff_own * col_inverse
    moment_new = buffer - (1.0 - MOMENTUM) * jnp.dot(orthonormal, coeffs.T, precision=PRECISE)
    qkv_group = 3 * HEADS * HEAD_DIM // tensor_count
    qkv_scale = 0.2 * math.sqrt(D * (3 * HEADS * HEAD_DIM) / RANK)
    mlp_scale = 0.2 * math.sqrt(D * FF / RANK)
    position = jnp.arange(group_cols, dtype=jnp.int32)
    col_scale = jnp.where(position < qkv_group, qkv_scale, mlp_scale).astype(jnp.float32)
    update = jnp.dot(orthonormal, (coeffs * col_inverse).T, precision=PRECISE) * col_scale[None, :]
    return (input_grad, gain_grad, moment_new, basis_new, update)


def solution(mesh):
    in_specs = (
        P("dp", None),
        P(),
        P("dp", "tensor"),
        P("dp", "tensor"),
        P("dp", "tensor"),
        P(("tensor", "dp"), None),
    )
    out_specs = (
        P("dp", "tensor"),
        P("tensor"),
        P("dp", "tensor"),
        P(("tensor", "dp"), None),
        P("dp", "tensor"),
    )
    return jax.shard_map(
        per_device, mesh=mesh, in_specs=in_specs, out_specs=out_specs, check_vma=False
    )
```

profile of v0, /device:TPU:1, one launch (start us, length us, event | category | flops | bytes accessed | tf_op | source)
XLA Modules:
  0.0 807.9 jit_solution(6138274977421186567)
XLA Ops:
  8.7 1.2 convert_reduce_fusion
  9.8 1.3 fusion.11
  11.6 1.2 multiply_convert_fusion
  13.5 1.1 copy.25
  14.6 8.6 %all-to-all-start.1 = ((bf16[32,32,192]{2,0,1:T(8,128)(2,1)}), bf16[32,32,192]{2,0,1:T(8,128)(2,1)S(1)}, u32[]{:S(2)}, u32[]{:S(2)}) async-start(bf16[32,32,192]{2,0,1:T(8,128)(2,1)} %copy.25), calls=%async_computation.1 | async-start | bytes 1048576 | tf_op jit(solution)/shard_map/all_to_all | solution.py:32
  23.1 47.0 %all-gather.8.cloned.1.call-done = f32[32,84,512]{2,1,0:T(8,128)} async-done(((f32[1,84,512]{2,1,0:T(8,128)}), f32[32,84,512]{2,1,0:T(8,128)}) %all-gather.8.cloned.1.call-update) | async-done | bytes 5505040 | tf_op jit(solution)/shard_map/all_gather | solution.py:57
  70.1 6.7 reshape.98
  76.8 47.9 %all-gather.6.cloned.1.call-done = bf16[1024,2688]{1,0:T(8,128)(2,1)} async-done(((bf16[32,2688]{1,0:T(8,128)(2,1)}), bf16[1024,2688]{1,0:T(8,128)(2,1)}) %all-gather.6.cloned.1.call-update) | async-done | bytes 5505040 | tf_op jit(solution)/shard_map/all_gather | solution.py:33
  124.7 5.2 fusion.51
  129.9 5.2 all-to-all-start
  135.2 4.7 convolution_add_fusion
  139.9 7.3 fusion.52
  147.2 4.9 all-to-all-done
  152.1 2.8 copy.24
  154.9 2.5 all_to_all.31
  157.5 69.9 %all-reduce.9.cloned.1.call-done = (f32[32,6144]{1,0:T(8,128)}, f32[192,512]{1,0:T(8,128)}) async-done(((f32[32,6144]{1,0:T(8,128)}, f32[192,512]{1,0:T(8,128)}), (f32[32,6144]{1,0:T(8,128)}, f32[192,512]{1,0:T(8,128)})) %all-reduce.9.cloned.1.call-update) | async-done | bytes 1179664 | tf_op jit(solution)/shard_map/psum | solution.py:43
  227.4 3.2 fusion.53
  231.4 117.4 %all-reduce.7.cloned.1.call-done = f32[512,512]{0,1:T(8,128)} async-done(((f32[512,512]{0,1:T(8,128)}), f32[512,512]{0,1:T(8,128)}) %all-reduce.7.cloned.1.call-update) | async-done | bytes 1048592 | tf_op jit(solution)/shard_map/psum | solution.py:62
  348.9 2.5 copy.27
  351.4 1.8 fusion.8
  354.8 12.5 %cholesky.104 = f32[128,128]{1,0:T(8,128)S(1)} custom-call(f32[128,128]{1,0:T(8,128)} %cholesky.266), custom_call_target="Cholesky" | custom-call | tf_op jit(solution)/shard_map/jit(cholesky)/cholesky | solution.py:63
  367.4 1.2 select_reduce_fusion.3
  368.6 1.1 cholesky.224
  369.7 10.6 %custom-call.30 = f32[1,128,128]{1,2,0:T(8,128)S(1)} custom-call(f32[1,128,128]{2,1,0:T(8,128)} %get-tuple-element.41), custom_call_target="InvertDiagBlocksLowerTriangular" | custom-call | tf_op jit(solution)/shard_map/jit(cholesky)/cholesky | solution.py:63
  380.4 1.9 constant_dynamic-update-slice_fusion.3
  382.3 1.2 convolution_subtract_fusion
  384.8 12.5 %cholesky.217 = f32[128,128]{1,0:T(8,128)S(1)} custom-call(f32[128,128]{1,0:T(8,128)} %cholesky.270), custom_call_target="Cholesky" | custom-call | tf_op jit(solution)/shard_map/jit(cholesky)/cholesky | solution.py:63
  397.4 1.2 select_reduce_fusion.2
  398.6 10.8 %custom-call.31 = f32[1,128,128]{1,2,0:T(8,128)S(1)} custom-call(f32[1,128,128]{2,1,0:T(8,128)} %get-tuple-element.38), custom_call_target="InvertDiagBlocksLowerTriangular" | custom-call | tf_op jit(solution)/shard_map/jit(cholesky)/cholesky | solution.py:63
  409.4 1.8 convolution_dynamic-update-slice_fusion
  411.2 1.4 convolution_subtract_fusion.1
  414.0 12.5 %cholesky.238 = f32[128,128]{1,0:T(8,128)S(1)} custom-call(f32[128,128]{1,0:T(8,128)} %cholesky.275), custom_call_target="Cholesky" | custom-call | tf_op jit(solution)/shard_map/jit(cholesky)/cholesky | solution.py:63
  426.5 1.2 select_reduce_fusion.1
  427.7 10.6 %custom-call.32 = f32[1,128,128]{1,2,0:T(8,128)S(1)} custom-call(f32[1,128,128]{2,1,0:T(8,128)} %get-tuple-element.35), custom_call_target="InvertDiagBlocksLowerTriangular" | custom-call | tf_op jit(solution)/shard_map/jit(cholesky)/cholesky | solution.py:63
  438.4 1.7 convolution_dynamic-update-slice_fusion.1
  440.0 1.4 convolution_subtract_fusion.5
  441.5 12.3 %cholesky.255 = f32[128,128]{1,0:T(8,128)} custom-call(f32[128,128]{1,0:T(8,128)S(1)} %convolution_subtract_fusion.5), custom_call_target="Cholesky" | custom-call | tf_op jit(solution)/shard_map/jit(cholesky)/cholesky | solution.py:63
  453.8 1.5 select_reduce_fusion
  455.3 1.4 compare_reduce_fusion.1
  457.3 1.7 compare_reduce_fusion.2
  461.5 2.3 select_select_fusion
  464.5 14.0 %while.1 = (s32[]{:T(128)}, f32[512,512]{1,0:T(8,128)}, s32[4,2]{0,1:T(2,128)S(1)}, f32[4,128,128]{2,1,0:T(8,128)}, s32[]{:T(128)}) while((s32[]{:T(128)}, f32[512,512]{1,0:T(8,128)}, s32[4,2]{0,1:T(2,128)S(1)}, f32[4,128,128]{2,1,0:T(8,128)}, s32[]{:T(128)}) %tuple.37), condition=%wide.while_cond, body=%wide.while_body.sunk | while | flops 2 | bytes 132205 | solution.py:64
  465.1 2.9 bitcast_dynamic-update-slice_fusion.2
  468.6 2.9 bitcast_dynamic-update-slice_fusion.2
  472.1 2.9 bitcast_dynamic-update-slice_fusion.2
  475.6 2.8 bitcast_dynamic-update-slice_fusion.2
  478.5 40.8 %custom-call.33 = f32[4,128,128]{1,2,0:T(8,128)} custom-call(f32[4,128,128]{2,1,0:T(8,128)} %get-tuple-element.12), custom_call_target="InvertDiagBlocksLowerTriangular" | custom-call | tf_op jit(solution)/shard_map/triangular_solve | solution.py:64
  520.3 1.1 convolution_subtract_fusion.2
  522.6 1.3 convolution_subtract_fusion.4
  524.9 1.4 convolution_subtract_fusion.3
  528.1 10.6 %fusion.33 = f32[2688,512]{1,0:T(8,128)} fusion(f32[192,2688]{1,0:T(8,128)S(1)} %convolution_add_fusion, f32[192,128]{1,0:T(8,128)S(1)} %fusion.34, f32[192,128]{1,0:T(8,128)S(1)} %fusion.35, f32[192,128]{1,0:T(8,128)S(1)} %fusion.36, f32[192,128]{1,0:T(8,128)S(1)} %fusion.28), kind=kOutput, calls=%fused_computation.57 | convolution fusion | flops 3171188736 | bytes 7962624 | tf_op jit(solution)/shard_map/dot_general | solution.py:69
  538.7 76.9 %fusion = f32[88,512]{1,0:T(8,128)} fusion(f32[2688,512]{1,0:T(8,128)} %fusion.33), kind=kCustom, calls=%all-reduce-scatter | all-reduce-scatter fusion | flops 1441793 | bytes 5686272
  615.6 1.9 collective-permute-start
  617.5 1.5 slice.114
  619.0 1.9 collective-permute-start.1
  622.3 4.8 concatenate.9
  628.1 79.5 %psum.39 = f32[512]{0:T(512)S(1)} all-reduce(f32[512]{0:T(512)S(1)} %multiply_reduce_fusion.2), channel_id=1, replica_groups=mesh['dp'=32,'tensor'=8] {'dp','tensor'}, use_global_device_ids=true, to_apply=%region_19.20 | all-reduce | flops 512 | bytes 4096 | tf_op jit(solution)/shard_map/psum | solution.py:80
  707.6 1.7 dynamic-slice_multiply_fusion
  709.4 2.6 fusion.49
  712.1 64.3 %psum.36 = f32[768]{0:T(1024)} all-reduce(f32[768]{0:T(1024)S(1)} %dynamic_slice.7), channel_id=1, replica_groups=mesh['dp'=32,'tensor'=8] {'dp'}, use_global_device_ids=true, to_apply=%region_6.0 | all-reduce | flops 768 | bytes 6144 | tf_op jit(solution)/shard_map/psum | solution.py:52
  776.5 1.6 fusion.32
  778.1 6.8 reshape.100
  785.0 9.4 %fusion.6 = f32[192,2688]{1,0:T(8,128)} fusion(f32[192,2688]{1,0:T(8,128)S(1)} %convolution_add_fusion, f32[2688,512]{1,0:T(8,128)} %reshape.100, f32[192,128]{1,0:T(8,128)S(1)} %copy-done.13, f32[192,128]{1,0:T(8,128)S(1)} %copy-done.11, f32[192,128]{1,0:T(8,128)S(1)} %copy-done.7, f32[192,128]{1,0:T(8,128)S(1)} %copy-done.4), kind=kOutput, calls=%fused_computation.6 | convolution fusion | flops 3172220928 | bytes 10027008 | tf_op jit(solution)/shard_map/dot_general | solution.py:84
  794.4 6.7 fusion.3
  (86 shorter events, 18.1 us)
Async XLA Ops:
  7.2 117.6 %copy-start = (bf16[192,2688]{1,0:T(8,128)(2,1)S(1)}, bf16[192,2688]{1,0:T(8,128)(2,1)}, u32[]{:S(2)}) copy-start(bf16[192,2688]{1,0:T(8,128)(2,1)} %param.9) | copy-start | bytes 3096580
  7.2 62.9 %all-gather.8.cloned.1.call-start = ((), (), s32[]{:S(2)}) async-start(), calls=%async_computation.4 | async-start | bytes 5947392 | tf_op jit(solution)/shard_map/all_gather | solution.py:57
  7.9 116.8 %all-gather.6.cloned.1.call-start = ((), (), s32[]{:S(2)}) async-start(), calls=%async_computation.2 | async-start | bytes 5677056 | tf_op jit(solution)/shard_map/all_gather | solution.py:33
  9.8 1.3 copy-start.19
  11.1 0.5 copy-start.17
  14.6 115.4 %all-to-all-start.1 = ((bf16[32,32,192]{2,0,1:T(8,128)(2,1)}), bf16[32,32,192]{2,0,1:T(8,128)(2,1)S(1)}, u32[]{:S(2)}, u32[]{:S(2)}) async-start(bf16[32,32,192]{2,0,1:T(8,128)(2,1)} %copy.25), calls=%async_computation.1 | async-start | bytes 1048576 | tf_op jit(solution)/shard_map/all_to_all | solution.py:32
  129.9 5.3 copy-start.5
  129.9 22.2 %all-to-all-start = ((f32[32,32,192]{2,1,0:T(8,128)}), f32[32,32,192]{2,1,0:T(8,128)}, u32[]{:S(2)}, u32[]{:S(2)}) async-start(f32[32,32,192]{2,1,0:T(8,128)} %bitcast), calls=%async_computation | async-start | bytes 2097152 | tf_op jit(solution)/shard_map/all_to_all | solution.py:40
  135.2 92.3 %all-reduce.9.cloned.1.call-start = ((), (), s32[]{:S(2)}) async-start(), calls=%async_computation.6 | async-start | bytes 2359296 | tf_op jit(solution)/shard_map/psum | solution.py:43
  157.4 191.4 %all-reduce.7.cloned.1.call-start = ((), (), s32[]{:S(2)}) async-start(), calls=%async_computation.3 | async-start | bytes 2097152 | tf_op jit(solution)/shard_map/psum | solution.py:62
  230.6 547.5 %all-gather.10.cloned.1.call-start = ((), (), s32[]{:S(2)}) async-start(), calls=%async_computation.5 | async-start | bytes 5947392 | tf_op jit(solution)/shard_map/all_gather | solution.py:81
  351.4 167.8 %copy-start.8 = (f32[192,512]{1,0:T(8,128)S(1)}, f32[192,512]{1,0:T(8,128)}, u32[]{:S(2)}) copy-start(f32[192,512]{1,0:T(8,128)} %get-tuple-element.25) | copy-start | bytes 1179652
  353.2 1.0 copy-start.9
  383.5 0.7 copy-start.14
  412.7 0.7 copy-start.15
  520.3 7.1 copy-start.3
  522.6 4.9 copy-start.6
  524.9 2.5 copy-start.10
  527.5 0.6 copy-start.12
  538.7 82.3 %copy-start.21 = (u32[256]{0:T(256)S(1)}, u32[256]{0:T(256)}, u32[]{:S(2)}) copy-start(u32[256]{0:T(256)} %constant.192) | copy-start | bytes 3076
  538.7 170.7 %copy-start.2 = (bf16[32,6144]{1,0:T(8,128)(2,1)S(1)}, bf16[32,6144]{1,0:T(8,128)(2,1)}, u32[]{:S(2)}) copy-start(bf16[32,6144]{1,0:T(8,128)(2,1)} %param.6) | copy-start | bytes 1179652
  538.7 170.7 %copy-start.16 = (f32[6144]{0:T(1024)S(1)}, f32[6144]{0:T(1024)}, u32[]{:S(2)}) copy-start(f32[6144]{0:T(1024)} %param.7) | copy-start | bytes 73732
  538.7 170.7 %copy-start.18 = (f32[32]{0:T(128)S(1)}, f32[32]{0:T(128)}, u32[]{:S(2)}) copy-start(f32[32]{0:T(128)} %copy-done.17) | copy-start | bytes 388
  538.7 170.7 %copy-start.20 = (f32[32]{0:T(128)S(1)}, f32[32]{0:T(128)}, u32[]{:S(2)}) copy-start(f32[32]{0:T(128)} %copy-done.19) | copy-start | bytes 388
  615.6 6.8 collective-permute-start
  619.0 3.2 collective-permute-start.1
  778.1 6.8 copy-start.4
  778.1 6.8 copy-start.7
  778.1 6.8 copy-start.11
  778.1 6.8 copy-start.13
  785.0 9.5 %copy-start.1 = (f32[2688,512]{1,0:T(8,128)S(1)}, f32[2688,512]{1,0:T(8,128)}, u32[]{:S(2)}) copy-start(f32[2688,512]{1,0:T(8,128)} %reshape.100) | copy-start | bytes 16515076
Sparse Core Ops, SparseCore 0:
  10.6 59.5 all-gather.7
  72.7 52.0 all-gather.5
  157.6 69.8 all-reduce.8
  231.1 117.7 all-reduce.6
  709.5 50.2 all-gather.9
where the time goes:
time: 818 us; the launch traced here: 808 us
  waiting for transfers between devices  289 us (35%)
  blocking collectives  221 us (27%)
  other arithmetic  147 us (18%)
  matrix products  64.7 us (8%)
  local copies, waits for them, and re-layouts  51.1 us (6%)
  starting transfers between devices  18 us (2%)
  between operations  17.6 us (2%)
    psum x1, waiting for transfers between devices, per_device(): gram = lax.psum(jnp.dot(projected.T, projected, precision=PRECISE), 'dp')  117 us
    another operation x14, other arithmetic, per_device(): factor = jnp.linalg.cholesky(gram)  90.9 us
    psum x1, blocking collectives, per_device(): lax.psum(jnp.sum(coeff_own * coeff_own, axis=0), ('dp', 'tensor'))  79.5 us
    unnamed x1, blocking collectives  76.9 us
    psum x1, waiting for transfers between devices, per_device(): normed_grad = lax.psum(back_mine, 'tensor')  69.9 us
    psum x1, blocking collectives, per_device(): gain_grad = lax.psum(gain_part, 'dp')  64.3 us
    all_gather x1, waiting for transfers between devices, per_device(): shard_in = lax.all_gather(out_grad, 'dp', axis=0, tiled=True)  47.9 us
    all_gather x1, waiting for transfers between devices, per_device(): lax.all_gather(right_basis, 'dp', axis=0, tiled=True)  47 us
  transfers between devices with their start and end apart: 9, of which 6 were waited for; matrix products, arithmetic and copies ran while one was open for 4% of the time, Pallas kernels for 0%

commit v1 on v0

v1 whole, which is shorter than its diff:
```python
import math

import jax
import jax.numpy as jnp
from jax import lax
from jax.experimental import pallas as pl
from jax.experimental.pallas import tpu as pltpu
from jax.sharding import PartitionSpec as P

D = 6144
HEADS = 24
HEAD_DIM = 128
FF = 12288
RANK = 512
MOMENTUM = 0.8
NORM_EPSILON = 1e-06

HI = lax.Precision.HIGHEST
MESH = pl.DeviceIdType.MESH
VMEM_LIMIT = 56 * 1024 * 1024
F32 = jnp.float32
BF16 = jnp.bfloat16


def dp_of(x, y, core):
    return (x * 4 + y) * 2 + core


def place():
    dp = lax.axis_index("dp")
    return dp // 8, (dp // 2) % 4, dp % 2, lax.axis_index("tensor")


def send(src, dst, send_sem, recv_sem, **peer):
    copy = pltpu.make_async_remote_copy(
        src_ref=src, dst_ref=dst, send_sem=send_sem, recv_sem=recv_sem,
        device_id=peer, device_id_type=MESH,
    )
    copy.start()
    return copy


def wait_recv(dst, recv_sem, **peer):
    pltpu.make_async_remote_copy(
        src_ref=dst, dst_ref=dst, send_sem=recv_sem, recv_sem=recv_sem,
        device_id=peer, device_id_type=MESH,
    ).wait_recv()


def greet(peers):
    barrier = pltpu.get_barrier_semaphore()
    for peer in peers:
        pl.semaphore_signal(barrier, inc=1, device_id=peer, device_id_type=MESH)
    pl.semaphore_wait(barrier, len(peers))


def plane_neighbours(x, y, core):
    return [
        {"dp": dp_of((x + 1) % 4, y, core)},
        {"dp": dp_of((x + 3) % 4, y, core)},
        {"dp": dp_of(x, (y + 1) % 4, core)},
        {"dp": dp_of(x, (y + 3) % 4, core)},
        {"dp": dp_of(x, y, 1 - core)},
    ]


def round_robin(generators):
    live = list(generators)
    while live:
        still = []
        for g in live:
            try:
                next(g)
                still.append(g)
            except StopIteration:
                pass
        live = still


def gather_stream(loc, first, ssem, rsem, base, sent):
    x0, y0, core, _ = place()
    a0, b0 = (x0, y0) if first == "x" else (y0, x0)
    sib = dp_of(x0, y0, 1 - core)

    def xy(a, b):
        return (a % 4, b % 4) if first == "x" else (b % 4, a % 4)

    def at(a, b, part, who=None):
        return loc(core if who is None else who, *xy(a, b), part)

    def to(a, b, block, part, slot):
        ref = at(*block, part)
        sent.append(send(ref, ref, ssem.at[base + slot], rsem.at[base + slot], dp=dp_of(*xy(a, b), core)))

    def got(block, part, slot):
        wait_recv(at(*block, part), rsem.at[base + slot], dp=sib)

    def share(block, slot):
        ref = at(*block, 2)
        sent.append(send(ref, ref, ssem.at[base + slot], rsem.at[base + slot], dp=sib))

    def spread(k, block):
        to(a0, b0 + 1, block, 2, 4 + 4 * k)
        to(a0, b0 - 1, block, 2, 5 + 4 * k)

    offs = (0, -1, 1, 2)
    to(a0 + 1, b0, (a0, b0), 2, 0)
    to(a0 - 1, b0, (a0, b0), 2, 1)
    yield
    spread(0, (a0, b0))
    share((a0, b0), 20)
    yield
    got((a0 - 1, b0), 2, 0)
    to(a0 + 1, b0, (a0 - 1, b0), 0, 2)
    spread(1, (a0 - 1, b0))
    yield
    got((a0 + 1, b0), 2, 1)
    to(a0 - 1, b0, (a0 + 1, b0), 1, 3)
    spread(2, (a0 + 1, b0))
    yield
    share((a0 - 1, b0), 21)
    share((a0 + 1, b0), 22)
    got((a0 + 2, b0), 0, 2)
    got((a0 + 2, b0), 1, 3)
    spread(3, (a0 + 2, b0))
    share((a0 + 2, b0), 23)
    yield
    for k in range(4):
        a = a0 + offs[k]
        got((a, b0 - 1), 2, 4 + 4 * k)
        to(a0, b0 + 1, (a, b0 - 1), 0, 6 + 4 * k)
        got((a, b0 + 1), 2, 5 + 4 * k)
        to(a0, b0 - 1, (a, b0 + 1), 1, 7 + 4 * k)
        share((a, b0 - 1), 24 + 3 * k)
        share((a, b0 + 1), 25 + 3 * k)
        yield
    for k in range(4):
        a = a0 + offs[k]
        got((a, b0 + 2), 0, 6 + 4 * k)
        got((a, b0 + 2), 1, 7 + 4 * k)
        share((a, b0 + 2), 26 + 3 * k)
        yield
    for k in range(4):
        a = a0 + offs[k]
        wait_recv(at(a, b0, 2, 1 - core), rsem.at[base + 20 + k], dp=sib)
        for j, b in enumerate((b0 - 1, b0 + 1, b0 + 2)):
            wait_recv(at(a, b, 2, 1 - core), rsem.at[base + 24 + 3 * k + j], dp=sib)
        yield


GATHER_SLOTS = 36


def gather_kernel(r_ref, g_ref, rall_ref, gall_ref, got_ref, ssem, rsem, hsem):
    x, y, core, _ = place()
    chip = x * 4 + y
    greet(plane_neighbours(x, y, core))
    rows = r_ref.shape[0]
    tokens = g_ref.shape[0]
    cols = g_ref.shape[1]
    cut = 1408
    other = pl.multiple_of(256 * (1 - core), 128)
    swap = send(r_ref.at[:, pl.ds(other, 256)], got_ref, hsem.at[0], hsem.at[1], dp=dp_of(x, y, 1 - core))
    own_g = pltpu.make_async_copy(
        g_ref, gall_ref.at[pl.ds(pl.multiple_of(tokens * (2 * chip + core), 32), tokens)], hsem.at[2]
    )
    own_g.start()

    def loc_r(s):
        def loc(who, bx, by, part):
            lo, n = ((0, 88), (88, 80), (0, 168))[part]
            row = pl.multiple_of((bx * 4 + by) * 168 + lo, 8)
            col = pl.multiple_of(256 * who + 128 * s, 128)
            return rall_ref.at[pl.ds(row, n), pl.ds(col, 128)]
        return loc

    def loc_g(s):
        def loc(who, bx, by, part):
            lo, n = ((0, cut), (cut, cols - cut), (0, cols))[part]
            row = pl.multiple_of(tokens * (2 * (bx * 4 + by) + who) + 16 * s, 16)
            return gall_ref.at[pl.ds(row, 16), pl.ds(lo, n)]
        return loc

    sent = []
    own_g.wait()
    g_streams = [
        gather_stream(loc_g(0), "x", ssem, rsem, 2 * GATHER_SLOTS, sent),
        gather_stream(loc_g(1), "y", ssem, rsem, 3 * GATHER_SLOTS, sent),
    ]
    swap.wait()
    mine = r_ref[:, pl.ds(pl.multiple_of(256 * core, 128), 256)]
    theirs = got_ref[...]
    first = jnp.where(core == 0, mine, theirs)
    second = jnp.where(core == 0, theirs, mine)
    row = pl.multiple_of(chip * 168, 8)
    col = pl.multiple_of(256 * core, 128)
    rall_ref[pl.ds(row, 168), pl.ds(col, 256)] = jnp.concatenate([first, second], axis=0)
    r_streams = [
        gather_stream(loc_r(0), "x", ssem, rsem, 0, sent),
        gather_stream(loc_r(1), "y", ssem, rsem, GATHER_SLOTS, sent),
    ]
    round_robin(r_streams + g_streams)
    for copy in sent:
        copy.wait_send()


def gather_both(right_basis, out_grad):
    vm = pl.BlockSpec(memory_space=pltpu.VMEM)
    return pl.pallas_call(
        gather_kernel,
        out_shape=(
            jax.ShapeDtypeStruct((32 * right_basis.shape[0], RANK), F32),
            jax.ShapeDtypeStruct((32 * out_grad.shape[0], out_grad.shape[1]), BF16),
        ),
        in_specs=[vm, vm],
        out_specs=(vm, vm),
        scratch_shapes=[
            pltpu.VMEM((right_basis.shape[0], 256), F32),
            pltpu.SemaphoreType.DMA((4 * GATHER_SLOTS,)),
            pltpu.SemaphoreType.DMA((4 * GATHER_SLOTS,)),
            pltpu.SemaphoreType.DMA((3,)),
        ],
        compiler_params=pltpu.CompilerParams(
            collective_id=1, has_side_effects=True, vmem_limit_bytes=VMEM_LIMIT
        ),
    )(right_basis, out_grad)


def gram_kernel(part_ref, p_ref, g_ref, zbuf, gbuf, cbuf, xbuf, ybuf, ssem, rsem):
    x, y, core, z = place()
    xs = [(x + d) % 4 for d in (1, 2, 3)]
    ys = [(y + d) % 4 for d in (1, 2, 3)]
    zs = [(z + d) % 8 for d in range(1, 8)]
    dp = lax.axis_index("dp")
    sib = dp_of(x, y, 1 - core)
    greet(
        [{"tensor": q} for q in zs]
        + [{"dp": dp_of(q, y, core)} for q in xs]
        + [{"dp": dp_of(x, q, core)} for q in ys]
        + [{"dp": sib}]
    )
    sent = []
    order = (3, 4, 2, 5, 1, 6, 0)

    def rows24(q):
        return pl.ds(pl.multiple_of(24 * q, 8), 24)

    for i in order:
        sent.append(send(part_ref.at[rows24(zs[i])], zbuf.at[i], ssem.at[i], rsem.at[i], tensor=zs[i]))
    total = part_ref[rows24(z), :]
    for i in reversed(order):
        wait_recv(zbuf.at[i], rsem.at[i], tensor=zs[i])
        total = total + zbuf[i]
    p_ref[rows24(z), :] = total
    mine = p_ref.at[rows24(z)]
    for i in order:
        sent.append(send(mine, mine, ssem.at[7 + i], rsem.at[7 + i], tensor=zs[i]))
    for i in reversed(order):
        src = (z + 7 - i) % 8
        wait_recv(p_ref.at[rows24(src)], rsem.at[7 + i], tensor=zs[i])

    gbuf[...] = lax.dot_general(
        p_ref[:, pl.ds(pl.multiple_of(128 * (z // 2), 128), 128)], p_ref[...],
        (((0,), (0,)), ((), ())), precision=HI, preferred_element_type=F32,
    )
    half = 64 * (z % 2)
    sent.append(send(gbuf.at[pl.ds(pl.multiple_of(half + 32 * (1 - core), 32), 32)], cbuf, ssem.at[14], rsem.at[14], dp=sib))
    wait_recv(cbuf, rsem.at[14], dp=sib)
    cbuf[...] += gbuf[pl.ds(pl.multiple_of(half + 32 * core, 32), 32), :]
    for i in range(3):
        sent.append(send(
            cbuf.at[pl.ds(pl.multiple_of(8 * xs[i], 8), 8)], xbuf.at[i], ssem.at[15 + i], rsem.at[15 + i],
            dp=dp_of(xs[i], y, core),
        ))
    total = cbuf[pl.ds(pl.multiple_of(8 * x, 8), 8), :]
    for i in range(3):
        wait_recv(xbuf.at[i], rsem.at[15 + i], dp=sib)
        total = total + xbuf[i]
    ybuf[y] = total
    for i in range(3):
        sent.append(send(ybuf.at[y], ybuf.at[y], ssem.at[18 + i], rsem.at[18 + i], dp=dp_of(x, ys[i], core)))
    for i in range(3):
        wait_recv(ybuf.at[(y + 3 - i) % 4], rsem.at[18 + i], dp=sib)
    g_ref[z, core, x] = (ybuf[0] + ybuf[1]) + (ybuf[2] + ybuf[3])
    mine = g_ref.at[z, core, x]
    for i in order:
        sent.append(send(mine, mine, ssem.at[21 + i], rsem.at[21 + i], tensor=zs[i]))
    for i in reversed(order):
        wait_recv(g_ref.at[(z + 7 - i) % 8, core, x], rsem.at[21 + i], tensor=zs[i])
    mine = g_ref.at[:, core, x]
    for i in range(3):
        sent.append(send(mine, mine, ssem.at[28 + i], rsem.at[28 + i], dp=dp_of(xs[i], y, core)))
    sent.append(send(mine, mine, ssem.at[31], rsem.at[31], dp=sib))
    for i in range(3):
        src = (x + 3 - i) % 4
        wait_recv(g_ref.at[:, core, src], rsem.at[28 + i], dp=sib)
        got = g_ref.at[:, core, src]
        sent.append(send(got, got, ssem.at[32 + i], rsem.at[32 + i], dp=sib))
    wait_recv(g_ref.at[:, 1 - core, x], rsem.at[31], dp=sib)
    for i in range(3):
        wait_recv(g_ref.at[:, 1 - core, (x + 3 - i) % 4], rsem.at[32 + i], dp=sib)
    for copy in sent:
        copy.wait_send()


def projected_gram(part):
    vm = pl.BlockSpec(memory_space=pltpu.VMEM)
    p, g = pl.pallas_call(
        gram_kernel,
        out_shape=(
            jax.ShapeDtypeStruct(part.shape, F32),
            jax.ShapeDtypeStruct((8, 2, 4, 8, RANK), F32),
        ),
        in_specs=[vm],
        out_specs=(vm, vm),
        scratch_shapes=[
            pltpu.VMEM((7, 24, RANK), F32),
            pltpu.VMEM((128, RANK), F32),
            pltpu.VMEM((32, RANK), F32),
            pltpu.VMEM((3, 8, RANK), F32),
            pltpu.VMEM((4, 8, RANK), F32),
            pltpu.SemaphoreType.DMA((35,)),
            pltpu.SemaphoreType.DMA((35,)),
        ],
        compiler_params=pltpu.CompilerParams(
            collective_id=2, has_side_effects=True, vmem_limit_bytes=VMEM_LIMIT
        ),
    )(part)
    return p, g.reshape(RANK, RANK)


def chol_kernel(g_ref, p_ref, ot_ref, s_ref, w_ref):
    n_p = p_ref.shape[1]
    s_ref[:, 0:512] = g_ref[...]
    s_ref[:, 512:512 + n_p] = p_ref[...]
    s_ref[:, 512 + n_p:] = jnp.zeros((512, s_ref.shape[1] - 512 - n_p), F32)
    lane = lax.broadcasted_iota(jnp.int32, (8, 128), 1)
    sub = lax.broadcasted_iota(jnp.int32, (8, 128), 0)

    def lane_splat(v, j):
        return jnp.broadcast_to(v[:, j:j + 1], (8, 128))

    def row_splat(v, i):
        return jnp.broadcast_to(v[i:i + 1, :], (8, 128))

    def block(kb, carry):
        base = pl.multiple_of(kb * 128, 128)
        tiles = [s_ref[pl.ds(pl.multiple_of(base + 8 * i, 8), 8), pl.ds(base, 128)] for i in range(16)]
        for k in range(16):
            x = tiles[k]
            inside = (lane >= 8 * k) & (lane < 8 * k + 8)
            c = [lane_splat(x, 8 * k + q) for q in range(8)]
            x = jnp.where(inside, (lane - 8 * k == sub).astype(F32), x)
            inv, up, rows = [], [], []
            scale = jnp.ones((8, 128), F32)
            for p in range(8):
                pd = row_splat(c[p], p)
                ip = 1.0 / pd
                scale = jnp.where(sub == p, lax.rsqrt(pd), scale)
                m = jnp.where(sub > p, c[p] * ip, 0.0)
                u = {}
                for q in range(p + 1, 8):
                    u[q] = row_splat(c[q], p)
                    c[q] = c[q] - m * u[q]
                r = row_splat(x, p)
                x = x - m * r
                inv.append(ip)
                up.append(u)
                rows.append(r)
            w_ref[8 * k:8 * k + 8, :] = jnp.where(lane <= sub + 8 * k, x * scale, 0.0)
            for g in range(k + 1, 16):
                v = tiles[g]
                e = [lane_splat(v, 8 * k + q) for q in range(8)]
                v = jnp.where(inside, 0.0, v)
                for p in range(8):
                    m = e[p] * inv[p]
                    for q in range(p + 1, 8):
                        e[q] = e[q] - m * up[p][q]
                    v = v - m * rows[p]
                tiles[g] = v
        rows_k = pl.ds(base, 128)
        s_ref[rows_k, :] = jnp.dot(w_ref[...], s_ref[rows_k, :], precision=HI, preferred_element_type=F32)
        for rb in range(1, 4):
            @pl.when(rb > kb)
            def _():
                ub = s_ref[rows_k, 128 * rb:128 * rb + 128]
                s_ref[128 * rb:128 * rb + 128, 128 * rb:] -= lax.dot_general(
                    ub, s_ref[rows_k, 128 * rb:], (((0,), (0,)), ((), ())), precision=HI,
                    preferred_element_type=F32,
                )
        return carry

    lax.fori_loop(0, 4, block, 0)
    ot_ref[...] = s_ref[:, 512:512 + n_p]


def chol_solve(gram, projected_t):
    n_p = projected_t.shape[1]
    vm = pl.BlockSpec(memory_space=pltpu.VMEM)
    return pl.pallas_call(
        chol_kernel,
        out_shape=jax.ShapeDtypeStruct((RANK, n_p), F32),
        in_specs=[vm, vm],
        out_specs=vm,
        scratch_shapes=[pltpu.VMEM((RANK, 768), F32), pltpu.VMEM((128, 128), F32)],
        compiler_params=pltpu.CompilerParams(vmem_limit_bytes=VMEM_LIMIT),
    )(gram, projected_t)


SPLIT = ((0, 96), (96, 80), (0, 176))


def coeff_kernel(c_ref, call_ref, cown_ref, csq_ref, pair, sbuf, rbuf, acc, s2, r2, fin, fsib, agb,
                 xsq, ysq, zsq, sqs, ssem, rsem, gs, gr):
    x, y, core, z = place()
    sib = dp_of(x, y, 1 - core)
    xs = [(x + d) % 4 for d in (1, 2, 3)]
    ys = [(y + d) % 4 for d in (1, 2, 3)]
    zs = [(z + d) % 8 for d in range(1, 8)]
    greet(
        [{"tensor": q} for q in zs]
        + [{"dp": dp_of(q, y, core)} for q in xs]
        + [{"dp": dp_of(x, q, core)} for q in ys]
        + [{"dp": sib}]
    )
    sent = []
    first = ("x", "y")

    def chunk(ref, s, a, cols=None):
        a = a % 4
        if cols is None:
            return ref.at[s, a] if s == 0 else ref.at[s, :, a]
        return ref.at[a, :, :, cols] if s == 0 else ref.at[:, a, :, cols]

    def cols_of(who, s):
        return pl.ds(pl.multiple_of(256 * who + 128 * s, 128), 128)

    a0 = (x, y)
    b0 = (y, x)
    n = 0
    pieces = {}
    for off in (2, 1, 3, 0):
        for s in (0, 1):
            sent.append(send(
                chunk(c_ref, s, a0[s] + off, cols_of(1 - core, s)), chunk(pair, s, a0[s] + off),
                ssem.at[n], rsem.at[n], dp=sib,
            ))
            pieces[off, s] = n
            n += 1

    def own(s, off, b):
        a = (a0[s] + off) % 4
        bx, by = (a, b) if s == 0 else (b, a)
        return c_ref[bx, by, :, cols_of(core, s)] + pair[s, bx, by]

    def pair_ready(s, off):
        wait_recv(chunk(pair, s, a0[s] + off), rsem.at[pieces[off, s]], dp=sib)

    def dev(s, a, b):
        a, b = a % 4, b % 4
        return dp_of(a, b, core) if s == 0 else dp_of(b, a, core)

    zero_pad = jnp.zeros((8, 128), F32)

    def padded(v):
        return jnp.concatenate([v, zero_pad], axis=0).astype(BF16)

    def reduce_stream(s):
        base = 8 + 8 * s
        a, b = a0[s], b0[s]
        right, left = dev(s, a + 1, b), dev(s, a - 1, b)
        pair_ready(s, 2)
        for j in range(4):
            sbuf[s, 0, j] = padded(own(s, 2, j))
        sent.append(send(sbuf.at[s, 0, 0:2], rbuf.at[s, 0, 0:2], ssem.at[base], rsem.at[base], dp=right))
        sent.append(send(sbuf.at[s, 0, 2:4], rbuf.at[s, 0, 2:4], ssem.at[base + 1], rsem.at[base + 1], dp=left))
        yield
        pair_ready(s, 1)
        pair_ready(s, 3)
        for j in (2, 3):
            sbuf[s, 1, j] = padded(own(s, 1, j))
        for j in (0, 1):
            sbuf[s, 2, j] = padded(own(s, 3, j))
        yield
        wait_recv(rbuf.at[s, 0, 0:2], rsem.at[base], dp=left)
        for j in (0, 1):
            sbuf[s, 1, j] = padded(own(s, 1, j) + rbuf[s, 0, j, 0:168].astype(F32))
        sent.append(send(sbuf.at[s, 1], rbuf.at[s, 1], ssem.at[base + 2], rsem.at[base + 2], dp=right))
        yield
        wait_recv(rbuf.at[s, 0, 2:4], rsem.at[base + 1], dp=right)
        for j in (2, 3):
            sbuf[s, 2, j] = padded(own(s, 3, j) + rbuf[s, 0, j, 0:168].astype(F32))
        sent.append(send(sbuf.at[s, 2], rbuf.at[s, 2], ssem.at[base + 3], rsem.at[base + 3], dp=left))
        yield
        pair_ready(s, 0)
        for j in range(4):
            acc[s, j] = own(s, 0, j)
        yield
        wait_recv(rbuf.at[s, 1], rsem.at[base + 2], dp=left)
        wait_recv(rbuf.at[s, 2], rsem.at[base + 3], dp=right)

        def summed(off):
            j = (b + off) % 4
            return acc[s, j] + (rbuf[s, 1, j, 0:168].astype(F32) + rbuf[s, 2, j, 0:168].astype(F32))

        right, left = dev(s, a, b + 1), dev(s, a, b - 1)
        s2[s, 0] = padded(summed(2))
        sent.append(send(s2.at[s, 0, 0:96], r2.at[s, 0, 0:96], ssem.at[base + 4], rsem.at[base + 4], dp=right))
        sent.append(send(s2.at[s, 0, 96:176], r2.at[s, 0, 96:176], ssem.at[base + 5], rsem.at[base + 5], dp=left))
        yield
        one, three, zero = summed(1), summed(3), summed(0)
        wait_recv(r2.at[s, 0, 0:96], rsem.at[base + 4], dp=left)
        s2[s, 1, 0:96] = (one[0:96] + r2[s, 0, 0:96].astype(F32)).astype(BF16)
        s2[s, 1, 96:176] = padded(one[96:168])
        sent.append(send(s2.at[s, 1], r2.at[s, 1], ssem.at[base + 6], rsem.at[base + 6], dp=right))
        wait_recv(r2.at[s, 0, 96:176], rsem.at[base + 5], dp=right)
        s2[s, 2, 0:96] = three[0:96].astype(BF16)
        s2[s, 2, 96:176] = padded(three[96:168] + r2[s, 0, 96:168].astype(F32))
        sent.append(send(s2.at[s, 2], r2.at[s, 2], ssem.at[base + 7], rsem.at[base + 7], dp=left))
        yield
        wait_recv(r2.at[s, 1], rsem.at[base + 6], dp=left)
        wait_recv(r2.at[s, 2], rsem.at[base + 7], dp=right)
        total = zero + (r2[s, 1, 0:168].astype(F32) + r2[s, 2, 0:168].astype(F32))
        fin[:, 128 * s:128 * s + 128] = total
        agb[x * 4 + y, :, cols_of(core, s)] = padded(total)
        yield

    round_robin([reduce_stream(0), reduce_stream(1)])

    def norms():
        sent.append(send(fin, fsib, ssem.at[24], rsem.at[24], dp=sib))
        v = fin[...]
        xsq[x] = jnp.broadcast_to(jnp.sum(v * v, axis=0, keepdims=True), (8, 256))
        for i in range(3):
            sent.append(send(xsq.at[x], xsq.at[x], ssem.at[25 + i], rsem.at[25 + i], dp=dp_of(xs[i], y, core)))
        yield
        for i in range(3):
            wait_recv(xsq.at[(x + 3 - i) % 4], rsem.at[25 + i], dp=sib)
        ysq[y] = (xsq[0] + xsq[1]) + (xsq[2] + xsq[3])
        for i in range(3):
            sent.append(send(ysq.at[y], ysq.at[y], ssem.at[28 + i], rsem.at[28 + i], dp=dp_of(x, ys[i], core)))
        yield
        for i in range(3):
            wait_recv(ysq.at[(y + 3 - i) % 4], rsem.at[28 + i], dp=sib)
        zsq[z] = (ysq[0] + ysq[1]) + (ysq[2] + ysq[3])
        for i in range(7):
            sent.append(send(zsq.at[z], zsq.at[z], ssem.at[31 + i], rsem.at[31 + i], tensor=zs[i]))
        yield
        for i in range(7):
            wait_recv(zsq.at[(z + 7 - i) % 8], rsem.at[31 + i], tensor=zs[i])
        total = zsq[0]
        for i in range(1, 8):
            total = total + zsq[i]
        sqs[core] = total
        sent.append(send(sqs.at[core], sqs.at[core], ssem.at[38], rsem.at[38], dp=sib))
        yield
        wait_recv(fsib, rsem.at[24], dp=sib)
        left = jnp.where(core == 0, fin[0:84], fsib[84:168])
        right = jnp.where(core == 0, fsib[0:84], fin[84:168])
        cown_ref[:, 0:256] = left
        cown_ref[:, 256:512] = right
        yield
        wait_recv(sqs.at[1 - core], rsem.at[38], dp=sib)
        csq_ref[:, 0:256] = sqs[0]
        csq_ref[:, 256:512] = sqs[1]
        yield

    def loc(s):
        def at(who, bx, by, part):
            lo, rows = SPLIT[part]
            return agb.at[bx * 4 + by, pl.ds(lo, rows), cols_of(who, s)]
        return at

    round_robin([
        gather_stream(loc(0), first[0], gs, gr, 0, sent),
        gather_stream(loc(1), first[1], gs, gr, GATHER_SLOTS, sent),
        norms(),
    ])
    for j in range(8):
        two = jnp.concatenate([agb[2 * j, 0:168].astype(F32), agb[2 * j + 1, 0:168].astype(F32)], axis=0)
        call_ref[336 * j:336 * j + 336, :] = two.astype(BF16)
    for copy in sent:
        copy.wait_send()


def coeff_sum(part):
    vm = pl.BlockSpec(memory_space=pltpu.VMEM)
    return pl.pallas_call(
        coeff_kernel,
        out_shape=(
            jax.ShapeDtypeStruct((2688, RANK), BF16),
            jax.ShapeDtypeStruct((84, RANK), F32),
            jax.ShapeDtypeStruct((8, RANK), F32),
        ),
        in_specs=[vm],
        out_specs=(vm, vm, vm),
        scratch_shapes=[
            pltpu.VMEM((2, 4, 4, 168, 128), F32),
            pltpu.VMEM((2, 3, 4, 176, 128), BF16),
            pltpu.VMEM((2, 3, 4, 176, 128), BF16),
            pltpu.VMEM((2, 4, 168, 128), F32),
            pltpu.VMEM((2, 3, 176, 128), BF16),
            pltpu.VMEM((2, 3, 176, 128), BF16),
            pltpu.VMEM((168, 256), F32),
            pltpu.VMEM((168, 256), F32),
            pltpu.VMEM((16, 176, RANK), BF16),
            pltpu.VMEM((4, 8, 256), F32),
            pltpu.VMEM((4, 8, 256), F32),
            pltpu.VMEM((8, 8, 256), F32),
            pltpu.VMEM((2, 8, 256), F32),
            pltpu.SemaphoreType.DMA((39,)),
            pltpu.SemaphoreType.DMA((39,)),
            pltpu.SemaphoreType.DMA((2 * GATHER_SLOTS,)),
            pltpu.SemaphoreType.DMA((2 * GATHER_SLOTS,)),
        ],
        compiler_params=pltpu.CompilerParams(
            collective_id=3, has_side_effects=True, vmem_limit_bytes=VMEM_LIMIT
        ),
    )(part.reshape(4, 4, 168, RANK))


def final_kernel(o_ref, inv_ref, c_ref, buf_ref, scale_ref, mom_ref, upd_ref, lhs):
    rows = o_ref.shape[0]

    @pl.when(pl.program_id(0) == 0)
    def _():
        o = o_ref[...]
        oi = o * inv_ref[...]
        for j, v in enumerate((o, oi)):
            top = v.astype(BF16)
            lhs[2 * j * rows:(2 * j + 1) * rows, :] = top
            lhs[(2 * j + 1) * rows:(2 * j + 2) * rows, :] = (v - top.astype(F32)).astype(BF16)

    out = lax.dot_general(lhs[...], c_ref[...], (((1,), (1,)), ((), ())), preferred_element_type=F32)
    mom_ref[...] = buf_ref[...] - (1.0 - MOMENTUM) * (out[0:rows] + out[rows:2 * rows])
    upd_ref[...] = (out[2 * rows:3 * rows] + out[3 * rows:4 * rows]) * scale_ref[...]


def final_products(o, inv, coeffs, buffer, scale):
    rows, cols = buffer.shape
    tile = 384
    return pl.pallas_call(
        final_kernel,
        grid=(cols // tile,),
        out_shape=(jax.ShapeDtypeStruct(buffer.shape, F32), jax.ShapeDtypeStruct(buffer.shape, F32)),
        in_specs=[
            pl.BlockSpec((rows, RANK), lambda i: (0, 0)),
            pl.BlockSpec((1, RANK), lambda i: (0, 0)),
            pl.BlockSpec((tile, RANK), lambda i: (i, 0)),
            pl.BlockSpec((rows, tile), lambda i: (0, i)),
            pl.BlockSpec((1, tile), lambda i: (0, i)),
        ],
        out_specs=(pl.BlockSpec((rows, tile), lambda i: (0, i)), pl.BlockSpec((rows, tile), lambda i: (0, i))),
        scratch_shapes=[pltpu.VMEM((4 * rows, RANK), BF16)],
        compiler_params=pltpu.CompilerParams(vmem_limit_bytes=VMEM_LIMIT),
    )(o, inv, coeffs, buffer, scale)


def per_device(inputs, norm_gain, out_grad, weight, moment, right_basis):
    tensor_count = lax.axis_size("tensor")
    tensor_index = lax.axis_index("tensor")
    width = inputs.shape[1]
    group_cols = weight.shape[1]
    widened = inputs.astype(F32)
    row_mean = jnp.mean(widened, axis=1, keepdims=True)
    centered = widened - row_mean
    row_var = jnp.mean(centered * centered, axis=1, keepdims=True)
    inv_std = lax.rsqrt(row_var + NORM_EPSILON)
    standard = centered * inv_std
    normed = (standard * norm_gain).astype(BF16)
    feature_block = lax.all_to_all(normed, "dp", split_axis=1, concat_axis=0, tiled=True)
    basis_all, shard_in = gather_both(right_basis, out_grad)
    grad_acc = lax.dot_general(feature_block, shard_in, (((0,), (0,)), ((), ())), preferred_element_type=F32)
    buffer = moment + grad_acc
    part = jnp.dot(buffer, basis_all, precision=HI, preferred_element_type=F32)
    projected, gram = projected_gram(part)
    ortho_t = chol_solve(gram, projected.T)
    coeff_part = lax.dot_general(
        buffer, ortho_t, (((0,), (1,)), ((), ())), precision=lax.Precision.HIGH, preferred_element_type=F32
    )
    coeffs, coeff_own, squares = coeff_sum(coeff_part)
    col_inverse = 1.0 / (jnp.sqrt(squares[0:1]) + 1e-08)
    basis_new = coeff_own * col_inverse
    qkv_group = 3 * HEADS * HEAD_DIM // tensor_count
    qkv_scale = 0.2 * math.sqrt(D * (3 * HEADS * HEAD_DIM) / RANK)
    mlp_scale = 0.2 * math.sqrt(D * FF / RANK)
    position = jnp.arange(group_cols, dtype=jnp.int32)
    col_scale = jnp.where(position < qkv_group, qkv_scale, mlp_scale).astype(F32)
    moment_new, update = final_products(ortho_t.T, col_inverse, coeffs, buffer, col_scale[None, :])

    share_cols = width // tensor_count
    offset = tensor_index * share_cols
    back_rows = lax.dot_general(shard_in, weight, (((1,), (1,)), ((), ())), preferred_element_type=F32)
    back_mine = lax.all_to_all(back_rows, "dp", split_axis=0, concat_axis=1, tiled=True)
    normed_grad = lax.psum_scatter(back_mine, "tensor", scatter_dimension=1, tiled=True)
    standard_here = lax.dynamic_slice_in_dim(standard, offset, share_cols, 1)
    gain_here = lax.dynamic_slice_in_dim(norm_gain, offset, share_cols, 0)
    scaled_grad = normed_grad * gain_here
    sums = jnp.stack([jnp.sum(scaled_grad, axis=1), jnp.sum(scaled_grad * standard_here, axis=1)])
    sums = lax.psum(sums, "tensor") * (1.0 / width)
    full_grad = inv_std * (scaled_grad - sums[0][:, None] - standard_here * sums[1][:, None])
    input_grad = full_grad.astype(BF16)
    gain_grad = lax.psum(jnp.sum(normed_grad * standard_here, axis=0), "dp")
    return (input_grad, gain_grad, moment_new, basis_new, update)


def solution(mesh):
    in_specs = (
        P("dp", None),
        P(),
        P("dp", "tensor"),
        P("dp", "tensor"),
        P("dp", "tensor"),
        P(("tensor", "dp"), None),
    )
    out_specs = (
        P("dp", "tensor"),
        P("tensor"),
        P("dp", "tensor"),
        P(("tensor", "dp"), None),
        P("dp", "tensor"),
    )
    return jax.shard_map(
        per_device, mesh=mesh, in_specs=in_specs, out_specs=out_specs, check_vma=False
    )
```

time: 818 us -> 347 us (0.42); the launches traced: 808 us -> 346 us
  waiting for transfers between devices: 289 us -> 22.4 us
  Pallas kernels: 0 us -> 182 us
  blocking collectives: 221 us -> 77.7 us
  other arithmetic: 147 us -> 6.96 us
  local copies, waits for them, and re-layouts: 51.1 us -> 7.69 us
  matrix products: 64.7 us -> 25.9 us
  starting transfers between devices: 18 us -> 8.47 us
    psum x2 -> x0, waiting for transfers between devices: 187 us -> none  [the longest x1 117 us: per_device(): gram = lax.psum(jnp.dot(projected.T, projected, precision=PRECISE), 'dp')]
    pallas_call x0 -> x5, Pallas kernels: none -> 182 us  [the longest x1 54.7 us: projected_gram(): pl.pallas_call(gram_kernel, out_shape=(jax.ShapeDtypeStruct(part.shape, F...]
    another operation x17 -> x1, other arithmetic: 135 us -> 0.01 us  [per_device(): jnp.stack([jnp.sum(scaled_grad, axis=1), jnp.sum(scaled_grad * standard_h...]
    all_gather x3 -> x0, waiting for transfers between devices: 94.9 us -> none  [the longest x1 47.9 us: per_device(): shard_in = lax.all_gather(out_grad, 'dp', axis=0, tiled=True)]
    unnamed x1 -> x0, blocking collectives: 76.9 us -> none
    psum x2, blocking collectives: 144 us -> 77.7 us  [the longest x1 66.2 us: per_device(): gain_grad = lax.psum(jnp.sum(normed_grad * standard_here, axis=0), 'dp')]
    unnamed x49 -> x12, local copies, waits for them, and re-layouts: 23.9 us -> 0.03 us
    dot_general x5 -> x2, matrix products: 37.2 us -> 15.9 us  [the longest x1 8.03 us: per_device(): part = jnp.dot(buffer, basis_all, precision=HI, preferred_element_type=F32)]
  transfers between devices with their start and end apart: 9 -> 3, of which waited for: 6 -> 2; matrix products, arithmetic and copies ran while one was open for 4% -> 9% of each run, Pallas kernels for 0% -> 39%
where the time goes in v1:
time: 347 us; the launch traced here: 346 us
  Pallas kernels  182 us (52%)
  blocking collectives  77.7 us (22%)
  matrix products  25.9 us (7%)
  waiting for transfers between devices  22.4 us (6%)
  between operations  14.2 us (4%)
  starting transfers between devices  8.47 us (2%)
  local copies, waits for them, and re-layouts  7.69 us (2%)
  other arithmetic  6.96 us (2%)
    psum x1, blocking collectives, per_device(): gain_grad = lax.psum(jnp.sum(normed_grad * standard_here, axis=0), 'dp')  66.2 us
    pallas_call x1, Pallas kernels, projected_gram(): pl.pallas_call(gram_kernel, out_shape=(jax.ShapeDtypeStruct(part.shape, F...  54.7 us
    pallas_call x1, Pallas kernels, coeff_sum(): pl.pallas_call(coeff_kernel, out_shape=(jax.ShapeDtypeStruct((2688, RANK)...  49.7 us
    pallas_call x1, Pallas kernels, gather_both(): pl.pallas_call(gather_kernel, out_shape=(jax.ShapeDtypeStruct((32 * right...  46.7 us
    pallas_call x1, Pallas kernels, chol_solve(): pl.pallas_call(chol_kernel, out_shape=jax.ShapeDtypeStruct((RANK, n_p), F...  23.1 us
    all_to_all x1, waiting for transfers between devices, per_device(): lax.all_to_all(back_rows, 'dp', split_axis=0, concat_axis=1, tiled=True)  13.5 us
    psum x1, blocking collectives, per_device(): sums = lax.psum(sums, 'tensor') * (1.0 / width)  11.6 us
    all_to_all x1, waiting for transfers between devices, per_device(): lax.all_to_all(normed, 'dp', split_axis=1, concat_axis=0, tiled=True)  8.87 us
  transfers between devices with their start and end apart: 3, of which 2 were waited for; matrix products, arithmetic and copies ran while one was open for 9% of the time, Pallas kernels for 39%

profile of v1, /device:TPU:1, one launch (start us, length us, event | category | flops | bytes accessed | tf_op | source)
XLA Modules:
  0.0 345.6 jit_solution(14783698649374909974)
XLA Ops:
  7.2 0.0 copy-start
  7.2 46.7 %shard_map.101 = (f32[2688,512]{1,0:T(8,128)}, bf16[1024,2688]{1,0:T(8,128)(2,1)}) custom-call(f32[84,512]{1,0:T(8,128)} %r_ref.1, bf16[32,2688]{1,0:T(8,128)(2,1)} %g_ref.1), custom_call_target="tpu_custom_call" | custom-call | tf_op jit(solution)/shard_map/pallas_call | solution.py:209
  53.8 0.0 copy-done
  53.9 0.0 copy-start.2
  53.9 5.2 %fusion.3 = f32[1024,192]{1,0:T(8,128)} fusion(bf16[1024,2688]{1,0:T(8,128)(2,1)} %get-tuple-element.14, bf16[192,2688]{1,0:T(8,128)(2,1)S(1)} %copy-done), kind=kOutput, calls=%fused_computation.20 | convolution fusion | flops 1056964608 | bytes 7323648 | tf_op jit(solution)/shard_map/dot_general | solution.py:693
  59.1 0.0 copy-start.4
  59.1 3.9 %all-to-all-start = ((f32[32,32,192]{2,1,0:T(8,128)}), f32[32,32,192]{2,1,0:T(8,128)S(1)}, u32[]{:S(2)}, u32[]{:S(2)}) async-start(f32[32,32,192]{2,1,0:T(8,128)} %bitcast), calls=%async_computation | async-start | bytes 2097152 | tf_op jit(solution)/shard_map/all_to_all | solution.py:694
  63.0 0.0 copy-done.2
  63.0 0.2 convert_reduce_fusion
  63.2 0.3 fusion.2
  63.5 0.0 copy-done.4
  63.5 1.1 multiply_convert_fusion
  64.6 0.6 all_to_all.32
  65.2 1.1 copy.20
  66.3 13.5 %all-to-all-done = f32[32,32,192]{2,1,0:T(8,128)S(1)} async-done(((f32[32,32,192]{2,1,0:T(8,128)}), f32[32,32,192]{2,1,0:T(8,128)S(1)}, u32[]{:S(2)}, u32[]{:S(2)}) %all-to-all-start) | async-done | bytes 786464 | tf_op jit(solution)/shard_map/all_to_all | solution.py:694
  79.8 4.4 %all-to-all-start.1 = ((bf16[32,32,192]{2,0,1:T(8,128)(2,1)}), bf16[32,32,192]{2,0,1:T(8,128)(2,1)}, u32[]{:S(2)}, u32[]{:S(2)}) async-start(bf16[32,32,192]{2,0,1:T(8,128)(2,1)} %copy.20), calls=%async_computation.2 | async-start | bytes 1048576 | tf_op jit(solution)/shard_map/all_to_all | solution.py:671
  84.2 0.2 reduce-scatter.2.cloned.1.call-start
  84.4 0.1 dynamic_slice.6
  84.5 0.6 compare_select_fusion.scale_ref
  85.1 0.6 copy.19
  85.7 1.3 all_to_all.31
  87.0 0.0 reduce-scatter.2.cloned.1.call-update
  87.0 8.9 %all-to-all-done.1 = bf16[32,32,192]{2,0,1:T(8,128)(2,1)} async-done(((bf16[32,32,192]{2,0,1:T(8,128)(2,1)}), bf16[32,32,192]{2,0,1:T(8,128)(2,1)}, u32[]{:S(2)}, u32[]{:S(2)}) %all-to-all-start.1) | async-done | bytes 393248 | tf_op jit(solution)/shard_map/all_to_all | solution.py:671
  95.9 4.7 %convolution_add_fusion.buf_ref = f32[192,2688]{1,0:T(8,128)S(1)} fusion(f32[192,2688]{1,0:T(8,128)} %param.10, bf16[1024,192]{1,0:T(8,128)(2,1)} %bitcast.7, bf16[1024,2688]{1,0:T(8,128)(2,1)} %get-tuple-element.14), kind=kOutput, calls=%fused_computation | convolution fusion | flops 1057480704 | bytes 10027008 | tf_op jit(solution)/shard_map/dot_general | solution.py:673
  100.6 0.0 copy-start.1
  100.6 8.0 %fusion.4.part_ref = f32[192,512]{1,0:T(8,128)} fusion(f32[192,2688]{1,0:T(8,128)S(1)} %convolution_add_fusion.buf_ref, f32[2688,512]{1,0:T(8,128)} %get-tuple-element.15), kind=kOutput, calls=%fused_computation.21 | convolution fusion | flops 3170893824 | bytes 7962624 | tf_op jit(solution)/shard_map/dot_general | solution.py:675
  108.6 54.7 %shard_map.102 = (f32[192,512]{1,0:T(8,128)}, f32[8,2,4,8,512]{4,3,2,1,0:T(8,128)}) custom-call(f32[192,512]{1,0:T(8,128)} %fusion.4.part_ref), custom_call_target="tpu_custom_call" | custom-call | tf_op jit(solution)/shard_map/pallas_call | solution.py:308
  163.3 2.0 copy.21
  165.3 23.1 %shard_map.103 = f32[512,192]{1,0:T(8,128)} custom-call(f32[512,512]{1,0:T(8,128)} %bitcast.28, f32[512,192]{1,0:T(8,128)} %bitcast.26), custom_call_target="tpu_custom_call" | custom-call | tf_op jit(solution)/shard_map/pallas_call | solution.py:400
  188.4 2.0 copy.22
  190.4 0.0 copy-done.1
  190.4 7.9 %fusion.5 = f32[2688,512]{1,0:T(8,128)} fusion(f32[192,2688]{1,0:T(8,128)S(1)} %convolution_add_fusion.buf_ref, f32[512,192]{1,0:T(8,128)} %shard_map.103), kind=kOutput, calls=%fused_computation.22 | convolution fusion | flops 1585446912 | bytes 7962624 | tf_op jit(solution)/shard_map/dot_general | solution.py:678
  198.3 49.7 %shard_map.104 = (bf16[2688,512]{1,0:T(8,128)(2,1)}, f32[84,512]{1,0:T(8,128)}, f32[8,512]{1,0:T(8,128)}) custom-call(f32[4,4,168,512]{3,2,1,0:T(8,128)} %bitcast.24), custom_call_target="tpu_custom_call" | custom-call | tf_op jit(solution)/shard_map/pallas_call | solution.py:588
  248.0 0.0 copy-start.3
  248.0 1.4 add_divide_fusion.inv_ref
  249.3 0.0 copy-start.5
  249.3 8.3 %shard_map.105 = (f32[192,2688]{1,0:T(8,128)}, f32[192,2688]{1,0:T(8,128)}) custom-call(f32[192,512]{1,0:T(8,128)} %bitcast.27, f32[1,512]{1,0:T(1,128)} %add_divide_fusion.inv_ref, bf16[2688,512]{1,0:T(8,128)(2,1)} %get-tuple-element.19.c_ref, f32[192,2688]{1,0:T(8,128)} %copy-done.1, f32[1,2688]{1,0:T(1,128)} %compare_select_fusion.scale_ref), custom_call_target="tpu_custom_call" | custom-call | tf_op jit(solution)/shard_map/pallas_call | solution.py:642
  257.6 0.0 copy-done.3
  257.6 0.0 copy-done.5
  257.6 0.7 broadcast_multiply_fusion
  258.3 0.0 reduce-scatter.2.cloned.1.call-done
  258.3 1.1 multiply_reduce_fusion
  259.4 11.6 %psum.14 = f32[2,32]{1,0:T(2,128)S(1)} all-reduce(f32[2,32]{1,0:T(2,128)S(1)} %pad_maximum_fusion), channel_id=1, replica_groups=mesh['dp'=32,'tensor'=8] {'tensor'}, use_global_device_ids=true, to_apply=%region_5.6 | all-reduce | flops 64 | bytes 512 | tf_op jit(solution)/shard_map/psum | solution.py:700
  270.9 66.2 %psum.15 = f32[768]{0:T(1024)} all-reduce(f32[768]{0:T(1024)S(1)} %get-tuple-element.23), channel_id=1, replica_groups=mesh['dp'=32,'tensor'=8] {'dp'}, use_global_device_ids=true, to_apply=%region_7.8 | all-reduce | flops 768 | bytes 6144 | tf_op jit(solution)/shard_map/psum | solution.py:703
  337.1 1.6 multiply_convert_fusion.1
  (5 shorter events, 0.0 us)
Async XLA Ops:
  7.2 46.7 %copy-start = (bf16[192,2688]{1,0:T(8,128)(2,1)S(1)}, bf16[192,2688]{1,0:T(8,128)(2,1)}, u32[]{:S(2)}) copy-start(bf16[192,2688]{1,0:T(8,128)(2,1)} %param.9) | copy-start | bytes 3096580
  53.9 9.1 %copy-start.2 = (bf16[32,6144]{1,0:T(8,128)(2,1)S(1)}, bf16[32,6144]{1,0:T(8,128)(2,1)}, u32[]{:S(2)}) copy-start(bf16[32,6144]{1,0:T(8,128)(2,1)} %param.6) | copy-start | bytes 1179652
  59.1 4.4 %copy-start.4 = (f32[6144]{0:T(1024)S(1)}, f32[6144]{0:T(1024)}, u32[]{:S(2)}) copy-start(f32[6144]{0:T(1024)} %param.7) | copy-start | bytes 73732
  59.1 20.7 %all-to-all-start = ((f32[32,32,192]{2,1,0:T(8,128)}), f32[32,32,192]{2,1,0:T(8,128)S(1)}, u32[]{:S(2)}, u32[]{:S(2)}) async-start(f32[32,32,192]{2,1,0:T(8,128)} %bitcast), calls=%async_computation | async-start | bytes 2097152 | tf_op jit(solution)/shard_map/all_to_all | solution.py:694
  79.8 16.1 %all-to-all-start.1 = ((bf16[32,32,192]{2,0,1:T(8,128)(2,1)}), bf16[32,32,192]{2,0,1:T(8,128)(2,1)}, u32[]{:S(2)}, u32[]{:S(2)}) async-start(bf16[32,32,192]{2,0,1:T(8,128)(2,1)} %copy.20), calls=%async_computation.2 | async-start | bytes 1048576 | tf_op jit(solution)/shard_map/all_to_all | solution.py:671
  84.2 174.1 %reduce-scatter.2.cloned.1.call-start = ((), (), s32[]{:S(2)}) async-start(), calls=%async_computation.3 | async-start | bytes 884736 | tf_op jit(solution)/shard_map/reduce_scatter | solution.py:695
  100.6 89.8 %copy-start.1 = (f32[192,2688]{1,0:T(8,128)}, f32[192,2688]{1,0:T(8,128)S(1)}, u32[]{:S(2)}) copy-start(f32[192,2688]{1,0:T(8,128)S(1)} %convolution_add_fusion.buf_ref) | copy-start | bytes 6193156
  248.0 9.6 %copy-start.3 = (f32[84,512]{1,0:T(8,128)S(1)}, f32[84,512]{1,0:T(8,128)}, u32[]{:S(2)}) copy-start(f32[84,512]{1,0:T(8,128)} %get-tuple-element.21) | copy-start | bytes 516100
  249.3 8.3 %copy-start.5 = (f32[1,512]{1,0:T(1,128)S(1)}, f32[1,512]{1,0:T(1,128)}, u32[]{:S(2)}) copy-start(f32[1,512]{1,0:T(1,128)} %add_divide_fusion.inv_ref) | copy-start | bytes 6148
Sparse Core Ops, SparseCore 0:
  87.6 40.7 reduce-scatter.1

commit v2 on v1

--- a/solution.py
+++ b/solution.py
@@ -54,14 +54,12 @@
     pl.semaphore_wait(barrier, len(peers))
 
 
-def plane_neighbours(x, y, core):
-    return [
-        {"dp": dp_of((x + 1) % 4, y, core)},
-        {"dp": dp_of((x + 3) % 4, y, core)},
-        {"dp": dp_of(x, (y + 1) % 4, core)},
-        {"dp": dp_of(x, (y + 3) % 4, core)},
-        {"dp": dp_of(x, y, 1 - core)},
-    ]
+def plane_peers(x, y, core):
+    return (
+        [{"dp": dp_of((x + d) % 4, y, core)} for d in (1, 2, 3)]
+        + [{"dp": dp_of(x, (y + d) % 4, core)} for d in (1, 2, 3)]
+        + [{"dp": dp_of(x, y, 1 - core)}]
+    )
 
 
 def round_robin(generators):
@@ -149,12 +147,39 @@
 
 
 GATHER_SLOTS = 36
-
-
-def gather_kernel(r_ref, g_ref, rall_ref, gall_ref, got_ref, ssem, rsem, hsem):
+EXCHANGE_SLOTS = 7
+
+
+def exchange_stream(src, xbuf, ybuf, out, ssem, rsem, base, sent):
+    x, y, core, _ = place()
+    sib = dp_of(x, y, 1 - core)
+    for i in range(3):
+        to = (x + 1 + i) % 4
+        sent.append(send(src.at[to], xbuf.at[x], ssem.at[base + i], rsem.at[base + i], dp=dp_of(to, y, core)))
+    xbuf[x] = src[x]
+    yield
+    for i in range(3):
+        wait_recv(xbuf.at[(x + 3 - i) % 4], rsem.at[base + i], dp=sib)
+    for i in range(3):
+        to = (y + 1 + i) % 4
+        sent.append(send(
+            xbuf.at[:, to], ybuf.at[:, y], ssem.at[base + 3 + i], rsem.at[base + 3 + i], dp=dp_of(x, to, core)
+        ))
+    ybuf[:, y] = xbuf[:, y]
+    yield
+    for i in range(3):
+        wait_recv(ybuf.at[:, (y + 3 - i) % 4], rsem.at[base + 3 + i], dp=sib)
+    sent.append(send(ybuf.at[:, :, 1 - core], out.at[:, :, core], ssem.at[base + 6], rsem.at[base + 6], dp=sib))
+    out[:, :, core] = ybuf[:, :, core]
+    yield
+    wait_recv(out.at[:, :, 1 - core], rsem.at[base + 6], dp=sib)
+    yield
+
+
+def gather_kernel(r_ref, g_ref, n_ref, rall_ref, gall_ref, nall_ref, got_ref, xbuf, ybuf, ssem, rsem, hsem):
     x, y, core, _ = place()
     chip = x * 4 + y
-    greet(plane_neighbours(x, y, core))
+    greet(plane_peers(x, y, core))
     rows = r_ref.shape[0]
     tokens = g_ref.shape[0]
     cols = g_ref.shape[1]
@@ -199,34 +224,45 @@
         gather_stream(loc_r(0), "x", ssem, rsem, 0, sent),
         gather_stream(loc_r(1), "y", ssem, rsem, GATHER_SLOTS, sent),
     ]
-    round_robin(r_streams + g_streams)
+    round_robin(
+        r_streams + g_streams + [exchange_stream(n_ref, xbuf, ybuf, nall_ref, ssem, rsem, 4 * GATHER_SLOTS, sent)]
+    )
     for copy in sent:
         copy.wait_send()
 
 
-def gather_both(right_basis, out_grad):
+def gather_both(right_basis, out_grad, normed):
     vm = pl.BlockSpec(memory_space=pltpu.VMEM)
     return pl.pallas_call(
         gather_kernel,
         out_shape=(
             jax.ShapeDtypeStruct((32 * right_basis.shape[0], RANK), F32),
             jax.ShapeDtypeStruct((32 * out_grad.shape[0], out_grad.shape[1]), BF16),
+            jax.ShapeDtypeStruct(normed.shape, BF16),
         ),
-        in_specs=[vm, vm],
-        out_specs=(vm, vm),
+        in_specs=[vm, vm, vm],
+        out_specs=(vm, vm, vm),
         scratch_shapes=[
             pltpu.VMEM((right_basis.shape[0], 256), F32),
-            pltpu.SemaphoreType.DMA((4 * GATHER_SLOTS,)),
-            pltpu.SemaphoreType.DMA((4 * GATHER_SLOTS,)),
+            pltpu.VMEM(normed.shape, BF16),
+            pltpu.VMEM(normed.shape, BF16),
+            pltpu.SemaphoreType.DMA((4 * GATHER_SLOTS + EXCHANGE_SLOTS,)),
+            pltpu.SemaphoreType.DMA((4 * GATHER_SLOTS + EXCHANGE_SLOTS,)),
             pltpu.SemaphoreType.DMA((3,)),
         ],
         compiler_params=pltpu.CompilerParams(
             collective_id=1, has_side_effects=True, vmem_limit_bytes=VMEM_LIMIT
         ),
-    )(right_basis, out_grad)
-
-
-def gram_kernel(part_ref, p_ref, g_ref, zbuf, gbuf, cbuf, xbuf, ybuf, ssem, rsem):
+    )(right_basis, out_grad, normed)
+
+
+def split(v):
+    top = v.astype(BF16)
+    return top, (v - top.astype(F32)).astype(BF16)
+
+
+def gram_kernel(b_ref, r_ref, back_ref, p_ref, g_ref, bt_ref, btsib_ref, backall_ref,
+                both, part_ref, zbuf, gbuf, cbuf, xbuf, ybuf, ex, ey, ssem, rsem):
     x, y, core, z = place()
     xs = [(x + d) % 4 for d in (1, 2, 3)]
     ys = [(y + d) % 4 for d in (1, 2, 3)]
@@ -241,12 +277,28 @@
     )
     sent = []
     order = (3, 4, 2, 5, 1, 6, 0)
+    back = exchange_stream(back_ref, ex, ey, backall_ref, ssem, rsem, 36, sent)
+    next(back)
+    rows, cols = b_ref.shape
+    top, low = split(b_ref[...])
+    both[0:rows, :] = top
+    both[rows:2 * rows, :] = low
+    part_ref[...] = jnp.zeros_like(part_ref)
+    for t in range(0, cols, 384):
+        r_top, r_low = split(r_ref[t:t + 384, :])
+        one = jnp.dot(both[:, t:t + 384], r_top, preferred_element_type=F32)
+        two = jnp.dot(both[0:rows, t:t + 384], r_low, preferred_element_type=F32)
+        part_ref[...] += one[0:rows] + (one[rows:] + two)
 
     def rows24(q):
         return pl.ds(pl.multiple_of(24 * q, 8), 24)
 
     for i in order:
         sent.append(send(part_ref.at[rows24(zs[i])], zbuf.at[i], ssem.at[i], rsem.at[i], tensor=zs[i]))
+    for t in range(0, cols, 384):
+        bt_ref[t:t + 384, :] = both[:, t:t + 384].astype(F32).T.astype(BF16)
+    sent.append(send(bt_ref, btsib_ref, ssem.at[35], rsem.at[35], dp=sib))
+    next(back)
     total = part_ref[rows24(z), :]
     for i in reversed(order):
         wait_recv(zbuf.at[i], rsem.at[i], tensor=zs[i])
@@ -258,6 +310,7 @@
     for i in reversed(order):
         src = (z + 7 - i) % 8
         wait_recv(p_ref.at[rows24(src)], rsem.at[7 + i], tensor=zs[i])
+    next(back)
 
     gbuf[...] = lax.dot_general(
         p_ref[:, pl.ds(pl.multiple_of(128 * (z // 2), 128), 128)], p_ref[...],
@@ -299,40 +352,50 @@
     wait_recv(g_ref.at[:, 1 - core, x], rsem.at[31], dp=sib)
     for i in range(3):
         wait_recv(g_ref.at[:, 1 - core, (x + 3 - i) % 4], rsem.at[32 + i], dp=sib)
+    next(back)
+    wait_recv(btsib_ref, rsem.at[35], dp=sib)
     for copy in sent:
         copy.wait_send()
 
 
-def projected_gram(part):
+def projected_gram(buffer, basis, back):
     vm = pl.BlockSpec(memory_space=pltpu.VMEM)
-    p, g = pl.pallas_call(
+    rows, cols = buffer.shape
+    p, g, bt, bt_sib, back_all = pl.pallas_call(
         gram_kernel,
         out_shape=(
-            jax.ShapeDtypeStruct(part.shape, F32),
+            jax.ShapeDtypeStruct((rows, RANK), F32),
             jax.ShapeDtypeStruct((8, 2, 4, 8, RANK), F32),
+            jax.ShapeDtypeStruct((cols, 2 * rows), BF16),
+            jax.ShapeDtypeStruct((cols, 2 * rows), BF16),
+            jax.ShapeDtypeStruct(back.shape, F32),
         ),
-        in_specs=[vm],
-        out_specs=(vm, vm),
+        in_specs=[vm, vm, vm],
+        out_specs=(vm, vm, vm, vm, vm),
         scratch_shapes=[
+            pltpu.VMEM((2 * rows, cols), BF16),
+            pltpu.VMEM((rows, RANK), F32),
             pltpu.VMEM((7, 24, RANK), F32),
             pltpu.VMEM((128, RANK), F32),
             pltpu.VMEM((32, RANK), F32),
             pltpu.VMEM((3, 8, RANK), F32),
             pltpu.VMEM((4, 8, RANK), F32),
-            pltpu.SemaphoreType.DMA((35,)),
-            pltpu.SemaphoreType.DMA((35,)),
+            pltpu.VMEM(back.shape, F32),
+            pltpu.VMEM(back.shape, F32),
+            pltpu.SemaphoreType.DMA((36 + EXCHANGE_SLOTS,)),
+            pltpu.SemaphoreType.DMA((36 + EXCHANGE_SLOTS,)),
         ],
         compiler_params=pltpu.CompilerParams(
             collective_id=2, has_side_effects=True, vmem_limit_bytes=VMEM_LIMIT
         ),
-    )(part)
-    return p, g.reshape(RANK, RANK)
-
-
-def chol_kernel(g_ref, p_ref, ot_ref, s_ref, w_ref):
-    n_p = p_ref.shape[1]
+    )(buffer, basis, back)
+    return p, g.reshape(RANK, RANK), bt, bt_sib, back_all
+
+
+def chol_kernel(g_ref, p_ref, o_ref, s_ref, w_ref):
+    n_p = p_ref.shape[0]
     s_ref[:, 0:512] = g_ref[...]
-    s_ref[:, 512:512 + n_p] = p_ref[...]
+    s_ref[:, 512:512 + n_p] = p_ref[...].T
     s_ref[:, 512 + n_p:] = jnp.zeros((512, s_ref.shape[1] - 512 - n_p), F32)
     lane = lax.broadcasted_iota(jnp.int32, (8, 128), 1)
     sub = lax.broadcasted_iota(jnp.int32, (8, 128), 0)
@@ -391,27 +454,28 @@
         return carry
 
     lax.fori_loop(0, 4, block, 0)
-    ot_ref[...] = s_ref[:, 512:512 + n_p]
-
-
-def chol_solve(gram, projected_t):
-    n_p = projected_t.shape[1]
+    o_ref[...] = s_ref[:, 512:512 + n_p].T
+
+
+def chol_solve(gram, projected):
     vm = pl.BlockSpec(memory_space=pltpu.VMEM)
     return pl.pallas_call(
         chol_kernel,
-        out_shape=jax.ShapeDtypeStruct((RANK, n_p), F32),
+        out_shape=jax.ShapeDtypeStruct(projected.shape, F32),
         in_specs=[vm, vm],
         out_specs=vm,
         scratch_shapes=[pltpu.VMEM((RANK, 768), F32), pltpu.VMEM((128, 128), F32)],
         compiler_params=pltpu.CompilerParams(vmem_limit_bytes=VMEM_LIMIT),
-    )(gram, projected_t)
+    )(gram, projected)
 
 
 SPLIT = ((0, 96), (96, 80), (0, 176))
 
 
-def coeff_kernel(c_ref, call_ref, cown_ref, csq_ref, pair, sbuf, rbuf, acc, s2, r2, fin, fsib, agb,
-                 xsq, ysq, zsq, sqs, ssem, rsem, gs, gr):
+def coeff_kernel(bt_ref, btsib_ref, o_ref, back_ref, std_ref, gain_ref, inv_ref,
+                 call_ref, cown_ref, csq_ref, ig_ref, gg_ref,
+                 osib, rhs, c_ref, sbuf, rbuf, acc, s2, r2, fin, fsib, agb,
+                 xsq, ysq, zsq, sqs, ngbuf, stat, gx, gy, gc, ssem, rsem, gs, gr, ns, nr):
     x, y, core, z = place()
     sib = dp_of(x, y, 1 - core)
     xs = [(x + d) % 4 for d in (1, 2, 3)]
@@ -426,35 +490,42 @@
     sent = []
     first = ("x", "y")
 
-    def chunk(ref, s, a, cols=None):
-        a = a % 4
-        if cols is None:
-            return ref.at[s, a] if s == 0 else ref.at[s, :, a]
-        return ref.at[a, :, :, cols] if s == 0 else ref.at[:, a, :, cols]
+    def half(who):
+        return pl.ds(pl.multiple_of(256 * who, 128), 256)
+
+    sent.append(send(o_ref.at[:, half(1 - core)], osib, ssem.at[0], rsem.at[0], dp=sib))
+    for i in range(7):
+        sent.append(send(back_ref.at[zs[i]], ngbuf.at[i], ns.at[i], nr.at[i], tensor=zs[i]))
+
+    def fill(v):
+        top, low = split(v)
+        n = v.shape[0]
+        rhs[0:n, 0:256] = top
+        rhs[n:2 * n, 0:256] = top
+        rhs[0:n, 256:512] = low
+        rhs[n:2 * n, 256:512] = low
+
+    cols = bt_ref.shape[0]
+    fill(o_ref[:, half(core)])
+    for t in range(0, cols, 384):
+        two = jnp.dot(bt_ref[t:t + 384, :], rhs[...], preferred_element_type=F32)
+        c_ref[t:t + 384, :] = two[:, 0:256] + two[:, 256:512]
+    wait_recv(osib, rsem.at[0], dp=sib)
+    fill(osib[...])
+    for t in range(0, cols, 384):
+        two = jnp.dot(btsib_ref[t:t + 384, :], rhs[...], preferred_element_type=F32)
+        c_ref[t:t + 384, :] += two[:, 0:256] + two[:, 256:512]
 
     def cols_of(who, s):
         return pl.ds(pl.multiple_of(256 * who + 128 * s, 128), 128)
 
     a0 = (x, y)
     b0 = (y, x)
-    n = 0
-    pieces = {}
-    for off in (2, 1, 3, 0):
-        for s in (0, 1):
-            sent.append(send(
-                chunk(c_ref, s, a0[s] + off, cols_of(1 - core, s)), chunk(pair, s, a0[s] + off),
-                ssem.at[n], rsem.at[n], dp=sib,
-            ))
-            pieces[off, s] = n
-            n += 1
 
     def own(s, off, b):
         a = (a0[s] + off) % 4
         bx, by = (a, b) if s == 0 else (b, a)
-        return c_ref[bx, by, :, cols_of(core, s)] + pair[s, bx, by]
-
-    def pair_ready(s, off):
-        wait_recv(chunk(pair, s, a0[s] + off), rsem.at[pieces[off, s]], dp=sib)
+        return c_ref[pl.ds(pl.multiple_of(168 * (bx * 4 + by), 8), 168), 128 * s:128 * s + 128]
 
     def dev(s, a, b):
         a, b = a % 4, b % 4
@@ -469,14 +540,11 @@
         base = 8 + 8 * s
         a, b = a0[s], b0[s]
         right, left = dev(s, a + 1, b), dev(s, a - 1, b)
-        pair_ready(s, 2)
         for j in range(4):
             sbuf[s, 0, j] = padded(own(s, 2, j))
         sent.append(send(sbuf.at[s, 0, 0:2], rbuf.at[s, 0, 0:2], ssem.at[base], rsem.at[base], dp=right))
         sent.append(send(sbuf.at[s, 0, 2:4], rbuf.at[s, 0, 2:4], ssem.at[base + 1], rsem.at[base + 1], dp=left))
         yield
-        pair_ready(s, 1)
-        pair_ready(s, 3)
         for j in (2, 3):
             sbuf[s, 1, j] = padded(own(s, 1, j))
         for j in (0, 1):
@@ -492,7 +560,6 @@
             sbuf[s, 2, j] = padded(own(s, 3, j) + rbuf[s, 0, j, 0:168].astype(F32))
         sent.append(send(sbuf.at[s, 2], rbuf.at[s, 2], ssem.at[base + 3], rsem.at[base + 3], dp=left))
         yield
-        pair_ready(s, 0)
         for j in range(4):
             acc[s, j] = own(s, 0, j)
         yield
@@ -565,6 +632,47 @@
         csq_ref[:, 256:512] = sqs[1]
         yield
 
+    def input_grad():
+        total = back_ref[z]
+        for i in range(7):
+            wait_recv(ngbuf.at[i], nr.at[i], tensor=zs[i])
+            total = total + ngbuf[i]
+        std = std_ref[...]
+        scaled = total * gain_ref[...]
+        lane = lax.broadcasted_iota(jnp.int32, (32, 128), 1)
+
+        def per_token(v):
+            return jnp.sum(jnp.sum(v, axis=0), axis=1, keepdims=True)
+
+        stat[z] = jnp.where(lane < 64, per_token(scaled), per_token(scaled * std))
+        for i in range(7):
+            sent.append(send(stat.at[z], stat.at[z], ns.at[7 + i], nr.at[7 + i], tensor=zs[i]))
+        gx[x] = jnp.broadcast_to(jnp.sum(total * std, axis=1, keepdims=True), gx.shape[1:])
+        for i in range(3):
+            sent.append(send(gx.at[x], gx.at[x], ns.at[14 + i], nr.at[14 + i], dp=dp_of(xs[i], y, core)))
+        yield
+        for i in range(3):
+            wait_recv(gx.at[(x + 3 - i) % 4], nr.at[14 + i], dp=sib)
+        gy[y] = (gx[0] + gx[1]) + (gx[2] + gx[3])
+        for i in range(3):
+            sent.append(send(gy.at[y], gy.at[y], ns.at[17 + i], nr.at[17 + i], dp=dp_of(x, ys[i], core)))
+        for i in range(7):
+            wait_recv(stat.at[(z + 7 - i) % 8], nr.at[7 + i], tensor=zs[i])
+        sums = stat[0]
+        for i in range(1, 8):
+            sums = sums + stat[i]
+        sums = sums * (1.0 / (32 * 192))
+        ig_ref[...] = (inv_ref[...] * (scaled - sums[:, 0:1] - std * sums[:, 64:65])).astype(BF16)
+        yield
+        for i in range(3):
+            wait_recv(gy.at[(y + 3 - i) % 4], nr.at[17 + i], dp=sib)
+        gc[core] = (gy[0] + gy[1]) + (gy[2] + gy[3])
+        sent.append(send(gc.at[core], gc.at[core], ns.at[20], nr.at[20], dp=sib))
+        yield
+        wait_recv(gc.at[1 - core], nr.at[20], dp=sib)
+        gg_ref[...] = gc[0] + gc[1]
+        yield
+
     def loc(s):
         def at(who, bx, by, part):
             lo, rows = SPLIT[part]
@@ -575,6 +683,7 @@
         gather_stream(loc(0), first[0], gs, gr, 0, sent),
         gather_stream(loc(1), first[1], gs, gr, GATHER_SLOTS, sent),
         norms(),
+        input_grad(),
     ])
     for j in range(8):
         two = jnp.concatenate([agb[2 * j, 0:168].astype(F32), agb[2 * j + 1, 0:168].astype(F32)], axis=0)
@@ -583,19 +692,24 @@
         copy.wait_send()
 
 
-def coeff_sum(part):
+def coeff_sum(bt, bt_sib, ortho, back, standard, gain, inv_std):
     vm = pl.BlockSpec(memory_space=pltpu.VMEM)
+    block = standard.shape
     return pl.pallas_call(
         coeff_kernel,
         out_shape=(
             jax.ShapeDtypeStruct((2688, RANK), BF16),
             jax.ShapeDtypeStruct((84, RANK), F32),
             jax.ShapeDtypeStruct((8, RANK), F32),
+            jax.ShapeDtypeStruct(block, BF16),
+            jax.ShapeDtypeStruct((4, 8, 192), F32),
         ),
-        in_specs=[vm],
-        out_specs=(vm, vm, vm),
+        in_specs=[vm] * 7,
+        out_specs=(vm,) * 5,
         scratch_shapes=[
-            pltpu.VMEM((2, 4, 4, 168, 128), F32),
+            pltpu.VMEM((192, 256), F32),
+            pltpu.VMEM((384, RANK), BF16),
+            pltpu.VMEM((2688, 256), F32),
             pltpu.VMEM((2, 3, 4, 176, 128), BF16),
             pltpu.VMEM((2, 3, 4, 176, 128), BF16),
             pltpu.VMEM((2, 4, 168, 128), F32),
@@ -608,15 +722,22 @@
             pltpu.VMEM((4, 8, 256), F32),
             pltpu.VMEM((8, 8, 256), F32),
             pltpu.VMEM((2, 8, 256), F32),
+            pltpu.VMEM((7,) + block, F32),
+            pltpu.VMEM((8, 32, 128), F32),
+            pltpu.VMEM((4, 4, 8, 192), F32),
+            pltpu.VMEM((4, 4, 8, 192), F32),
+            pltpu.VMEM((2, 4, 8, 192), F32),
             pltpu.SemaphoreType.DMA((39,)),
             pltpu.SemaphoreType.DMA((39,)),
             pltpu.SemaphoreType.DMA((2 * GATHER_SLOTS,)),
             pltpu.SemaphoreType.DMA((2 * GATHER_SLOTS,)),
+            pltpu.SemaphoreType.DMA((21,)),
+            pltpu.SemaphoreType.DMA((21,)),
         ],
         compiler_params=pltpu.CompilerParams(
             collective_id=3, has_side_effects=True, vmem_limit_bytes=VMEM_LIMIT
         ),
-    )(part.reshape(4, 4, 168, RANK))
+    )(bt, bt_sib, ortho, back, standard, gain, inv_std)
 
 
 def final_kernel(o_ref, inv_ref, c_ref, buf_ref, scale_ref, mom_ref, upd_ref, lhs):
@@ -626,19 +747,19 @@
     def _():
         o = o_ref[...]
         oi = o * inv_ref[...]
-        for j, v in enumerate((o, oi)):
-            top = v.astype(BF16)
-            lhs[2 * j * rows:(2 * j + 1) * rows, :] = top
-            lhs[(2 * j + 1) * rows:(2 * j + 2) * rows, :] = (v - top.astype(F32)).astype(BF16)
+        lhs[0:rows, :] = o.astype(BF16)
+        top, low = split(oi)
+        lhs[rows:2 * rows, :] = top
+        lhs[2 * rows:3 * rows, :] = low
 
     out = lax.dot_general(lhs[...], c_ref[...], (((1,), (1,)), ((), ())), preferred_element_type=F32)
-    mom_ref[...] = buf_ref[...] - (1.0 - MOMENTUM) * (out[0:rows] + out[rows:2 * rows])
-    upd_ref[...] = (out[2 * rows:3 * rows] + out[3 * rows:4 * rows]) * scale_ref[...]
+    mom_ref[...] = buf_ref[...] - (1.0 - MOMENTUM) * out[0:rows]
+    upd_ref[...] = (out[rows:2 * rows] + out[2 * rows:3 * rows]) * scale_ref[...]
 
 
 def final_products(o, inv, coeffs, buffer, scale):
     rows, cols = buffer.shape
-    tile = 384
+    tile = 896
     return pl.pallas_call(
         final_kernel,
         grid=(cols // tile,),
@@ -651,7 +772,7 @@
             pl.BlockSpec((1, tile), lambda i: (0, i)),
         ],
         out_specs=(pl.BlockSpec((rows, tile), lambda i: (0, i)), pl.BlockSpec((rows, tile), lambda i: (0, i))),
-        scratch_shapes=[pltpu.VMEM((4 * rows, RANK), BF16)],
+        scratch_shapes=[pltpu.VMEM((3 * rows, RANK), BF16)],
         compiler_params=pltpu.CompilerParams(vmem_limit_bytes=VMEM_LIMIT),
     )(o, inv, coeffs, buffer, scale)
 
@@ -668,17 +789,31 @@
     inv_std = lax.rsqrt(row_var + NORM_EPSILON)
     standard = centered * inv_std
     normed = (standard * norm_gain).astype(BF16)
-    feature_block = lax.all_to_all(normed, "dp", split_axis=1, concat_axis=0, tiled=True)
-    basis_all, shard_in = gather_both(right_basis, out_grad)
-    grad_acc = lax.dot_general(feature_block, shard_in, (((0,), (0,)), ((), ())), preferred_element_type=F32)
+    tokens, features = inputs.shape[0], weight.shape[0]
+    to_owners = normed.reshape(tokens, 4, 4, 2, features).transpose(1, 2, 3, 0, 4)
+    basis_all, shard_in, feature_block = gather_both(right_basis, out_grad, to_owners)
+    grad_acc = lax.dot_general(
+        feature_block.reshape(32 * tokens, features), shard_in, (((0,), (0,)), ((), ())), preferred_element_type=F32
+    )
     buffer = moment + grad_acc
-    part = jnp.dot(buffer, basis_all, precision=HI, preferred_element_type=F32)
-    projected, gram = projected_gram(part)
-    ortho_t = chol_solve(gram, projected.T)
-    coeff_part = lax.dot_general(
-        buffer, ortho_t, (((0,), (1,)), ((), ())), precision=lax.Precision.HIGH, preferred_element_type=F32
-    )
-    coeffs, coeff_own, squares = coeff_sum(coeff_part)
+    back_rows = lax.dot_general(shard_in, weight, (((1,), (1,)), ((), ())), preferred_element_type=F32)
+    projected, gram, bt, bt_sib, back_all = projected_gram(
+        buffer, basis_all, back_rows.reshape(4, 4, 2, tokens, features)
+    )
+    ortho = chol_solve(gram, projected)
+    share_cols = width // tensor_count
+    share_blocks = share_cols // features
+
+    def here(v):
+        own = lax.dynamic_slice_in_dim(v, tensor_index * share_cols, share_cols, 1)
+        return own.reshape(v.shape[0], share_blocks, features).transpose(1, 0, 2)
+
+    coeffs, coeff_own, squares, input_grad, gain_grad = coeff_sum(
+        bt, bt_sib, ortho, back_all.reshape(tensor_count, share_blocks, tokens, features),
+        here(standard), here(norm_gain[None, :]), jnp.broadcast_to(inv_std, (tokens, features)),
+    )
+    input_grad = input_grad.transpose(1, 0, 2).reshape(tokens, share_cols)
+    gain_grad = gain_grad[:, 0].reshape(share_cols)
     col_inverse = 1.0 / (jnp.sqrt(squares[0:1]) + 1e-08)
     basis_new = coeff_own * col_inverse
     qkv_group = 3 * HEADS * HEAD_DIM // tensor_count
@@ -686,21 +821,7 @@
     mlp_scale = 0.2 * math.sqrt(D * FF / RANK)
     position = jnp.arange(group_cols, dtype=jnp.int32)
     col_scale = jnp.where(position < qkv_group, qkv_scale, mlp_scale).astype(F32)
-    moment_new, update = final_products(ortho_t.T, col_inverse, coeffs, buffer, col_scale[None, :])
-
-    share_cols = width // tensor_count
-    offset = tensor_index * share_cols
-    back_rows = lax.dot_general(shard_in, weight, (((1,), (1,)), ((), ())), preferred_element_type=F32)
-    back_mine = lax.all_to_all(back_rows, "dp", split_axis=0, concat_axis=1, tiled=True)
-    normed_grad = lax.psum_scatter(back_mine, "tensor", scatter_dimension=1, tiled=True)
-    standard_here = lax.dynamic_slice_in_dim(standard, offset, share_cols, 1)
-    gain_here = lax.dynamic_slice_in_dim(norm_gain, offset, share_cols, 0)
-    scaled_grad = normed_grad * gain_here
-    sums = jnp.stack([jnp.sum(scaled_grad, axis=1), jnp.sum(scaled_grad * standard_here, axis=1)])
-    sums = lax.psum(sums, "tensor") * (1.0 / width)
-    full_grad = inv_std * (scaled_grad - sums[0][:, None] - standard_here * sums[1][:, None])
-    input_grad = full_grad.astype(BF16)
-    gain_grad = lax.psum(jnp.sum(normed_grad * standard_here, axis=0), "dp")
+    moment_new, update = final_products(ortho, col_inverse, coeffs, buffer, col_scale[None, :])
     return (input_grad, gain_grad, moment_new, basis_new, update)
 
 

time: 347 us -> 227 us (0.65)
  blocking collectives: 77.7 us -> 0 us
  waiting for transfers between devices: 22.4 us -> 0 us
  Pallas kernels: 182 us -> 203 us
  matrix products: 25.9 us -> 8.02 us
  between operations: 14.2 us -> 0.78 us
  starting transfers between devices: 8.47 us -> 0 us
    psum x2 -> x0, blocking collectives: 77.7 us -> none  [the longest x1 66.2 us: per_device(): gain_grad = lax.psum(jnp.sum(normed_grad * standard_here, axis=0), 'dp')]
    all_to_all x2 -> x0, waiting for transfers between devices: 22.4 us -> none  [the longest x1 13.5 us: per_device(): lax.all_to_all(back_rows, 'dp', split_axis=0, concat_axis=1, tiled=True)]
    dot_general x3 -> x1, matrix products: 20.6 us -> 2.67 us  [per_device(): lax.dot_general(feature_block.reshape(32 * tokens, features), shard_in, (...]
    pallas_call x1, Pallas kernels: 46.7 us -> 56.5 us  [gather_both(): pl.pallas_call(gather_kernel, out_shape=(jax.ShapeDtypeStruct((32 * right...]
    pallas_call x2, Pallas kernels: 77.7 us -> 86.5 us  [the longest x1 63.2 us: projected_gram(): pl.pallas_call(gram_kernel, out_shape=(jax.ShapeDtypeStruct((rows, RANK),...]
    all_to_all x2 -> x0, starting transfers between devices: 8.25 us -> none  [the longest x1 4.4 us: per_device(): lax.all_to_all(normed, 'dp', split_axis=1, concat_axis=0, tiled=True)]
    pallas_call x2 -> x0, local copies, waits for them, and re-layouts: 3.98 us -> none  [the longest x1 1.99 us: projected_gram(): pl.pallas_call(gram_kernel, out_shape=(jax.ShapeDtypeStruct(part.shape, F...]
    pallas_call x1, Pallas kernels: 49.7 us -> 53.7 us  [coeff_sum(): pl.pallas_call(coeff_kernel, out_shape=(jax.ShapeDtypeStruct((2688, RANK)...]
  transfers between devices with their start and end apart: 3 -> 0, of which waited for: 2 -> 0; matrix products, arithmetic and copies ran while one was open for 9% -> 0% of each run, Pallas kernels for 39% -> 0%
where the time goes in v2:
time: 227 us; the launch traced here: 226 us
  Pallas kernels  203 us (89%)
  matrix products  8.02 us (4%)
  local copies, waits for them, and re-layouts  7.88 us (3%)
  other arithmetic  6.31 us (3%)
    pallas_call x1, Pallas kernels, projected_gram(): pl.pallas_call(gram_kernel, out_shape=(jax.ShapeDtypeStruct((rows, RANK),...  63.2 us
    pallas_call x1, Pallas kernels, gather_both(): pl.pallas_call(gather_kernel, out_shape=(jax.ShapeDtypeStruct((32 * right...  56.5 us
    pallas_call x1, Pallas kernels, coeff_sum(): pl.pallas_call(coeff_kernel, out_shape=(jax.ShapeDtypeStruct((2688, RANK)...  53.7 us
    pallas_call x1, Pallas kernels, chol_solve(): pl.pallas_call(chol_kernel, out_shape=jax.ShapeDtypeStruct(projected.shap...  23.2 us
    pallas_call x1, Pallas kernels, final_products(): pl.pallas_call(final_kernel, grid=(cols // tile,), out_shape=(jax.ShapeDt...  6.54 us
    dot_general x1, matrix products, per_device(): lax.dot_general(shard_in, weight, (((1,), (1,)), ((), ())), preferred_ele...  5.34 us

profile of v2, /device:TPU:1, one launch (start us, length us, event | category | flops | bytes accessed | tf_op | source)
XLA Modules:
  0.0 226.2 jit_solution(18034149982565035213)
XLA Ops:
  0.6 0.0 copy-start
  0.7 1.2 convert_reduce_fusion
  1.9 1.3 fusion.2
  3.2 0.8 dynamic-slice.3
  4.0 0.7 transpose_reshape.3.gain_ref
  4.6 0.6 compare_select_fusion.scale_ref
  5.2 0.7 broadcast_in_dim.8.inv_ref
  5.9 1.2 fusion
  7.1 0.1 reshape.61
  7.3 0.7 copy.20
  8.0 0.7 reshape.56
  8.6 1.1 copy.19
  9.7 56.5 %shard_map.101 = (f32[2688,512]{1,0:T(8,128)}, bf16[1024,2688]{1,0:T(8,128)(2,1)}, bf16[4,4,2,32,192]{4,3,2,1,0:T(8,128)(2,1)}) custom-call(f32[84,512]{1,0:T(8,128)} %r_ref.1, bf16[32,2688]{1,0:T(8,128)(2,1)} %g_ref.1, bf16[4,4,2,32,192]{4,3,2,1,0:T(8,128)(2,1)} %bitcast.18), custom_call_target="tpu_custom_call" | custom-call | tf_op jit(solution)/shard_map/pallas_call | solution.py:236
  66.3 0.0 slice-start
  66.3 0.0 copy-done
  66.3 0.0 slice-start.1
  66.3 0.0 copy-start.1
  66.3 0.0 copy-start.2
  66.3 5.3 %fusion.3 = f32[1024,192]{1,0:T(8,128)} fusion(bf16[1024,2688]{1,0:T(8,128)(2,1)} %get-tuple-element.21, bf16[192,2688]{1,0:T(8,128)(2,1)S(1)} %copy-done), kind=kOutput, calls=%fused_computation.16 | convolution fusion | flops 1056964608 | bytes 7323648 | tf_op jit(solution)/shard_map/dot_general | solution.py:799
  71.7 0.0 slice-done
  71.7 0.0 slice-done.1
  71.7 0.0 copy-done.1
  71.7 0.0 copy-done.2
  71.7 2.7 %convolution_add_fusion.b_ref.buf_ref = f32[192,2688]{1,0:T(8,128)} fusion(f32[192,2688]{1,0:T(8,128)S(1)} %copy-done.1, bf16[1024,192]{1,0:T(8,128)(2,1)S(1)} %bitcast.19, bf16[1024,2688]{1,0:T(8,128)(2,1)S(1)} %bitcast.17), kind=kOutput, calls=%fused_computation | convolution fusion | flops 1057480704 | bytes 10027008 | tf_op jit(solution)/shard_map/dot_general | solution.py:795
  74.4 63.2 %shard_map.102 = (f32[192,512]{1,0:T(8,128)}, f32[8,2,4,8,512]{4,3,2,1,0:T(8,128)}, bf16[2688,384]{1,0:T(8,128)(2,1)}, bf16[2688,384]{1,0:T(8,128)(2,1)}, f32[4,4,2,32,192]{4,3,2,1,0:T(8,128)}) custom-call(f32[192,2688]{1,0:T(8,128)} %convolution_add_fusion.b_ref.buf_ref, f32[2688,512]{1,0:T(8,128)} %get-tuple-element.22.r_ref, f32[4,4,2,32,192]{4,3,2,1,0:T(8,128)} %bitcast.21), custom_call_target="tpu_custom_call" | custom-call | tf_op jit(solution)/shard_map/pallas_call | solution.py:364
  137.6 23.2 %shard_map.103.o_ref = f32[192,512]{1,0:T(8,128)} custom-call(f32[512,512]{1,0:T(8,128)} %bitcast.22, f32[192,512]{1,0:T(8,128)} %get-tuple-element.26.p_ref), custom_call_target="tpu_custom_call" | custom-call | tf_op jit(solution)/shard_map/pallas_call | solution.py:462
  160.9 53.7 %shard_map.104 = (bf16[2688,512]{1,0:T(8,128)(2,1)}, f32[84,512]{1,0:T(8,128)}, f32[8,512]{1,0:T(8,128)}, bf16[4,32,192]{2,1,0:T(8,128)(2,1)}, f32[4,8,192]{2,1,0:T(8,128)}) custom-call(bf16[2688,384]{1,0:T(8,128)(2,1)} %get-tuple-element.23.bt_ref, bf16[2688,384]{1,0:T(8,128)(2,1)} %get-tuple-element.24.btsib_ref, f32[192,512]{1,0:T(8,128)} %shard_map.103.o_ref, ...), custom_call_target="tpu_custom_call" | custom-call | tf_op jit(solution)/shard_map/pallas_call | solution.py:698
  214.5 0.0 copy-start.3
  214.5 0.9 copy.15
  215.5 0.7 reshape.62
  216.2 1.3 add_divide_fusion.inv_ref
  217.5 0.0 copy-start.4
  217.5 6.5 %shard_map.105 = (f32[192,2688]{1,0:T(8,128)}, f32[192,2688]{1,0:T(8,128)}) custom-call(f32[192,512]{1,0:T(8,128)} %shard_map.103.o_ref, f32[1,512]{1,0:T(1,128)} %add_divide_fusion.inv_ref, bf16[2688,512]{1,0:T(8,128)(2,1)} %get-tuple-element.31.c_ref, f32[192,2688]{1,0:T(8,128)} %convolution_add_fusion.b_ref.buf_ref, f32[1,2688]{1,0:T(1,128)} %compare_select_fusion.scale_ref), custom_call_target="tpu_custom_call" | custom-call | tf_op jit(solution)/shard_map/pallas_call | solution.py:763
  224.1 0.0 copy-done.3
  224.1 0.0 copy-done.4
  224.1 0.7 broadcast_multiply_fusion
  224.8 0.8 slice_reduce_fusion
  225.5 0.7 reshape_squeeze.3
  (4 shorter events, 0.0 us)
Async XLA Ops:
  0.6 65.7 %copy-start = (bf16[192,2688]{1,0:T(8,128)(2,1)S(1)}, bf16[192,2688]{1,0:T(8,128)(2,1)}, u32[]{:S(2)}) copy-start(bf16[192,2688]{1,0:T(8,128)(2,1)} %param.9) | copy-start | bytes 3096580
  66.3 5.4 %slice-start = ((s8[5505024]{0:T(1024)(128)(4,1)}), s8[4194304]{0:T(1024)(128)(4,1)S(1)}, s32[]{:S(2)}) async-start(s8[5505024]{0:T(1024)(128)(4,1)} %bitcast.16), calls=%async_computation | async-start | bytes 8388608
  66.3 5.4 %slice-start.1 = ((s8[5505024]{0:T(1024)(128)(4,1)}), s8[1310720]{0:T(1024)(128)(4,1)S(1)}, s32[]{:S(2)}) async-start(s8[5505024]{0:T(1024)(128)(4,1)} %bitcast.16), calls=%async_computation.1 | async-start | bytes 2621440
  66.3 5.4 %copy-start.1 = (f32[192,2688]{1,0:T(8,128)S(1)}, f32[192,2688]{1,0:T(8,128)}, u32[]{:S(2)}) copy-start(f32[192,2688]{1,0:T(8,128)} %param.10) | copy-start | bytes 6193156
  66.3 5.4 %copy-start.2 = (bf16[4,4,2,32,192]{4,3,2,1,0:T(8,128)(2,1)S(1)}, bf16[4,4,2,32,192]{4,3,2,1,0:T(8,128)(2,1)}, u32[]{:S(2)}) copy-start(bf16[4,4,2,32,192]{4,3,2,1,0:T(8,128)(2,1)} %get-tuple-element.20) | copy-start | bytes 1179652
  214.5 9.5 %copy-start.3 = (f32[84,512]{1,0:T(8,128)S(1)}, f32[84,512]{1,0:T(8,128)}, u32[]{:S(2)}) copy-start(f32[84,512]{1,0:T(8,128)} %get-tuple-element.33) | copy-start | bytes 516100
  217.5 6.6 %copy-start.4 = (f32[1,512]{1,0:T(1,128)S(1)}, f32[1,512]{1,0:T(1,128)}, u32[]{:S(2)}) copy-start(f32[1,512]{1,0:T(1,128)} %add_divide_fusion.inv_ref) | copy-start | bytes 6148

commit v3 on v2

--- a/solution.py
+++ b/solution.py
@@ -110,10 +110,9 @@
     yield
     got((a0 - 1, b0), 2, 0)
     to(a0 + 1, b0, (a0 - 1, b0), 0, 2)
-    spread(1, (a0 - 1, b0))
-    yield
     got((a0 + 1, b0), 2, 1)
     to(a0 - 1, b0, (a0 + 1, b0), 1, 3)
+    spread(1, (a0 - 1, b0))
     spread(2, (a0 + 1, b0))
     yield
     share((a0 - 1, b0), 21)
@@ -143,253 +142,323 @@
         wait_recv(at(a, b0, 2, 1 - core), rsem.at[base + 20 + k], dp=sib)
         for j, b in enumerate((b0 - 1, b0 + 1, b0 + 2)):
             wait_recv(at(a, b, 2, 1 - core), rsem.at[base + 24 + 3 * k + j], dp=sib)
-        yield
+    yield
 
 
 GATHER_SLOTS = 36
-EXCHANGE_SLOTS = 7
-
-
-def exchange_stream(src, xbuf, ybuf, out, ssem, rsem, base, sent):
+EXCHANGE_SLOTS = 6
+
+
+def exchange_stream(src, mid, out, s, ssem, rsem, base, sent):
     x, y, core, _ = place()
     sib = dp_of(x, y, 1 - core)
-    for i in range(3):
-        to = (x + 1 + i) % 4
-        sent.append(send(src.at[to], xbuf.at[x], ssem.at[base + i], rsem.at[base + i], dp=dp_of(to, y, core)))
-    xbuf[x] = src[x]
+    half = slice(16 * s, 16 * s + 16)
+
+    def part(ref, a):
+        return ref.at[a, :, half] if s == 0 else ref.at[:, a, half]
+
+    def swapped(ref, b):
+        return ref.at[:, b, half] if s == 0 else ref.at[b, :, half]
+
+    a0, b0 = (x, y) if s == 0 else (y, x)
+
+    def dev(a, b):
+        return dp_of(a, b, core) if s == 0 else dp_of(b, a, core)
+
+    mine = pltpu.make_async_copy(part(src, a0), mid.at[s, a0], ssem.at[base + 6])
+    mine.start()
+    for i in range(3):
+        to = (a0 + 1 + i) % 4
+        sent.append(send(part(src, to), mid.at[s, a0], ssem.at[base + i], rsem.at[base + i], dp=dev(to, b0)))
     yield
     for i in range(3):
-        wait_recv(xbuf.at[(x + 3 - i) % 4], rsem.at[base + i], dp=sib)
-    for i in range(3):
-        to = (y + 1 + i) % 4
+        wait_recv(mid.at[s, (a0 + 3 - i) % 4], rsem.at[base + i], dp=sib)
+    mine.wait()
+    own = pltpu.make_async_copy(mid.at[s, :, b0], swapped(out, b0), ssem.at[base + 6])
+    own.start()
+    for i in range(3):
+        to = (b0 + 1 + i) % 4
         sent.append(send(
-            xbuf.at[:, to], ybuf.at[:, y], ssem.at[base + 3 + i], rsem.at[base + 3 + i], dp=dp_of(x, to, core)
+            mid.at[s, :, to], swapped(out, b0), ssem.at[base + 3 + i], rsem.at[base + 3 + i], dp=dev(a0, to)
         ))
-    ybuf[:, y] = xbuf[:, y]
     yield
-    for i in range(3):
-        wait_recv(ybuf.at[:, (y + 3 - i) % 4], rsem.at[base + 3 + i], dp=sib)
-    sent.append(send(ybuf.at[:, :, 1 - core], out.at[:, :, core], ssem.at[base + 6], rsem.at[base + 6], dp=sib))
-    out[:, :, core] = ybuf[:, :, core]
+    own.wait()
+    for i in range(3):
+        wait_recv(swapped(out, (b0 + 3 - i) % 4), rsem.at[base + 3 + i], dp=sib)
     yield
-    wait_recv(out.at[:, :, 1 - core], rsem.at[base + 6], dp=sib)
-    yield
-
-
-def gather_kernel(r_ref, g_ref, n_ref, rall_ref, gall_ref, nall_ref, got_ref, xbuf, ybuf, ssem, rsem, hsem):
-    x, y, core, _ = place()
+
+
+def split(v):
+    top = v.astype(BF16)
+    return top, (v - top.astype(F32)).astype(BF16)
+
+
+EX = 4 * GATHER_SLOTS
+ZP = EX + 28
+OTHER = ZP + 35
+
+
+def front_kernel(in_ref, gain_ref, g_ref, w_ref, m_ref, r_ref,
+                 p_ref, gram_ref, bt_ref, btsib_ref, buf_ref, backall_ref, std_ref, inv_ref,
+                 rall, gall, got, std, nrm, exmid, exout, exsib, xt, both, bk, bksib, bsrc, bmid,
+                 part, zbuf, gbuf, cbuf, xbuf, ybuf, ssem, rsem):
+    x, y, core, z = place()
     chip = x * 4 + y
-    greet(plane_peers(x, y, core))
-    rows = r_ref.shape[0]
-    tokens = g_ref.shape[0]
-    cols = g_ref.shape[1]
+    sib = dp_of(x, y, 1 - core)
+    xs = [(x + d) % 4 for d in (1, 2, 3)]
+    ys = [(y + d) % 4 for d in (1, 2, 3)]
+    zs = [(z + d) % 8 for d in range(1, 8)]
+    greet([{"tensor": q} for q in zs] + plane_peers(x, y, core))
+    sent = []
+    rows, cols = m_ref.shape
+    tokens, width = in_ref.shape
     cut = 1408
+
     other = pl.multiple_of(256 * (1 - core), 128)
-    swap = send(r_ref.at[:, pl.ds(other, 256)], got_ref, hsem.at[0], hsem.at[1], dp=dp_of(x, y, 1 - core))
-    own_g = pltpu.make_async_copy(
-        g_ref, gall_ref.at[pl.ds(pl.multiple_of(tokens * (2 * chip + core), 32), tokens)], hsem.at[2]
-    )
-    own_g.start()
+    sent.append(send(r_ref.at[:, pl.ds(other, 256)], got, ssem.at[OTHER], rsem.at[OTHER], dp=sib))
+    gall[core, pl.ds(pl.multiple_of(32 * chip, 32), 32)] = g_ref[...]
+
+    def loc_g(s):
+        def loc(who, bx, by, part):
+            lo, n = ((0, cut), (cut, cols - cut), (0, cols))[part]
+            return gall.at[who, pl.ds(pl.multiple_of(32 * (bx * 4 + by) + 16 * s, 16), 16), pl.ds(lo, n)]
+        return loc
 
     def loc_r(s):
         def loc(who, bx, by, part):
             lo, n = ((0, 88), (88, 80), (0, 168))[part]
             row = pl.multiple_of((bx * 4 + by) * 168 + lo, 8)
-            col = pl.multiple_of(256 * who + 128 * s, 128)
-            return rall_ref.at[pl.ds(row, n), pl.ds(col, 128)]
+            return rall.at[pl.ds(row, n), pl.ds(pl.multiple_of(256 * who + 128 * s, 128), 128)]
         return loc
 
-    def loc_g(s):
-        def loc(who, bx, by, part):
-            lo, n = ((0, cut), (cut, cols - cut), (0, cols))[part]
-            row = pl.multiple_of(tokens * (2 * (bx * 4 + by) + who) + 16 * s, 16)
-            return gall_ref.at[pl.ds(row, 16), pl.ds(lo, n)]
-        return loc
-
-    sent = []
-    own_g.wait()
-    g_streams = [
-        gather_stream(loc_g(0), "x", ssem, rsem, 2 * GATHER_SLOTS, sent),
-        gather_stream(loc_g(1), "y", ssem, rsem, 3 * GATHER_SLOTS, sent),
-    ]
-    swap.wait()
+    g_streams = [gather_stream(loc_g(s), "xy"[s], ssem, rsem, (2 + s) * GATHER_SLOTS, sent) for s in (0, 1)]
+    for g in g_streams:
+        next(g)
+    for g in g_streams:
+        next(g)
+
+    wide = [in_ref[:, 384 * b:384 * b + 384].astype(F32) for b in range(16)]
+    mean = sum(jnp.sum(v, axis=1, keepdims=True) for v in wide) * (1.0 / width)
+    centered = [in_ref[:, 384 * b:384 * b + 384].astype(F32) - mean for b in range(16)]
+    var = sum(jnp.sum(v * v, axis=1, keepdims=True) for v in centered) * (1.0 / width)
+    inv = lax.rsqrt(var + NORM_EPSILON)
+    inv_ref[...] = jnp.broadcast_to(inv, inv_ref.shape)
+    for b in range(16):
+        v = (in_ref[:, 384 * b:384 * b + 384].astype(F32) - mean) * inv
+        std[b // 2, b % 2] = v
+        nrm[b // 4, b % 4] = (v * gain_ref[:, 384 * b:384 * b + 384]).astype(BF16)
+    std_ref[...] = std[z]
+    ex = [exchange_stream(nrm, exmid, exout, s, ssem, rsem, EX + 7 * s, sent) for s in (0, 1)]
+    for g in ex:
+        next(g)
+
+    wait_recv(got, rsem.at[OTHER], dp=sib)
     mine = r_ref[:, pl.ds(pl.multiple_of(256 * core, 128), 256)]
-    theirs = got_ref[...]
-    first = jnp.where(core == 0, mine, theirs)
-    second = jnp.where(core == 0, theirs, mine)
-    row = pl.multiple_of(chip * 168, 8)
-    col = pl.multiple_of(256 * core, 128)
-    rall_ref[pl.ds(row, 168), pl.ds(col, 256)] = jnp.concatenate([first, second], axis=0)
-    r_streams = [
-        gather_stream(loc_r(0), "x", ssem, rsem, 0, sent),
-        gather_stream(loc_r(1), "y", ssem, rsem, GATHER_SLOTS, sent),
-    ]
-    round_robin(
-        r_streams + g_streams + [exchange_stream(n_ref, xbuf, ybuf, nall_ref, ssem, rsem, 4 * GATHER_SLOTS, sent)]
-    )
-    for copy in sent:
-        copy.wait_send()
-
-
-def gather_both(right_basis, out_grad, normed):
-    vm = pl.BlockSpec(memory_space=pltpu.VMEM)
-    return pl.pallas_call(
-        gather_kernel,
-        out_shape=(
-            jax.ShapeDtypeStruct((32 * right_basis.shape[0], RANK), F32),
-            jax.ShapeDtypeStruct((32 * out_grad.shape[0], out_grad.shape[1]), BF16),
-            jax.ShapeDtypeStruct(normed.shape, BF16),
-        ),
-        in_specs=[vm, vm, vm],
-        out_specs=(vm, vm, vm),
-        scratch_shapes=[
-            pltpu.VMEM((right_basis.shape[0], 256), F32),
-            pltpu.VMEM(normed.shape, BF16),
-            pltpu.VMEM(normed.shape, BF16),
-            pltpu.SemaphoreType.DMA((4 * GATHER_SLOTS + EXCHANGE_SLOTS,)),
-            pltpu.SemaphoreType.DMA((4 * GATHER_SLOTS + EXCHANGE_SLOTS,)),
-            pltpu.SemaphoreType.DMA((3,)),
-        ],
-        compiler_params=pltpu.CompilerParams(
-            collective_id=1, has_side_effects=True, vmem_limit_bytes=VMEM_LIMIT
-        ),
-    )(right_basis, out_grad, normed)
-
-
-def split(v):
-    top = v.astype(BF16)
-    return top, (v - top.astype(F32)).astype(BF16)
-
-
-def gram_kernel(b_ref, r_ref, back_ref, p_ref, g_ref, bt_ref, btsib_ref, backall_ref,
-                both, part_ref, zbuf, gbuf, cbuf, xbuf, ybuf, ex, ey, ssem, rsem):
-    x, y, core, z = place()
-    xs = [(x + d) % 4 for d in (1, 2, 3)]
-    ys = [(y + d) % 4 for d in (1, 2, 3)]
-    zs = [(z + d) % 8 for d in range(1, 8)]
-    dp = lax.axis_index("dp")
-    sib = dp_of(x, y, 1 - core)
-    greet(
-        [{"tensor": q} for q in zs]
-        + [{"dp": dp_of(q, y, core)} for q in xs]
-        + [{"dp": dp_of(x, q, core)} for q in ys]
-        + [{"dp": sib}]
-    )
-    sent = []
-    order = (3, 4, 2, 5, 1, 6, 0)
-    back = exchange_stream(back_ref, ex, ey, backall_ref, ssem, rsem, 36, sent)
-    next(back)
-    rows, cols = b_ref.shape
-    top, low = split(b_ref[...])
-    both[0:rows, :] = top
-    both[rows:2 * rows, :] = low
-    part_ref[...] = jnp.zeros_like(part_ref)
+    theirs = got[...]
+    rall[pl.ds(pl.multiple_of(chip * 168, 8), 168), pl.ds(pl.multiple_of(256 * core, 128), 256)] = jnp.concatenate(
+        [jnp.where(core == 0, mine, theirs), jnp.where(core == 0, theirs, mine)], axis=0
+    )
+    r_streams = [gather_stream(loc_r(s), "xy"[s], ssem, rsem, s * GATHER_SLOTS, sent) for s in (0, 1)]
+
+    def run(gens):
+        live = []
+        for g in gens:
+            try:
+                next(g)
+                live.append(g)
+            except StopIteration:
+                pass
+        return live
+
+    def mine192(v):
+        return jnp.where(core == 0, v[:, 0:192].astype(F32), v[:, 192:384].astype(F32))
+
+    def after_exchange():
+        sent.append(send(exout, exsib, ssem.at[OTHER + 1], rsem.at[OTHER + 1], dp=sib))
+        for q in range(4):
+            v = exout[q].reshape(4 * tokens, 384)
+            xt[core, :, 128 * q:128 * q + 128] = mine192(v).T.astype(BF16)
+        yield
+        wait_recv(exsib, rsem.at[OTHER + 1], dp=sib)
+        for q in range(4):
+            v = exsib[q].reshape(4 * tokens, 384)
+            xt[1 - core, :, 128 * q:128 * q + 128] = mine192(v).T.astype(BF16)
+        yield
+
+    def compute():
+        for t in range(0, cols, 384):
+            acc = m_ref[:, t:t + 384]
+            for c in (0, 1):
+                acc = acc + jnp.dot(xt[c], gall[c, :, t:t + 384], preferred_element_type=F32)
+            buf_ref[:, t:t + 384] = acc
+            top, low = split(acc)
+            both[0:rows, t:t + 384] = top
+            both[rows:2 * rows, t:t + 384] = low
+            bt_ref[t:t + 384, :] = jnp.concatenate([top, low], axis=0).astype(F32).T.astype(BF16)
+            yield
+        sent.append(send(bt_ref, btsib_ref, ssem.at[OTHER + 2], rsem.at[OTHER + 2], dp=sib))
+        for c in (0, 1):
+            for q in (0, 256):
+                bk[c, q:q + 256, 0:192] = lax.dot_general(
+                    gall[c, q:q + 256, :], w_ref[...], (((1,), (1,)), ((), ())), preferred_element_type=F32
+                )
+                yield
+        sent.append(send(bk.at[1 - core], bksib, ssem.at[OTHER + 3], rsem.at[OTHER + 3], dp=sib))
+        yield
+
+    bk[:, :, 128:256] = jnp.zeros((2, 512, 128), F32)
+    tail = after_exchange()
+    work = compute()
+    r_live, g_live, x_live = r_streams, g_streams, ex
+    r_live = run(r_live)
+    turn = 0
+    tail_live = [tail]
+    while g_live or x_live or tail_live:
+        g_live = run(g_live)
+        if x_live:
+            x_live = run(x_live)
+        elif tail_live:
+            tail_live = run(tail_live)
+        turn += 1
+        if turn % 2:
+            r_live = run(r_live)
+    work_live = [work]
+    while r_live or work_live:
+        r_live = run(r_live)
+        work_live = run(work_live)
+
+    part[...] = jnp.zeros_like(part)
     for t in range(0, cols, 384):
-        r_top, r_low = split(r_ref[t:t + 384, :])
+        r_top, r_low = split(rall[t:t + 384, :])
         one = jnp.dot(both[:, t:t + 384], r_top, preferred_element_type=F32)
         two = jnp.dot(both[0:rows, t:t + 384], r_low, preferred_element_type=F32)
-        part_ref[...] += one[0:rows] + (one[rows:] + two)
+        part[...] += one[0:rows] + (one[rows:] + two)
+
+    order = (3, 4, 2, 5, 1, 6, 0)
 
     def rows24(q):
         return pl.ds(pl.multiple_of(24 * q, 8), 24)
 
     for i in order:
-        sent.append(send(part_ref.at[rows24(zs[i])], zbuf.at[i], ssem.at[i], rsem.at[i], tensor=zs[i]))
-    for t in range(0, cols, 384):
-        bt_ref[t:t + 384, :] = both[:, t:t + 384].astype(F32).T.astype(BF16)
-    sent.append(send(bt_ref, btsib_ref, ssem.at[35], rsem.at[35], dp=sib))
-    next(back)
-    total = part_ref[rows24(z), :]
+        sent.append(send(part.at[rows24(zs[i])], zbuf.at[i], ssem.at[ZP + i], rsem.at[ZP + i], tensor=zs[i]))
+
+    wait_recv(bksib, rsem.at[OTHER + 3], dp=sib)
+    for q in range(4):
+        ours = bk[core, 128 * q:128 * q + 128, 0:192]
+        their = bksib[128 * q:128 * q + 128, 0:192]
+        bsrc[q] = jnp.concatenate(
+            [jnp.where(core == 0, ours, their), jnp.where(core == 0, their, ours)], axis=1
+        ).reshape(4, tokens, 384)
+    back = [exchange_stream(bsrc, bmid, backall_ref, s, ssem, rsem, EX + 14 + 7 * s, sent) for s in (0, 1)]
+    back = run(back)
+
+    total = part[rows24(z), :]
     for i in reversed(order):
-        wait_recv(zbuf.at[i], rsem.at[i], tensor=zs[i])
+        wait_recv(zbuf.at[i], rsem.at[ZP + i], tensor=zs[i])
         total = total + zbuf[i]
     p_ref[rows24(z), :] = total
     mine = p_ref.at[rows24(z)]
     for i in order:
-        sent.append(send(mine, mine, ssem.at[7 + i], rsem.at[7 + i], tensor=zs[i]))
+        sent.append(send(mine, mine, ssem.at[ZP + 7 + i], rsem.at[ZP + 7 + i], tensor=zs[i]))
+    back = run(back)
     for i in reversed(order):
         src = (z + 7 - i) % 8
-        wait_recv(p_ref.at[rows24(src)], rsem.at[7 + i], tensor=zs[i])
-    next(back)
-
+        wait_recv(p_ref.at[rows24(src)], rsem.at[ZP + 7 + i], tensor=zs[i])
     gbuf[...] = lax.dot_general(
         p_ref[:, pl.ds(pl.multiple_of(128 * (z // 2), 128), 128)], p_ref[...],
         (((0,), (0,)), ((), ())), precision=HI, preferred_element_type=F32,
     )
     half = 64 * (z % 2)
-    sent.append(send(gbuf.at[pl.ds(pl.multiple_of(half + 32 * (1 - core), 32), 32)], cbuf, ssem.at[14], rsem.at[14], dp=sib))
-    wait_recv(cbuf, rsem.at[14], dp=sib)
+    away = gbuf.at[pl.ds(pl.multiple_of(half + 32 * (1 - core), 32), 32)]
+    sent.append(send(away, cbuf, ssem.at[ZP + 14], rsem.at[ZP + 14], dp=sib))
+    wait_recv(cbuf, rsem.at[ZP + 14], dp=sib)
     cbuf[...] += gbuf[pl.ds(pl.multiple_of(half + 32 * core, 32), 32), :]
     for i in range(3):
         sent.append(send(
-            cbuf.at[pl.ds(pl.multiple_of(8 * xs[i], 8), 8)], xbuf.at[i], ssem.at[15 + i], rsem.at[15 + i],
+            cbuf.at[pl.ds(pl.multiple_of(8 * xs[i], 8), 8)], xbuf.at[i], ssem.at[ZP + 15 + i], rsem.at[ZP + 15 + i],
             dp=dp_of(xs[i], y, core),
         ))
     total = cbuf[pl.ds(pl.multiple_of(8 * x, 8), 8), :]
     for i in range(3):
-        wait_recv(xbuf.at[i], rsem.at[15 + i], dp=sib)
+        wait_recv(xbuf.at[i], rsem.at[ZP + 15 + i], dp=sib)
         total = total + xbuf[i]
     ybuf[y] = total
     for i in range(3):
-        sent.append(send(ybuf.at[y], ybuf.at[y], ssem.at[18 + i], rsem.at[18 + i], dp=dp_of(x, ys[i], core)))
-    for i in range(3):
-        wait_recv(ybuf.at[(y + 3 - i) % 4], rsem.at[18 + i], dp=sib)
-    g_ref[z, core, x] = (ybuf[0] + ybuf[1]) + (ybuf[2] + ybuf[3])
-    mine = g_ref.at[z, core, x]
+        sent.append(send(
+            ybuf.at[y], ybuf.at[y], ssem.at[ZP + 18 + i], rsem.at[ZP + 18 + i], dp=dp_of(x, ys[i], core)
+        ))
+    for i in range(3):
+        wait_recv(ybuf.at[(y + 3 - i) % 4], rsem.at[ZP + 18 + i], dp=sib)
+    gram_ref[z, core, x] = (ybuf[0] + ybuf[1]) + (ybuf[2] + ybuf[3])
+    mine = gram_ref.at[z, core, x]
     for i in order:
-        sent.append(send(mine, mine, ssem.at[21 + i], rsem.at[21 + i], tensor=zs[i]))
+        sent.append(send(mine, mine, ssem.at[ZP + 21 + i], rsem.at[ZP + 21 + i], tensor=zs[i]))
     for i in reversed(order):
-        wait_recv(g_ref.at[(z + 7 - i) % 8, core, x], rsem.at[21 + i], tensor=zs[i])
-    mine = g_ref.at[:, core, x]
-    for i in range(3):
-        sent.append(send(mine, mine, ssem.at[28 + i], rsem.at[28 + i], dp=dp_of(xs[i], y, core)))
-    sent.append(send(mine, mine, ssem.at[31], rsem.at[31], dp=sib))
+        wait_recv(gram_ref.at[(z + 7 - i) % 8, core, x], rsem.at[ZP + 21 + i], tensor=zs[i])
+    mine = gram_ref.at[:, core, x]
+    for i in range(3):
+        sent.append(send(mine, mine, ssem.at[ZP + 28 + i], rsem.at[ZP + 28 + i], dp=dp_of(xs[i], y, core)))
+    sent.append(send(mine, mine, ssem.at[ZP + 31], rsem.at[ZP + 31], dp=sib))
     for i in range(3):
         src = (x + 3 - i) % 4
-        wait_recv(g_ref.at[:, core, src], rsem.at[28 + i], dp=sib)
-        got = g_ref.at[:, core, src]
-        sent.append(send(got, got, ssem.at[32 + i], rsem.at[32 + i], dp=sib))
-    wait_recv(g_ref.at[:, 1 - core, x], rsem.at[31], dp=sib)
-    for i in range(3):
-        wait_recv(g_ref.at[:, 1 - core, (x + 3 - i) % 4], rsem.at[32 + i], dp=sib)
-    next(back)
-    wait_recv(btsib_ref, rsem.at[35], dp=sib)
+        wait_recv(gram_ref.at[:, core, src], rsem.at[ZP + 28 + i], dp=sib)
+        there = gram_ref.at[:, core, src]
+        sent.append(send(there, there, ssem.at[ZP + 32 + i], rsem.at[ZP + 32 + i], dp=sib))
+    back = run(back)
+    wait_recv(gram_ref.at[:, 1 - core, x], rsem.at[ZP + 31], dp=sib)
+    for i in range(3):
+        wait_recv(gram_ref.at[:, 1 - core, (x + 3 - i) % 4], rsem.at[ZP + 32 + i], dp=sib)
+    wait_recv(btsib_ref, rsem.at[OTHER + 2], dp=sib)
     for copy in sent:
         copy.wait_send()
 
 
-def projected_gram(buffer, basis, back):
+def front(inputs, gain, out_grad, weight, moment, right_basis):
     vm = pl.BlockSpec(memory_space=pltpu.VMEM)
-    rows, cols = buffer.shape
-    p, g, bt, bt_sib, back_all = pl.pallas_call(
-        gram_kernel,
+    rows, cols = moment.shape
+    tokens = inputs.shape[0]
+    return pl.pallas_call(
+        front_kernel,
         out_shape=(
             jax.ShapeDtypeStruct((rows, RANK), F32),
             jax.ShapeDtypeStruct((8, 2, 4, 8, RANK), F32),
             jax.ShapeDtypeStruct((cols, 2 * rows), BF16),
             jax.ShapeDtypeStruct((cols, 2 * rows), BF16),
-            jax.ShapeDtypeStruct(back.shape, F32),
+            jax.ShapeDtypeStruct((rows, cols), F32),
+            jax.ShapeDtypeStruct((4, 4, tokens, 384), F32),
+            jax.ShapeDtypeStruct((2, tokens, 384), F32),
+            jax.ShapeDtypeStruct((tokens, 384), F32),
         ),
-        in_specs=[vm, vm, vm],
-        out_specs=(vm, vm, vm, vm, vm),
+        in_specs=[vm] * 6,
+        out_specs=(vm,) * 8,
         scratch_shapes=[
+            pltpu.VMEM((cols, RANK), F32),
+            pltpu.VMEM((2, 16 * tokens, cols), BF16),
+            pltpu.VMEM((right_basis.shape[0], 256), F32),
+            pltpu.VMEM((8, 2, tokens, 384), F32),
+            pltpu.VMEM((4, 4, tokens, 384), BF16),
+            pltpu.VMEM((2, 4, 4, 16, 384), BF16),
+            pltpu.VMEM((4, 4, tokens, 384), BF16),
+            pltpu.VMEM((4, 4, tokens, 384), BF16),
+            pltpu.VMEM((2, rows, 16 * tokens), BF16),
             pltpu.VMEM((2 * rows, cols), BF16),
+            pltpu.VMEM((2, 16 * tokens, 256), F32),
+            pltpu.VMEM((16 * tokens, 256), F32),
+            pltpu.VMEM((4, 4, tokens, 384), F32),
+            pltpu.VMEM((2, 4, 4, 16, 384), F32),
             pltpu.VMEM((rows, RANK), F32),
             pltpu.VMEM((7, 24, RANK), F32),
             pltpu.VMEM((128, RANK), F32),
             pltpu.VMEM((32, RANK), F32),
             pltpu.VMEM((3, 8, RANK), F32),
             pltpu.VMEM((4, 8, RANK), F32),
-            pltpu.VMEM(back.shape, F32),
-            pltpu.VMEM(back.shape, F32),
-            pltpu.SemaphoreType.DMA((36 + EXCHANGE_SLOTS,)),
-            pltpu.SemaphoreType.DMA((36 + EXCHANGE_SLOTS,)),
+            pltpu.SemaphoreType.DMA((OTHER + 4,)),
+            pltpu.SemaphoreType.DMA((OTHER + 4,)),
         ],
         compiler_params=pltpu.CompilerParams(
-            collective_id=2, has_side_effects=True, vmem_limit_bytes=VMEM_LIMIT
+            collective_id=1, has_side_effects=True, vmem_limit_bytes=VMEM_LIMIT
         ),
-    )(buffer, basis, back)
-    return p, g.reshape(RANK, RANK), bt, bt_sib, back_all
+    )(inputs, gain, out_grad, weight, moment, right_basis)
 
 
 def chol_kernel(g_ref, p_ref, o_ref, s_ref, w_ref):
@@ -638,7 +707,7 @@
             wait_recv(ngbuf.at[i], nr.at[i], tensor=zs[i])
             total = total + ngbuf[i]
         std = std_ref[...]
-        scaled = total * gain_ref[...]
+        scaled = total * gain_ref[z]
         lane = lax.broadcasted_iota(jnp.int32, (32, 128), 1)
 
         def per_token(v):
@@ -661,8 +730,10 @@
         sums = stat[0]
         for i in range(1, 8):
             sums = sums + stat[i]
-        sums = sums * (1.0 / (32 * 192))
-        ig_ref[...] = (inv_ref[...] * (scaled - sums[:, 0:1] - std * sums[:, 64:65])).astype(BF16)
+        sums = sums * (1.0 / (16 * 384))
+        full = inv_ref[...] * (scaled - sums[:, 0:1] - std * sums[:, 64:65])
+        ig_ref[:, 0:384] = full[0].astype(BF16)
+        ig_ref[:, 384:768] = full[1].astype(BF16)
         yield
         for i in range(3):
             wait_recv(gy.at[(y + 3 - i) % 4], nr.at[17 + i], dp=sib)
@@ -670,7 +741,8 @@
         sent.append(send(gc.at[core], gc.at[core], ns.at[20], nr.at[20], dp=sib))
         yield
         wait_recv(gc.at[1 - core], nr.at[20], dp=sib)
-        gg_ref[...] = gc[0] + gc[1]
+        gg_ref[:, 0:384] = gc[0, 0] + gc[1, 0]
+        gg_ref[:, 384:768] = gc[0, 1] + gc[1, 1]
         yield
 
     def loc(s):
@@ -701,8 +773,8 @@
             jax.ShapeDtypeStruct((2688, RANK), BF16),
             jax.ShapeDtypeStruct((84, RANK), F32),
             jax.ShapeDtypeStruct((8, RANK), F32),
-            jax.ShapeDtypeStruct(block, BF16),
-            jax.ShapeDtypeStruct((4, 8, 192), F32),
+            jax.ShapeDtypeStruct((32, 768), BF16),
+            jax.ShapeDtypeStruct((8, 768), F32),
         ),
         in_specs=[vm] * 7,
         out_specs=(vm,) * 5,
@@ -724,9 +796,9 @@
             pltpu.VMEM((2, 8, 256), F32),
             pltpu.VMEM((7,) + block, F32),
             pltpu.VMEM((8, 32, 128), F32),
-            pltpu.VMEM((4, 4, 8, 192), F32),
-            pltpu.VMEM((4, 4, 8, 192), F32),
-            pltpu.VMEM((2, 4, 8, 192), F32),
+            pltpu.VMEM((4, 2, 8, 384), F32),
+            pltpu.VMEM((4, 2, 8, 384), F32),
+            pltpu.VMEM((2, 2, 8, 384), F32),
             pltpu.SemaphoreType.DMA((39,)),
             pltpu.SemaphoreType.DMA((39,)),
             pltpu.SemaphoreType.DMA((2 * GATHER_SLOTS,)),
@@ -740,89 +812,83 @@
     )(bt, bt_sib, ortho, back, standard, gain, inv_std)
 
 
-def final_kernel(o_ref, inv_ref, c_ref, buf_ref, scale_ref, mom_ref, upd_ref, lhs):
+def final_kernel(group, qkv_scale, mlp_scale, o_ref, csq_ref, c_ref, buf_ref, cown_ref, ig_ref, gg_ref,
+                 mom_ref, upd_ref, basis_ref, igo_ref, ggo_ref, lhs):
     rows = o_ref.shape[0]
-
-    @pl.when(pl.program_id(0) == 0)
+    step = pl.program_id(0)
+
+    @pl.when(step == 0)
     def _():
+        inv = 1.0 / (jnp.sqrt(csq_ref[0:1]) + 1e-08)
         o = o_ref[...]
-        oi = o * inv_ref[...]
         lhs[0:rows, :] = o.astype(BF16)
-        top, low = split(oi)
+        top, low = split(o * inv)
         lhs[rows:2 * rows, :] = top
         lhs[2 * rows:3 * rows, :] = low
+        basis_ref[...] = cown_ref[...] * inv
+        igo_ref[...] = ig_ref[...]
+        ggo_ref[...] = gg_ref[0:1]
 
     out = lax.dot_general(lhs[...], c_ref[...], (((1,), (1,)), ((), ())), preferred_element_type=F32)
+    tile = out.shape[1]
+    position = lax.broadcasted_iota(jnp.int32, (1, tile), 1) + step * tile
+    scale = jnp.where(position < group, qkv_scale, mlp_scale)
     mom_ref[...] = buf_ref[...] - (1.0 - MOMENTUM) * out[0:rows]
-    upd_ref[...] = (out[rows:2 * rows] + out[2 * rows:3 * rows]) * scale_ref[...]
-
-
-def final_products(o, inv, coeffs, buffer, scale):
+    upd_ref[...] = (out[rows:2 * rows] + out[2 * rows:3 * rows]) * scale
+
+
+def final_products(o, squares, coeffs, buffer, coeff_own, input_grad, gain_grad, *scales):
     rows, cols = buffer.shape
     tile = 896
+
+    def whole(v):
+        return pl.BlockSpec(v.shape, lambda i: (0,) * v.ndim)
+
+    by_col = pl.BlockSpec((rows, tile), lambda i: (0, i))
+    gain_out = jax.ShapeDtypeStruct((1, gain_grad.shape[1]), F32)
     return pl.pallas_call(
-        final_kernel,
+        lambda *refs: final_kernel(*scales, *refs),
         grid=(cols // tile,),
-        out_shape=(jax.ShapeDtypeStruct(buffer.shape, F32), jax.ShapeDtypeStruct(buffer.shape, F32)),
+        out_shape=(
+            jax.ShapeDtypeStruct(buffer.shape, F32),
+            jax.ShapeDtypeStruct(buffer.shape, F32),
+            jax.ShapeDtypeStruct(coeff_own.shape, F32),
+            jax.ShapeDtypeStruct(input_grad.shape, BF16),
+            gain_out,
+        ),
         in_specs=[
-            pl.BlockSpec((rows, RANK), lambda i: (0, 0)),
-            pl.BlockSpec((1, RANK), lambda i: (0, 0)),
+            whole(o),
+            whole(squares),
             pl.BlockSpec((tile, RANK), lambda i: (i, 0)),
-            pl.BlockSpec((rows, tile), lambda i: (0, i)),
-            pl.BlockSpec((1, tile), lambda i: (0, i)),
+            by_col,
+            whole(coeff_own),
+            whole(input_grad),
+            whole(gain_grad),
         ],
-        out_specs=(pl.BlockSpec((rows, tile), lambda i: (0, i)), pl.BlockSpec((rows, tile), lambda i: (0, i))),
+        out_specs=(by_col, by_col, whole(coeff_own), whole(input_grad), whole(gain_out)),
         scratch_shapes=[pltpu.VMEM((3 * rows, RANK), BF16)],
         compiler_params=pltpu.CompilerParams(vmem_limit_bytes=VMEM_LIMIT),
-    )(o, inv, coeffs, buffer, scale)
+    )(o, squares, coeffs, buffer, coeff_own, input_grad, gain_grad)
 
 
 def per_device(inputs, norm_gain, out_grad, weight, moment, right_basis):
     tensor_count = lax.axis_size("tensor")
-    tensor_index = lax.axis_index("tensor")
-    width = inputs.shape[1]
-    group_cols = weight.shape[1]
-    widened = inputs.astype(F32)
-    row_mean = jnp.mean(widened, axis=1, keepdims=True)
-    centered = widened - row_mean
-    row_var = jnp.mean(centered * centered, axis=1, keepdims=True)
-    inv_std = lax.rsqrt(row_var + NORM_EPSILON)
-    standard = centered * inv_std
-    normed = (standard * norm_gain).astype(BF16)
-    tokens, features = inputs.shape[0], weight.shape[0]
-    to_owners = normed.reshape(tokens, 4, 4, 2, features).transpose(1, 2, 3, 0, 4)
-    basis_all, shard_in, feature_block = gather_both(right_basis, out_grad, to_owners)
-    grad_acc = lax.dot_general(
-        feature_block.reshape(32 * tokens, features), shard_in, (((0,), (0,)), ((), ())), preferred_element_type=F32
-    )
-    buffer = moment + grad_acc
-    back_rows = lax.dot_general(shard_in, weight, (((1,), (1,)), ((), ())), preferred_element_type=F32)
-    projected, gram, bt, bt_sib, back_all = projected_gram(
-        buffer, basis_all, back_rows.reshape(4, 4, 2, tokens, features)
-    )
-    ortho = chol_solve(gram, projected)
-    share_cols = width // tensor_count
-    share_blocks = share_cols // features
-
-    def here(v):
-        own = lax.dynamic_slice_in_dim(v, tensor_index * share_cols, share_cols, 1)
-        return own.reshape(v.shape[0], share_blocks, features).transpose(1, 0, 2)
-
+    gain = norm_gain[None, :]
+    projected, gram, bt, bt_sib, buffer, back_all, standard, inv_std = front(
+        inputs, gain, out_grad, weight, moment, right_basis
+    )
+    ortho = chol_solve(gram.reshape(RANK, RANK), projected)
     coeffs, coeff_own, squares, input_grad, gain_grad = coeff_sum(
-        bt, bt_sib, ortho, back_all.reshape(tensor_count, share_blocks, tokens, features),
-        here(standard), here(norm_gain[None, :]), jnp.broadcast_to(inv_std, (tokens, features)),
-    )
-    input_grad = input_grad.transpose(1, 0, 2).reshape(tokens, share_cols)
-    gain_grad = gain_grad[:, 0].reshape(share_cols)
-    col_inverse = 1.0 / (jnp.sqrt(squares[0:1]) + 1e-08)
-    basis_new = coeff_own * col_inverse
+        bt, bt_sib, ortho, back_all.reshape(tensor_count, 2, inputs.shape[0], 384),
+        standard, gain.reshape(tensor_count, 2, 1, 384), inv_std,
+    )
     qkv_group = 3 * HEADS * HEAD_DIM // tensor_count
     qkv_scale = 0.2 * math.sqrt(D * (3 * HEADS * HEAD_DIM) / RANK)
     mlp_scale = 0.2 * math.sqrt(D * FF / RANK)
-    position = jnp.arange(group_cols, dtype=jnp.int32)
-    col_scale = jnp.where(position < qkv_group, qkv_scale, mlp_scale).astype(F32)
-    moment_new, update = final_products(ortho, col_inverse, coeffs, buffer, col_scale[None, :])
-    return (input_grad, gain_grad, moment_new, basis_new, update)
+    moment_new, update, basis_new, input_grad, gain_grad = final_products(
+        ortho, squares, coeffs, buffer, coeff_own, input_grad, gain_grad, qkv_group, qkv_scale, mlp_scale
+    )
+    return (input_grad, gain_grad.reshape(gain_grad.shape[1]), moment_new, basis_new, update)
 
 
 def solution(mesh):

time: 227 us -> 187 us (0.82)
  Pallas kernels: 203 us -> 185 us
  matrix products: 8.02 us -> 0 us
  local copies, waits for them, and re-layouts: 7.88 us -> 0 us
  other arithmetic: 6.31 us -> 1.28 us
    pallas_call x3 -> x2, Pallas kernels: 126 us -> 112 us  [the longest x1 106 us: front(): pl.pallas_call(front_kernel, out_shape=(jax.ShapeDtypeStruct((rows, RANK)...]
    dot_general x2 -> x0, matrix products: 8.02 us -> none  [the longest x1 5.34 us: per_device(): lax.dot_general(shard_in, weight, (((1,), (1,)), ((), ())), preferred_ele...]
    pallas_call x1, Pallas kernels: 53.7 us -> 49 us  [coeff_sum(): pl.pallas_call(coeff_kernel, out_shape=(jax.ShapeDtypeStruct((2688, RANK)...]
    reshape x5 -> x0, local copies, waits for them, and re-layouts: 3.31 us -> none  [the longest x2 1.77 us: per_device(): normed.reshape(tokens, 4, 4, 2, features).transpose(1, 2, 3, 0, 4)]
    reduce_sum x2 -> x0, other arithmetic: 2.52 us -> none  [the longest x1 1.28 us: per_device(): row_var = jnp.mean(centered * centered, axis=1, keepdims=True)]
where the time goes in v3:
time: 187 us
  Pallas kernels  185 us (99%)
    pallas_call x1, Pallas kernels, front(): pl.pallas_call(front_kernel, out_shape=(jax.ShapeDtypeStruct((rows, RANK)...  106 us
    pallas_call x1, Pallas kernels, coeff_sum(): pl.pallas_call(coeff_kernel, out_shape=(jax.ShapeDtypeStruct((2688, RANK)...  49 us
    pallas_call x1, Pallas kernels, chol_solve(): pl.pallas_call(chol_kernel, out_shape=jax.ShapeDtypeStruct(projected.shap...  23.2 us
    pallas_call x1, Pallas kernels, final_products(): pl.pallas_call(lambda *refs: final_kernel(*scales, *refs), grid=(cols //...  6.42 us

profile of v3, /device:TPU:1, one launch (start us, length us, event | category | flops | bytes accessed | tf_op | source)
XLA Modules:
  0.0 186.5 jit_solution(3690605185741769094)
XLA Ops:
  0.6 105.9 %shard_map.101 = (f32[192,512]{1,0:T(8,128)}, f32[8,2,4,8,512]{4,3,2,1,0:T(8,128)}, bf16[2688,384]{1,0:T(8,128)(2,1)}, bf16[2688,384]{1,0:T(8,128)(2,1)}, f32[19...) custom-call(bf16[32,6144]{1,0:T(8,128)(2,1)} %in_ref.1, ...), custom_call_target="tpu_custom_call" | custom-call | tf_op jit(solution)/shard_map/pallas_call | solution.py:420
  106.6 23.2 %shard_map.102.o_ref.refs_0_ = f32[192,512]{1,0:T(8,128)} custom-call(f32[512,512]{1,0:T(8,128)} %bitcast.4, f32[192,512]{1,0:T(8,128)} %get-tuple-element.24.p_ref), custom_call_target="tpu_custom_call" | custom-call | tf_op jit(solution)/shard_map/pallas_call | solution.py:531
  129.8 49.0 %shard_map.103 = (bf16[2688,512]{1,0:T(8,128)(2,1)}, f32[84,512]{1,0:T(8,128)}, f32[8,512]{1,0:T(8,128)}, bf16[32,768]{1,0:T(8,128)(2,1)}, f32[8,768]{1,0:T(8,128)}) custom-call(bf16[2688,384]{1,0:T(8,128)(2,1)} %get-tuple-element.25.bt_ref, bf16[2688,384]{1,0:T(8,128)(2,1)} %get-tuple-element.26.btsib_ref, f32[192,512]{1,0:T(8,128)} %shard_map.102.o_ref.refs_0_, ...), custom_call_target="tpu_custom_call" | custom-call | tf_op jit(solution)/shard_map/pallas_call | solution.py:770
  178.8 6.4 %shard_map.104 = (f32[192,2688]{1,0:T(8,128)}, f32[192,2688]{1,0:T(8,128)}, f32[84,512]{1,0:T(8,128)}, bf16[32,768]{1,0:T(8,128)(2,1)}, f32[1,768]{1,0:T(1,128)}) custom-call(f32[192,512]{1,0:T(8,128)} %shard_map.102.o_ref.refs_0_, f32[8,512]{1,0:T(8,128)} %get-tuple-element.30.refs_1_, bf16[2688,512]{1,0:T(8,128)(2,1)} %get-tuple-element.31.refs_2_, ...), custom_call_target="tpu_custom_call" | custom-call | tf_op jit(solution)/shard_map/pallas_call | solution.py:849
  185.2 1.3 reduce

commit v4 on v3

--- a/solution.py
+++ b/solution.py
@@ -195,7 +195,7 @@
 
 EX = 4 * GATHER_SLOTS
 ZP = EX + 28
-OTHER = ZP + 35
+OTHER = ZP + 39
 
 
 def front_kernel(in_ref, gain_ref, g_ref, w_ref, m_ref, r_ref,
@@ -286,6 +286,13 @@
         yield
 
     def compute():
+        for c in (0, 1):
+            for q in (0, 256):
+                bk[c, q:q + 256, 0:192] = lax.dot_general(
+                    gall[c, q:q + 256, :], w_ref[...], (((1,), (1,)), ((), ())), preferred_element_type=F32
+                )
+                yield
+        sent.append(send(bk.at[1 - core], bksib, ssem.at[OTHER + 3], rsem.at[OTHER + 3], dp=sib))
         for t in range(0, cols, 384):
             acc = m_ref[:, t:t + 384]
             for c in (0, 1):
@@ -297,13 +304,13 @@
             bt_ref[t:t + 384, :] = jnp.concatenate([top, low], axis=0).astype(F32).T.astype(BF16)
             yield
         sent.append(send(bt_ref, btsib_ref, ssem.at[OTHER + 2], rsem.at[OTHER + 2], dp=sib))
-        for c in (0, 1):
-            for q in (0, 256):
-                bk[c, q:q + 256, 0:192] = lax.dot_general(
-                    gall[c, q:q + 256, :], w_ref[...], (((1,), (1,)), ((), ())), preferred_element_type=F32
-                )
-                yield
-        sent.append(send(bk.at[1 - core], bksib, ssem.at[OTHER + 3], rsem.at[OTHER + 3], dp=sib))
+        wait_recv(bksib, rsem.at[OTHER + 3], dp=sib)
+        for q in range(4):
+            ours = bk[core, 128 * q:128 * q + 128, 0:192]
+            their = bksib[128 * q:128 * q + 128, 0:192]
+            bsrc[q] = jnp.concatenate(
+                [jnp.where(core == 0, ours, their), jnp.where(core == 0, their, ours)], axis=1
+            ).reshape(4, tokens, 384)
         yield
 
     bk[:, :, 128:256] = jnp.zeros((2, 512, 128), F32)
@@ -311,7 +318,6 @@
     work = compute()
     r_live, g_live, x_live = r_streams, g_streams, ex
     r_live = run(r_live)
-    turn = 0
     tail_live = [tail]
     while g_live or x_live or tail_live:
         g_live = run(g_live)
@@ -319,9 +325,7 @@
             x_live = run(x_live)
         elif tail_live:
             tail_live = run(tail_live)
-        turn += 1
-        if turn % 2:
-            r_live = run(r_live)
+        r_live = run(r_live)
     work_live = [work]
     while r_live or work_live:
         r_live = run(r_live)
@@ -342,13 +346,6 @@
     for i in order:
         sent.append(send(part.at[rows24(zs[i])], zbuf.at[i], ssem.at[ZP + i], rsem.at[ZP + i], tensor=zs[i]))
 
-    wait_recv(bksib, rsem.at[OTHER + 3], dp=sib)
-    for q in range(4):
-        ours = bk[core, 128 * q:128 * q + 128, 0:192]
-        their = bksib[128 * q:128 * q + 128, 0:192]
-        bsrc[q] = jnp.concatenate(
-            [jnp.where(core == 0, ours, their), jnp.where(core == 0, their, ours)], axis=1
-        ).reshape(4, tokens, 384)
     back = [exchange_stream(bsrc, bmid, backall_ref, s, ssem, rsem, EX + 14 + 7 * s, sent) for s in (0, 1)]
     back = run(back)
 
@@ -391,23 +388,22 @@
         wait_recv(ybuf.at[(y + 3 - i) % 4], rsem.at[ZP + 18 + i], dp=sib)
     gram_ref[z, core, x] = (ybuf[0] + ybuf[1]) + (ybuf[2] + ybuf[3])
     mine = gram_ref.at[z, core, x]
+    for i in range(3):
+        sent.append(send(mine, mine, ssem.at[ZP + 21 + i], rsem.at[ZP + 21 + i], dp=dp_of(xs[i], y, core)))
+    for i in range(3):
+        wait_recv(gram_ref.at[z, core, (x + 3 - i) % 4], rsem.at[ZP + 21 + i], dp=sib)
+    mine = gram_ref.at[z, core]
     for i in order:
-        sent.append(send(mine, mine, ssem.at[ZP + 21 + i], rsem.at[ZP + 21 + i], tensor=zs[i]))
+        sent.append(send(mine, mine, ssem.at[ZP + 24 + i], rsem.at[ZP + 24 + i], tensor=zs[i]))
+    sent.append(send(mine, mine, ssem.at[ZP + 31], rsem.at[ZP + 31], dp=sib))
     for i in reversed(order):
-        wait_recv(gram_ref.at[(z + 7 - i) % 8, core, x], rsem.at[ZP + 21 + i], tensor=zs[i])
-    mine = gram_ref.at[:, core, x]
-    for i in range(3):
-        sent.append(send(mine, mine, ssem.at[ZP + 28 + i], rsem.at[ZP + 28 + i], dp=dp_of(xs[i], y, core)))
-    sent.append(send(mine, mine, ssem.at[ZP + 31], rsem.at[ZP + 31], dp=sib))
-    for i in range(3):
-        src = (x + 3 - i) % 4
-        wait_recv(gram_ref.at[:, core, src], rsem.at[ZP + 28 + i], dp=sib)
-        there = gram_ref.at[:, core, src]
+        there = gram_ref.at[(z + 7 - i) % 8, core]
+        wait_recv(there, rsem.at[ZP + 24 + i], tensor=zs[i])
         sent.append(send(there, there, ssem.at[ZP + 32 + i], rsem.at[ZP + 32 + i], dp=sib))
     back = run(back)
-    wait_recv(gram_ref.at[:, 1 - core, x], rsem.at[ZP + 31], dp=sib)
-    for i in range(3):
-        wait_recv(gram_ref.at[:, 1 - core, (x + 3 - i) % 4], rsem.at[ZP + 32 + i], dp=sib)
+    wait_recv(gram_ref.at[z, 1 - core], rsem.at[ZP + 31], dp=sib)
+    for i in reversed(order):
+        wait_recv(gram_ref.at[(z + 7 - i) % 8, 1 - core], rsem.at[ZP + 32 + i], dp=sib)
     wait_recv(btsib_ref, rsem.at[OTHER + 2], dp=sib)
     for copy in sent:
         copy.wait_send()
@@ -493,7 +489,7 @@
                 u = {}
                 for q in range(p + 1, 8):
                     u[q] = row_splat(c[q], p)
-                    c[q] = c[q] - m * u[q]
+                    c[q] = c[q] - (c[p] * u[q]) * ip
                 r = row_splat(x, p)
                 x = x - m * r
                 inv.append(ip)
@@ -605,63 +601,44 @@
     def padded(v):
         return jnp.concatenate([v, zero_pad], axis=0).astype(BF16)
 
-    def reduce_stream(s):
-        base = 8 + 8 * s
+    def reduce_direct(s):
+        base = 8 + 6 * s
         a, b = a0[s], b0[s]
-        right, left = dev(s, a + 1, b), dev(s, a - 1, b)
-        for j in range(4):
-            sbuf[s, 0, j] = padded(own(s, 2, j))
-        sent.append(send(sbuf.at[s, 0, 0:2], rbuf.at[s, 0, 0:2], ssem.at[base], rsem.at[base], dp=right))
-        sent.append(send(sbuf.at[s, 0, 2:4], rbuf.at[s, 0, 2:4], ssem.at[base + 1], rsem.at[base + 1], dp=left))
-        yield
-        for j in (2, 3):
-            sbuf[s, 1, j] = padded(own(s, 1, j))
-        for j in (0, 1):
-            sbuf[s, 2, j] = padded(own(s, 3, j))
-        yield
-        wait_recv(rbuf.at[s, 0, 0:2], rsem.at[base], dp=left)
-        for j in (0, 1):
-            sbuf[s, 1, j] = padded(own(s, 1, j) + rbuf[s, 0, j, 0:168].astype(F32))
-        sent.append(send(sbuf.at[s, 1], rbuf.at[s, 1], ssem.at[base + 2], rsem.at[base + 2], dp=right))
-        yield
-        wait_recv(rbuf.at[s, 0, 2:4], rsem.at[base + 1], dp=right)
-        for j in (2, 3):
-            sbuf[s, 2, j] = padded(own(s, 3, j) + rbuf[s, 0, j, 0:168].astype(F32))
-        sent.append(send(sbuf.at[s, 2], rbuf.at[s, 2], ssem.at[base + 3], rsem.at[base + 3], dp=left))
-        yield
+        offs = (2, 1, 3)
+        for i in range(3):
+            for j in range(4):
+                sbuf[s, i, j] = padded(own(s, offs[i], j))
+            sent.append(send(
+                sbuf.at[s, i], rbuf.at[s, i], ssem.at[base + i], rsem.at[base + i], dp=dev(s, a + offs[i], b)
+            ))
+            yield
         for j in range(4):
             acc[s, j] = own(s, 0, j)
-        yield
-        wait_recv(rbuf.at[s, 1], rsem.at[base + 2], dp=left)
-        wait_recv(rbuf.at[s, 2], rsem.at[base + 3], dp=right)
+        for i in (1, 2, 0):
+            wait_recv(rbuf.at[s, i], rsem.at[base + i], dp=sib)
+        yield
 
         def summed(off):
             j = (b + off) % 4
-            return acc[s, j] + (rbuf[s, 1, j, 0:168].astype(F32) + rbuf[s, 2, j, 0:168].astype(F32))
-
-        right, left = dev(s, a, b + 1), dev(s, a, b - 1)
-        s2[s, 0] = padded(summed(2))
-        sent.append(send(s2.at[s, 0, 0:96], r2.at[s, 0, 0:96], ssem.at[base + 4], rsem.at[base + 4], dp=right))
-        sent.append(send(s2.at[s, 0, 96:176], r2.at[s, 0, 96:176], ssem.at[base + 5], rsem.at[base + 5], dp=left))
-        yield
-        one, three, zero = summed(1), summed(3), summed(0)
-        wait_recv(r2.at[s, 0, 0:96], rsem.at[base + 4], dp=left)
-        s2[s, 1, 0:96] = (one[0:96] + r2[s, 0, 0:96].astype(F32)).astype(BF16)
-        s2[s, 1, 96:176] = padded(one[96:168])
-        sent.append(send(s2.at[s, 1], r2.at[s, 1], ssem.at[base + 6], rsem.at[base + 6], dp=right))
-        wait_recv(r2.at[s, 0, 96:176], rsem.at[base + 5], dp=right)
-        s2[s, 2, 0:96] = three[0:96].astype(BF16)
-        s2[s, 2, 96:176] = padded(three[96:168] + r2[s, 0, 96:168].astype(F32))
-        sent.append(send(s2.at[s, 2], r2.at[s, 2], ssem.at[base + 7], rsem.at[base + 7], dp=left))
-        yield
-        wait_recv(r2.at[s, 1], rsem.at[base + 6], dp=left)
-        wait_recv(r2.at[s, 2], rsem.at[base + 7], dp=right)
-        total = zero + (r2[s, 1, 0:168].astype(F32) + r2[s, 2, 0:168].astype(F32))
+            return (acc[s, j] + rbuf[s, 0, j, 0:168].astype(F32)) + (
+                rbuf[s, 1, j, 0:168].astype(F32) + rbuf[s, 2, j, 0:168].astype(F32)
+            )
+
+        for i in range(3):
+            s2[s, i] = padded(summed(offs[i]))
+            sent.append(send(
+                s2.at[s, i], r2.at[s, i], ssem.at[base + 3 + i], rsem.at[base + 3 + i], dp=dev(s, a, b + offs[i])
+            ))
+        yield
+        total = summed(0)
+        for i in (1, 2, 0):
+            wait_recv(r2.at[s, i], rsem.at[base + 3 + i], dp=sib)
+            total = total + r2[s, i, 0:168].astype(F32)
         fin[:, 128 * s:128 * s + 128] = total
         agb[x * 4 + y, :, cols_of(core, s)] = padded(total)
         yield
 
-    round_robin([reduce_stream(0), reduce_stream(1)])
+    round_robin([reduce_direct(0), reduce_direct(1)])
 
     def norms():
         sent.append(send(fin, fsib, ssem.at[24], rsem.at[24], dp=sib))
@@ -827,7 +804,7 @@
         lhs[2 * rows:3 * rows, :] = low
         basis_ref[...] = cown_ref[...] * inv
         igo_ref[...] = ig_ref[...]
-        ggo_ref[...] = gg_ref[0:1]
+        ggo_ref[...] = gg_ref[0]
 
     out = lax.dot_general(lhs[...], c_ref[...], (((1,), (1,)), ((), ())), preferred_element_type=F32)
     tile = out.shape[1]
@@ -845,7 +822,7 @@
         return pl.BlockSpec(v.shape, lambda i: (0,) * v.ndim)
 
     by_col = pl.BlockSpec((rows, tile), lambda i: (0, i))
-    gain_out = jax.ShapeDtypeStruct((1, gain_grad.shape[1]), F32)
+    gain_out = jax.ShapeDtypeStruct((gain_grad.shape[1],), F32)
     return pl.pallas_call(
         lambda *refs: final_kernel(*scales, *refs),
         grid=(cols // tile,),
@@ -888,7 +865,7 @@
     moment_new, update, basis_new, input_grad, gain_grad = final_products(
         ortho, squares, coeffs, buffer, coeff_own, input_grad, gain_grad, qkv_group, qkv_scale, mlp_scale
     )
-    return (input_grad, gain_grad.reshape(gain_grad.shape[1]), moment_new, basis_new, update)
+    return (input_grad, gain_grad, moment_new, basis_new, update)
 
 
 def solution(mesh):

time: 187 us -> 187 us (level)
    pallas_call x1, Pallas kernels: 106 us -> 109 us  [front(): pl.pallas_call(front_kernel, out_shape=(jax.ShapeDtypeStruct((rows, RANK)...]
where the time goes in v4:
time: 187 us; the launch traced here: 186 us
  Pallas kernels  186 us (99%)
    pallas_call x1, Pallas kernels, front(): pl.pallas_call(front_kernel, out_shape=(jax.ShapeDtypeStruct((rows, RANK)...  109 us
    pallas_call x1, Pallas kernels, coeff_sum(): pl.pallas_call(coeff_kernel, out_shape=(jax.ShapeDtypeStruct((2688, RANK)...  48.5 us
    pallas_call x1, Pallas kernels, chol_solve(): pl.pallas_call(chol_kernel, out_shape=jax.ShapeDtypeStruct(projected.shap...  21.6 us
    pallas_call x1, Pallas kernels, final_products(): pl.pallas_call(lambda *refs: final_kernel(*scales, *refs), grid=(cols //...  6.41 us

profile of v4, /device:TPU:1, one launch (start us, length us, event | category | flops | bytes accessed | tf_op | source)
XLA Modules:
  0.0 186.4 jit_solution(3254307853928679528)
XLA Ops:
  0.6 109.2 %shard_map.101 = (f32[192,512]{1,0:T(8,128)}, f32[8,2,4,8,512]{4,3,2,1,0:T(8,128)}, bf16[2688,384]{1,0:T(8,128)(2,1)}, bf16[2688,384]{1,0:T(8,128)(2,1)}, f32[19...) custom-call(bf16[32,6144]{1,0:T(8,128)(2,1)} %in_ref.1, ...), custom_call_target="tpu_custom_call" | custom-call | tf_op jit(solution)/shard_map/pallas_call | solution.py:416
  109.9 21.6 %shard_map.102.o_ref.refs_0_ = f32[192,512]{1,0:T(8,128)} custom-call(f32[512,512]{1,0:T(8,128)} %bitcast.4, f32[192,512]{1,0:T(8,128)} %get-tuple-element.24.p_ref), custom_call_target="tpu_custom_call" | custom-call | tf_op jit(solution)/shard_map/pallas_call | solution.py:527
  131.5 48.5 %shard_map.103 = (bf16[2688,512]{1,0:T(8,128)(2,1)}, f32[84,512]{1,0:T(8,128)}, f32[8,512]{1,0:T(8,128)}, bf16[32,768]{1,0:T(8,128)(2,1)}, f32[8,768]{1,0:T(8,128)}) custom-call(bf16[2688,384]{1,0:T(8,128)(2,1)} %get-tuple-element.25.bt_ref, bf16[2688,384]{1,0:T(8,128)(2,1)} %get-tuple-element.26.btsib_ref, f32[192,512]{1,0:T(8,128)} %shard_map.102.o_ref.refs_0_, ...), custom_call_target="tpu_custom_call" | custom-call | tf_op jit(solution)/shard_map/pallas_call | solution.py:747
  180.0 6.4 %shard_map.104 = (f32[192,2688]{1,0:T(8,128)}, f32[192,2688]{1,0:T(8,128)}, f32[84,512]{1,0:T(8,128)}, bf16[32,768]{1,0:T(8,128)(2,1)}, f32[768]{0:T(1024)}) custom-call(f32[192,512]{1,0:T(8,128)} %shard_map.102.o_ref.refs_0_, f32[8,512]{1,0:T(8,128)} %get-tuple-element.30.refs_1_, bf16[2688,512]{1,0:T(8,128)(2,1)} %get-tuple-element.31.refs_2_, ...), custom_call_target="tpu_custom_call" | custom-call | tf_op jit(solution)/shard_map/pallas_call | solution.py:826

commit v5 on v4

--- a/solution.py
+++ b/solution.py
@@ -195,21 +195,19 @@
 
 EX = 4 * GATHER_SLOTS
 ZP = EX + 28
-OTHER = ZP + 39
-
-
-def front_kernel(in_ref, gain_ref, g_ref, w_ref, m_ref, r_ref,
-                 p_ref, gram_ref, bt_ref, btsib_ref, buf_ref, backall_ref, std_ref, inv_ref,
-                 rall, gall, got, std, nrm, exmid, exout, exsib, xt, both, bk, bksib, bsrc, bmid,
-                 part, zbuf, gbuf, cbuf, xbuf, ybuf, ssem, rsem):
+OTHER = ZP + 35
+
+
+def front_steps(sent, in_ref, gain_ref, g_ref, w_ref, m_ref, r_ref,
+                p_ref, gram_ref, bt_ref, btsib_ref, buf_ref, backall_ref, std_ref, inv_ref,
+                rall, gall, got, std, nrm, exmid, exout, exsib, xt, both, bk, bksib, bsrc, bmid,
+                part, zbuf, gbuf, cbuf, xbuf, ybuf, ssem, rsem):
     x, y, core, z = place()
     chip = x * 4 + y
     sib = dp_of(x, y, 1 - core)
     xs = [(x + d) % 4 for d in (1, 2, 3)]
     ys = [(y + d) % 4 for d in (1, 2, 3)]
     zs = [(z + d) % 8 for d in range(1, 8)]
-    greet([{"tensor": q} for q in zs] + plane_peers(x, y, core))
-    sent = []
     rows, cols = m_ref.shape
     tokens, width = in_ref.shape
     cut = 1408
@@ -286,13 +284,6 @@
         yield
 
     def compute():
-        for c in (0, 1):
-            for q in (0, 256):
-                bk[c, q:q + 256, 0:192] = lax.dot_general(
-                    gall[c, q:q + 256, :], w_ref[...], (((1,), (1,)), ((), ())), preferred_element_type=F32
-                )
-                yield
-        sent.append(send(bk.at[1 - core], bksib, ssem.at[OTHER + 3], rsem.at[OTHER + 3], dp=sib))
         for t in range(0, cols, 384):
             acc = m_ref[:, t:t + 384]
             for c in (0, 1):
@@ -301,17 +292,7 @@
             top, low = split(acc)
             both[0:rows, t:t + 384] = top
             both[rows:2 * rows, t:t + 384] = low
-            bt_ref[t:t + 384, :] = jnp.concatenate([top, low], axis=0).astype(F32).T.astype(BF16)
             yield
-        sent.append(send(bt_ref, btsib_ref, ssem.at[OTHER + 2], rsem.at[OTHER + 2], dp=sib))
-        wait_recv(bksib, rsem.at[OTHER + 3], dp=sib)
-        for q in range(4):
-            ours = bk[core, 128 * q:128 * q + 128, 0:192]
-            their = bksib[128 * q:128 * q + 128, 0:192]
-            bsrc[q] = jnp.concatenate(
-                [jnp.where(core == 0, ours, their), jnp.where(core == 0, their, ours)], axis=1
-            ).reshape(4, tokens, 384)
-        yield
 
     bk[:, :, 128:256] = jnp.zeros((2, 512, 128), F32)
     tail = after_exchange()
@@ -346,6 +327,22 @@
     for i in order:
         sent.append(send(part.at[rows24(zs[i])], zbuf.at[i], ssem.at[ZP + i], rsem.at[ZP + i], tensor=zs[i]))
 
+    for c in (0, 1):
+        for q in (0, 256):
+            bk[c, q:q + 256, 0:192] = lax.dot_general(
+                gall[c, q:q + 256, :], w_ref[...], (((1,), (1,)), ((), ())), preferred_element_type=F32
+            )
+    sent.append(send(bk.at[1 - core], bksib, ssem.at[OTHER + 3], rsem.at[OTHER + 3], dp=sib))
+    for t in range(0, cols, 384):
+        bt_ref[t:t + 384, :] = both[:, t:t + 384].astype(F32).T.astype(BF16)
+    wait_recv(bksib, rsem.at[OTHER + 3], dp=sib)
+    for q in range(4):
+        ours = bk[core, 128 * q:128 * q + 128, 0:192]
+        their = bksib[128 * q:128 * q + 128, 0:192]
+        bsrc[q] = jnp.concatenate(
+            [jnp.where(core == 0, ours, their), jnp.where(core == 0, their, ours)], axis=1
+        ).reshape(4, tokens, 384)
+    sent.append(send(bt_ref, btsib_ref, ssem.at[OTHER + 2], rsem.at[OTHER + 2], dp=sib))
     back = [exchange_stream(bsrc, bmid, backall_ref, s, ssem, rsem, EX + 14 + 7 * s, sent) for s in (0, 1)]
     back = run(back)
 
@@ -388,78 +385,29 @@
         wait_recv(ybuf.at[(y + 3 - i) % 4], rsem.at[ZP + 18 + i], dp=sib)
     gram_ref[z, core, x] = (ybuf[0] + ybuf[1]) + (ybuf[2] + ybuf[3])
     mine = gram_ref.at[z, core, x]
-    for i in range(3):
-        sent.append(send(mine, mine, ssem.at[ZP + 21 + i], rsem.at[ZP + 21 + i], dp=dp_of(xs[i], y, core)))
-    for i in range(3):
-        wait_recv(gram_ref.at[z, core, (x + 3 - i) % 4], rsem.at[ZP + 21 + i], dp=sib)
-    mine = gram_ref.at[z, core]
     for i in order:
-        sent.append(send(mine, mine, ssem.at[ZP + 24 + i], rsem.at[ZP + 24 + i], tensor=zs[i]))
+        sent.append(send(mine, mine, ssem.at[ZP + 21 + i], rsem.at[ZP + 21 + i], tensor=zs[i]))
+    back = run(back)
+    for i in reversed(order):
+        wait_recv(gram_ref.at[(z + 7 - i) % 8, core, x], rsem.at[ZP + 21 + i], tensor=zs[i])
+    mine = gram_ref.at[:, core, x]
+    for i in range(3):
+        sent.append(send(mine, mine, ssem.at[ZP + 28 + i], rsem.at[ZP + 28 + i], dp=dp_of(xs[i], y, core)))
     sent.append(send(mine, mine, ssem.at[ZP + 31], rsem.at[ZP + 31], dp=sib))
-    for i in reversed(order):
-        there = gram_ref.at[(z + 7 - i) % 8, core]
-        wait_recv(there, rsem.at[ZP + 24 + i], tensor=zs[i])
+    for i in range(3):
+        src = (x + 3 - i) % 4
+        there = gram_ref.at[:, core, src]
+        wait_recv(there, rsem.at[ZP + 28 + i], dp=sib)
         sent.append(send(there, there, ssem.at[ZP + 32 + i], rsem.at[ZP + 32 + i], dp=sib))
-    back = run(back)
-    wait_recv(gram_ref.at[z, 1 - core], rsem.at[ZP + 31], dp=sib)
-    for i in reversed(order):
-        wait_recv(gram_ref.at[(z + 7 - i) % 8, 1 - core], rsem.at[ZP + 32 + i], dp=sib)
+    wait_recv(gram_ref.at[:, 1 - core, x], rsem.at[ZP + 31], dp=sib)
+    for i in range(3):
+        wait_recv(gram_ref.at[:, 1 - core, (x + 3 - i) % 4], rsem.at[ZP + 32 + i], dp=sib)
     wait_recv(btsib_ref, rsem.at[OTHER + 2], dp=sib)
-    for copy in sent:
-        copy.wait_send()
-
-
-def front(inputs, gain, out_grad, weight, moment, right_basis):
-    vm = pl.BlockSpec(memory_space=pltpu.VMEM)
-    rows, cols = moment.shape
-    tokens = inputs.shape[0]
-    return pl.pallas_call(
-        front_kernel,
-        out_shape=(
-            jax.ShapeDtypeStruct((rows, RANK), F32),
-            jax.ShapeDtypeStruct((8, 2, 4, 8, RANK), F32),
-            jax.ShapeDtypeStruct((cols, 2 * rows), BF16),
-            jax.ShapeDtypeStruct((cols, 2 * rows), BF16),
-            jax.ShapeDtypeStruct((rows, cols), F32),
-            jax.ShapeDtypeStruct((4, 4, tokens, 384), F32),
-            jax.ShapeDtypeStruct((2, tokens, 384), F32),
-            jax.ShapeDtypeStruct((tokens, 384), F32),
-        ),
-        in_specs=[vm] * 6,
-        out_specs=(vm,) * 8,
-        scratch_shapes=[
-            pltpu.VMEM((cols, RANK), F32),
-            pltpu.VMEM((2, 16 * tokens, cols), BF16),
-            pltpu.VMEM((right_basis.shape[0], 256), F32),
-            pltpu.VMEM((8, 2, tokens, 384), F32),
-            pltpu.VMEM((4, 4, tokens, 384), BF16),
-            pltpu.VMEM((2, 4, 4, 16, 384), BF16),
-            pltpu.VMEM((4, 4, tokens, 384), BF16),
-            pltpu.VMEM((4, 4, tokens, 384), BF16),
-            pltpu.VMEM((2, rows, 16 * tokens), BF16),
-            pltpu.VMEM((2 * rows, cols), BF16),
-            pltpu.VMEM((2, 16 * tokens, 256), F32),
-            pltpu.VMEM((16 * tokens, 256), F32),
-            pltpu.VMEM((4, 4, tokens, 384), F32),
-            pltpu.VMEM((2, 4, 4, 16, 384), F32),
-            pltpu.VMEM((rows, RANK), F32),
-            pltpu.VMEM((7, 24, RANK), F32),
-            pltpu.VMEM((128, RANK), F32),
-            pltpu.VMEM((32, RANK), F32),
-            pltpu.VMEM((3, 8, RANK), F32),
-            pltpu.VMEM((4, 8, RANK), F32),
-            pltpu.SemaphoreType.DMA((OTHER + 4,)),
-            pltpu.SemaphoreType.DMA((OTHER + 4,)),
-        ],
-        compiler_params=pltpu.CompilerParams(
-            collective_id=1, has_side_effects=True, vmem_limit_bytes=VMEM_LIMIT
-        ),
-    )(inputs, gain, out_grad, weight, moment, right_basis)
-
-
-def chol_kernel(g_ref, p_ref, o_ref, s_ref, w_ref):
+
+
+def chol_steps(g_ref, p_ref, o_ref, s_ref, w_ref):
     n_p = p_ref.shape[0]
-    s_ref[:, 0:512] = g_ref[...]
+    s_ref[:, 0:512] = g_ref[...].reshape(512, 512)
     s_ref[:, 512:512 + n_p] = p_ref[...].T
     s_ref[:, 512 + n_p:] = jnp.zeros((512, s_ref.shape[1] - 512 - n_p), F32)
     lane = lax.broadcasted_iota(jnp.int32, (8, 128), 1)
@@ -473,9 +421,10 @@
 
     def block(kb, carry):
         base = pl.multiple_of(kb * 128, 128)
-        tiles = [s_ref[pl.ds(pl.multiple_of(base + 8 * i, 8), 8), pl.ds(base, 128)] for i in range(16)]
+        rest = s_ref[pl.ds(base, 128), pl.ds(base, 128)]
         for k in range(16):
-            x = tiles[k]
+            x = rest[0:8]
+            below = rest[8:]
             inside = (lane >= 8 * k) & (lane < 8 * k + 8)
             c = [lane_splat(x, 8 * k + q) for q in range(8)]
             x = jnp.where(inside, (lane - 8 * k == sub).astype(F32), x)
@@ -488,24 +437,24 @@
                 m = jnp.where(sub > p, c[p] * ip, 0.0)
                 u = {}
                 for q in range(p + 1, 8):
-                    u[q] = row_splat(c[q], p)
-                    c[q] = c[q] - (c[p] * u[q]) * ip
-                r = row_splat(x, p)
+                    u[q] = c[q][p:p + 1]
+                    c[q] = c[q] - (c[p] * row_splat(c[q], p)) * ip
+                r = x[p:p + 1]
                 x = x - m * r
-                inv.append(ip)
+                inv.append(ip[0:1])
                 up.append(u)
                 rows.append(r)
             w_ref[8 * k:8 * k + 8, :] = jnp.where(lane <= sub + 8 * k, x * scale, 0.0)
-            for g in range(k + 1, 16):
-                v = tiles[g]
-                e = [lane_splat(v, 8 * k + q) for q in range(8)]
-                v = jnp.where(inside, 0.0, v)
+            if k < 15:
+                n = below.shape[0]
+                e = [jnp.broadcast_to(below[:, 8 * k + q:8 * k + q + 1], (n, 128)) for q in range(8)]
+                below = jnp.where(inside[0:1], 0.0, below)
                 for p in range(8):
                     m = e[p] * inv[p]
                     for q in range(p + 1, 8):
                         e[q] = e[q] - m * up[p][q]
-                    v = v - m * rows[p]
-                tiles[g] = v
+                    below = below - m * rows[p]
+                rest = below
         rows_k = pl.ds(base, 128)
         s_ref[rows_k, :] = jnp.dot(w_ref[...], s_ref[rows_k, :], precision=HI, preferred_element_type=F32)
         for rb in range(1, 4):
@@ -522,37 +471,18 @@
     o_ref[...] = s_ref[:, 512:512 + n_p].T
 
 
-def chol_solve(gram, projected):
-    vm = pl.BlockSpec(memory_space=pltpu.VMEM)
-    return pl.pallas_call(
-        chol_kernel,
-        out_shape=jax.ShapeDtypeStruct(projected.shape, F32),
-        in_specs=[vm, vm],
-        out_specs=vm,
-        scratch_shapes=[pltpu.VMEM((RANK, 768), F32), pltpu.VMEM((128, 128), F32)],
-        compiler_params=pltpu.CompilerParams(vmem_limit_bytes=VMEM_LIMIT),
-    )(gram, projected)
-
-
 SPLIT = ((0, 96), (96, 80), (0, 176))
 
 
-def coeff_kernel(bt_ref, btsib_ref, o_ref, back_ref, std_ref, gain_ref, inv_ref,
-                 call_ref, cown_ref, csq_ref, ig_ref, gg_ref,
-                 osib, rhs, c_ref, sbuf, rbuf, acc, s2, r2, fin, fsib, agb,
-                 xsq, ysq, zsq, sqs, ngbuf, stat, gx, gy, gc, ssem, rsem, gs, gr, ns, nr):
+def coeff_steps(sent, bt_ref, btsib_ref, o_ref, back_ref, std_ref, gain_ref, inv_ref,
+                call_ref, cown_ref, csq_ref, ig_ref, gg_ref,
+                osib, rhs, c_ref, sbuf, rbuf, acc, s2, r2, fin, fsib, agb,
+                xsq, ysq, zsq, sqs, ngbuf, stat, gx, gy, gc, ssem, rsem, gs, gr, ns, nr):
     x, y, core, z = place()
     sib = dp_of(x, y, 1 - core)
     xs = [(x + d) % 4 for d in (1, 2, 3)]
     ys = [(y + d) % 4 for d in (1, 2, 3)]
     zs = [(z + d) % 8 for d in range(1, 8)]
-    greet(
-        [{"tensor": q} for q in zs]
-        + [{"dp": dp_of(q, y, core)} for q in xs]
-        + [{"dp": dp_of(x, q, core)} for q in ys]
-        + [{"dp": sib}]
-    )
-    sent = []
     first = ("x", "y")
 
     def half(who):
@@ -560,7 +490,7 @@
 
     sent.append(send(o_ref.at[:, half(1 - core)], osib, ssem.at[0], rsem.at[0], dp=sib))
     for i in range(7):
-        sent.append(send(back_ref.at[zs[i]], ngbuf.at[i], ns.at[i], nr.at[i], tensor=zs[i]))
+        sent.append(send(back_ref.at[zs[i] // 2, pl.ds(2 * (zs[i] % 2), 2)], ngbuf.at[i], ns.at[i], nr.at[i], tensor=zs[i]))
 
     def fill(v):
         top, low = split(v)
@@ -679,12 +609,13 @@
         yield
 
     def input_grad():
-        total = back_ref[z]
+        total = back_ref[z // 2, pl.ds(2 * (z % 2), 2)]
         for i in range(7):
             wait_recv(ngbuf.at[i], nr.at[i], tensor=zs[i])
             total = total + ngbuf[i]
         std = std_ref[...]
-        scaled = total * gain_ref[z]
+        gain = gain_ref[:, pl.ds(pl.multiple_of(768 * z, 128), 768)]
+        scaled = total * jnp.stack([gain[:, 0:384], gain[:, 384:768]])
         lane = lax.broadcasted_iota(jnp.int32, (32, 128), 1)
 
         def per_token(v):
@@ -737,56 +668,116 @@
     for j in range(8):
         two = jnp.concatenate([agb[2 * j, 0:168].astype(F32), agb[2 * j + 1, 0:168].astype(F32)], axis=0)
         call_ref[336 * j:336 * j + 336, :] = two.astype(BF16)
+
+
+def whole_kernel(*refs):
+    ins, refs = refs[:6], refs[6:]
+    buf, ortho, call, cown, csq, ig, gg = refs[:7]
+    refs = refs[7:]
+    front_scratch, refs = refs[:29], refs[29:]
+    s_scr, w_scr, refs = refs[0], refs[1], refs[2:]
+    p, gram, bt, btsib, backall, stdz, inv = front_scratch[:7]
+    x, y, core, z = place()
+    greet([{"tensor": (z + d) % 8} for d in range(1, 8)] + plane_peers(x, y, core))
+    sent = []
+    front_steps(sent, *ins, p, gram, bt, btsib, buf, backall, stdz, inv, *front_scratch[7:])
+    chol_steps(gram, p, ortho, s_scr, w_scr)
+    coeff_steps(sent, bt, btsib, ortho, backall, stdz, ins[1], inv, call, cown, csq, ig, gg, *refs)
     for copy in sent:
         copy.wait_send()
 
 
-def coeff_sum(bt, bt_sib, ortho, back, standard, gain, inv_std):
+def whole(inputs, gain, out_grad, weight, moment, right_basis):
     vm = pl.BlockSpec(memory_space=pltpu.VMEM)
-    block = standard.shape
+    rows, cols = moment.shape
+    tokens = inputs.shape[0]
+    block = (2, tokens, 384)
+
+    def f32(*shape):
+        return pltpu.VMEM(shape, F32)
+
+    def bf16(*shape):
+        return pltpu.VMEM(shape, BF16)
+
+    dma = pltpu.SemaphoreType.DMA
+    front_scratch = [
+        f32(rows, RANK),
+        f32(8, 2, 4, 8, RANK),
+        bf16(cols, 2 * rows),
+        bf16(cols, 2 * rows),
+        f32(4, 4, tokens, 384),
+        f32(*block),
+        f32(tokens, 384),
+        f32(cols, RANK),
+        bf16(2, 16 * tokens, cols),
+        f32(right_basis.shape[0], 256),
+        f32(8, 2, tokens, 384),
+        bf16(4, 4, tokens, 384),
+        bf16(2, 4, 4, 16, 384),
+        bf16(4, 4, tokens, 384),
+        bf16(4, 4, tokens, 384),
+        bf16(2, rows, 16 * tokens),
+        bf16(2 * rows, cols),
+        f32(2, 16 * tokens, 256),
+        f32(16 * tokens, 256),
+        f32(4, 4, tokens, 384),
+        f32(2, 4, 4, 16, 384),
+        f32(rows, RANK),
+        f32(7, 24, RANK),
+        f32(128, RANK),
+        f32(32, RANK),
+        f32(3, 8, RANK),
+        f32(4, 8, RANK),
+        dma((OTHER + 4,)),
+        dma((OTHER + 4,)),
+    ]
+    chol_scratch = [f32(RANK, 768), f32(128, 128)]
+    coeff_scratch = [
+        f32(192, 256),
+        bf16(384, RANK),
+        f32(2688, 256),
+        bf16(2, 3, 4, 176, 128),
+        bf16(2, 3, 4, 176, 128),
+        f32(2, 4, 168, 128),
+        bf16(2, 3, 176, 128),
+        bf16(2, 3, 176, 128),
+        f32(168, 256),
+        f32(168, 256),
+        bf16(16, 176, RANK),
+        f32(4, 8, 256),
+        f32(4, 8, 256),
+        f32(8, 8, 256),
+        f32(2, 8, 256),
+        f32(7, *block),
+        f32(8, 32, 128),
+        f32(4, 2, 8, 384),
+        f32(4, 2, 8, 384),
+        f32(2, 2, 8, 384),
+        dma((39,)),
+        dma((39,)),
+        dma((2 * GATHER_SLOTS,)),
+        dma((2 * GATHER_SLOTS,)),
+        dma((21,)),
+        dma((21,)),
+    ]
     return pl.pallas_call(
-        coeff_kernel,
+        whole_kernel,
         out_shape=(
-            jax.ShapeDtypeStruct((2688, RANK), BF16),
+            jax.ShapeDtypeStruct((rows, cols), F32),
+            jax.ShapeDtypeStruct((rows, RANK), F32),
+            jax.ShapeDtypeStruct((cols, RANK), BF16),
             jax.ShapeDtypeStruct((84, RANK), F32),
             jax.ShapeDtypeStruct((8, RANK), F32),
-            jax.ShapeDtypeStruct((32, 768), BF16),
+            jax.ShapeDtypeStruct((tokens, 768), BF16),
             jax.ShapeDtypeStruct((8, 768), F32),
         ),
-        in_specs=[vm] * 7,
-        out_specs=(vm,) * 5,
-        scratch_shapes=[
-            pltpu.VMEM((192, 256), F32),
-            pltpu.VMEM((384, RANK), BF16),
-            pltpu.VMEM((2688, 256), F32),
-            pltpu.VMEM((2, 3, 4, 176, 128), BF16),
-            pltpu.VMEM((2, 3, 4, 176, 128), BF16),
-            pltpu.VMEM((2, 4, 168, 128), F32),
-            pltpu.VMEM((2, 3, 176, 128), BF16),
-            pltpu.VMEM((2, 3, 176, 128), BF16),
-            pltpu.VMEM((168, 256), F32),
-            pltpu.VMEM((168, 256), F32),
-            pltpu.VMEM((16, 176, RANK), BF16),
-            pltpu.VMEM((4, 8, 256), F32),
-            pltpu.VMEM((4, 8, 256), F32),
-            pltpu.VMEM((8, 8, 256), F32),
-            pltpu.VMEM((2, 8, 256), F32),
-            pltpu.VMEM((7,) + block, F32),
-            pltpu.VMEM((8, 32, 128), F32),
-            pltpu.VMEM((4, 2, 8, 384), F32),
-            pltpu.VMEM((4, 2, 8, 384), F32),
-            pltpu.VMEM((2, 2, 8, 384), F32),
-            pltpu.SemaphoreType.DMA((39,)),
-            pltpu.SemaphoreType.DMA((39,)),
-            pltpu.SemaphoreType.DMA((2 * GATHER_SLOTS,)),
-            pltpu.SemaphoreType.DMA((2 * GATHER_SLOTS,)),
-            pltpu.SemaphoreType.DMA((21,)),
-            pltpu.SemaphoreType.DMA((21,)),
-        ],
+        in_specs=[vm] * 6,
+        out_specs=(vm,) * 7,
+        scratch_shapes=front_scratch + chol_scratch + coeff_scratch,
         compiler_params=pltpu.CompilerParams(
-            collective_id=3, has_side_effects=True, vmem_limit_bytes=VMEM_LIMIT
+            collective_id=1, has_side_effects=True, vmem_limit_bytes=VMEM_LIMIT
         ),
-    )(bt, bt_sib, ortho, back, standard, gain, inv_std)
+    )(inputs, gain, out_grad, weight, moment, right_basis)
 
 
 def final_kernel(group, qkv_scale, mlp_scale, o_ref, csq_ref, c_ref, buf_ref, cown_ref, ig_ref, gg_ref,
@@ -818,7 +809,7 @@
     rows, cols = buffer.shape
     tile = 896
 
-    def whole(v):
+    def all_of(v):
         return pl.BlockSpec(v.shape, lambda i: (0,) * v.ndim)
 
     by_col = pl.BlockSpec((rows, tile), lambda i: (0, i))
@@ -834,15 +825,15 @@
             gain_out,
         ),
         in_specs=[
-            whole(o),
-            whole(squares),
+            all_of(o),
+            all_of(squares),
             pl.BlockSpec((tile, RANK), lambda i: (i, 0)),
             by_col,
-            whole(coeff_own),
-            whole(input_grad),
-            whole(gain_grad),
+            all_of(coeff_own),
+            all_of(input_grad),
+            all_of(gain_grad),
         ],
-        out_specs=(by_col, by_col, whole(coeff_own), whole(input_grad), whole(gain_out)),
+        out_specs=(by_col, by_col, all_of(coeff_own), all_of(input_grad), all_of(gain_out)),
         scratch_shapes=[pltpu.VMEM((3 * rows, RANK), BF16)],
         compiler_params=pltpu.CompilerParams(vmem_limit_bytes=VMEM_LIMIT),
     )(o, squares, coeffs, buffer, coeff_own, input_grad, gain_grad)
@@ -851,13 +842,8 @@
 def per_device(inputs, norm_gain, out_grad, weight, moment, right_basis):
     tensor_count = lax.axis_size("tensor")
     gain = norm_gain[None, :]
-    projected, gram, bt, bt_sib, buffer, back_all, standard, inv_std = front(
+    buffer, ortho, coeffs, coeff_own, squares, input_grad, gain_grad = whole(
         inputs, gain, out_grad, weight, moment, right_basis
-    )
-    ortho = chol_solve(gram.reshape(RANK, RANK), projected)
-    coeffs, coeff_own, squares, input_grad, gain_grad = coeff_sum(
-        bt, bt_sib, ortho, back_all.reshape(tensor_count, 2, inputs.shape[0], 384),
-        standard, gain.reshape(tensor_count, 2, 1, 384), inv_std,
     )
     qkv_group = 3 * HEADS * HEAD_DIM // tensor_count
     qkv_scale = 0.2 * math.sqrt(D * (3 * HEADS * HEAD_DIM) / RANK)

time: 187 us -> 170 us (0.909)
  Pallas kernels: 186 us -> 169 us
    pallas_call x3 -> x1, Pallas kernels: 179 us -> 163 us  [whole(): pl.pallas_call(whole_kernel, out_shape=(jax.ShapeDtypeStruct((rows, cols)...]
where the time goes in v5:
time: 170 us
  Pallas kernels  169 us (99%)
    pallas_call x1, Pallas kernels, whole(): pl.pallas_call(whole_kernel, out_shape=(jax.ShapeDtypeStruct((rows, cols)...  163 us
    pallas_call x1, Pallas kernels, final_products(): pl.pallas_call(lambda *refs: final_kernel(*scales, *refs), grid=(cols //...  6.42 us

profile of v5, /device:TPU:1, one launch (start us, length us, event | category | flops | bytes accessed | tf_op | source)
XLA Modules:
  0.0 169.8 jit_solution(12839620530895021273)
XLA Ops:
  0.6 162.7 %shard_map.101 = (f32[192,2688]{1,0:T(8,128)}, f32[192,512]{1,0:T(8,128)}, bf16[2688,512]{1,0:T(8,128)(2,1)}, f32[84,512]{1,0:T(8,128)}, f32[8,512]{1,0:T(8,128)...) custom-call(bf16[32,6144]{1,0:T(8,128)(2,1)} %refs_0_.1, f32[1,6144]{1,0:T(1,128)} %bitcast.1, bf16[32,2688]{1,0:T(8,128)(2,1)} %refs_2_.1, ...), custom_call_target="tpu_custom_call" | custom-call | tf_op jit(solution)/shard_map/pallas_call | solution.py:763
  163.4 6.4 %shard_map.102 = (f32[192,2688]{1,0:T(8,128)}, f32[192,2688]{1,0:T(8,128)}, f32[84,512]{1,0:T(8,128)}, bf16[32,768]{1,0:T(8,128)(2,1)}, f32[768]{0:T(1024)}) custom-call(f32[192,512]{1,0:T(8,128)} %get-tuple-element.17.refs_0_, f32[8,512]{1,0:T(8,128)} %get-tuple-element.18.refs_1_, bf16[2688,512]{1,0:T(8,128)(2,1)} %get-tuple-element.19.refs_2_, ...), custom_call_target="tpu_custom_call" | custom-call | tf_op jit(solution)/shard_map/pallas_call | solution.py:817

commit v6 on v5

--- a/solution.py
+++ b/solution.py
@@ -196,9 +196,10 @@
 EX = 4 * GATHER_SLOTS
 ZP = EX + 28
 OTHER = ZP + 35
-
-
-def front_steps(sent, in_ref, gain_ref, g_ref, w_ref, m_ref, r_ref,
+ZA = OTHER + 4
+
+
+def front_steps(sent, fetch, store, in_ref, gain_ref, g_ref, w_ref, m_ref, r_ref,
                 p_ref, gram_ref, bt_ref, btsib_ref, buf_ref, backall_ref, std_ref, inv_ref,
                 rall, gall, got, std, nrm, exmid, exout, exsib, xt, both, bk, bksib, bsrc, bmid,
                 part, zbuf, gbuf, cbuf, xbuf, ybuf, ssem, rsem):
@@ -284,6 +285,8 @@
         yield
 
     def compute():
+        for copy in fetch:
+            copy.wait()
         for t in range(0, cols, 384):
             acc = m_ref[:, t:t + 384]
             for c in (0, 1):
@@ -293,6 +296,7 @@
             both[0:rows, t:t + 384] = top
             both[rows:2 * rows, t:t + 384] = low
             yield
+        store.start()
 
     bk[:, :, 128:256] = jnp.zeros((2, 512, 128), F32)
     tail = after_exchange()
@@ -312,21 +316,25 @@
         r_live = run(r_live)
         work_live = run(work_live)
 
-    part[...] = jnp.zeros_like(part)
-    for t in range(0, cols, 384):
-        r_top, r_low = split(rall[t:t + 384, :])
-        one = jnp.dot(both[:, t:t + 384], r_top, preferred_element_type=F32)
-        two = jnp.dot(both[0:rows, t:t + 384], r_low, preferred_element_type=F32)
-        part[...] += one[0:rows] + (one[rows:] + two)
-
     order = (3, 4, 2, 5, 1, 6, 0)
 
     def rows24(q):
-        return pl.ds(pl.multiple_of(24 * q, 8), 24)
-
-    for i in order:
-        sent.append(send(part.at[rows24(zs[i])], zbuf.at[i], ssem.at[ZP + i], rsem.at[ZP + i], tensor=zs[i]))
-
+        return pl.ds(pl.multiple_of(24 * (q % 8), 8), 24)
+
+    halves = [slice(0, 256), slice(256, 512)]
+    for h, hc in enumerate(halves):
+        acc = jnp.zeros((rows, 256), F32)
+        for t in range(0, cols, 384):
+            r_top, r_low = split(rall[t:t + 384, hc])
+            one = jnp.dot(both[:, t:t + 384], r_top, preferred_element_type=F32)
+            two = jnp.dot(both[0:rows, t:t + 384], r_low, preferred_element_type=F32)
+            acc = acc + (one[0:rows] + (one[rows:] + two))
+        part[:, hc] = acc
+        for i in order:
+            sent.append(send(
+                part.at[rows24(zs[i]), hc], zbuf.at[i, :, hc], ssem.at[ZP + 7 * h + i], rsem.at[ZP + 7 * h + i],
+                tensor=zs[i],
+            ))
     for c in (0, 1):
         for q in (0, 256):
             bk[c, q:q + 256, 0:192] = lax.dot_general(
@@ -346,18 +354,47 @@
     back = [exchange_stream(bsrc, bmid, backall_ref, s, ssem, rsem, EX + 14 + 7 * s, sent) for s in (0, 1)]
     back = run(back)
 
-    total = part[rows24(z), :]
-    for i in reversed(order):
-        wait_recv(zbuf.at[i], rsem.at[ZP + i], tensor=zs[i])
-        total = total + zbuf[i]
-    p_ref[rows24(z), :] = total
-    mine = p_ref.at[rows24(z)]
-    for i in order:
-        sent.append(send(mine, mine, ssem.at[ZP + 7 + i], rsem.at[ZP + 7 + i], tensor=zs[i]))
+    def planes(h):
+        hc = halves[h]
+        quarters = (slice(256 * h, 256 * h + 128), slice(256 * h + 128, 256 * h + 256))
+
+        def pass_on(source, to, slot, cut=hc):
+            ref = p_ref.at[rows24(source), cut]
+            sent.append(send(ref, ref, ssem.at[ZA + 8 * h + slot], rsem.at[ZA + 8 * h + slot], tensor=(to + 8) % 8))
+
+        def arrived(source, slot, cut=hc):
+            wait_recv(p_ref.at[rows24(source + 8), cut], rsem.at[ZA + 8 * h + slot], tensor=(z + 1) % 8)
+
+        total = part[rows24(z), hc]
+        for i in reversed(order):
+            wait_recv(zbuf.at[i, :, hc], rsem.at[ZP + 7 * h + i], tensor=zs[i])
+            total = total + zbuf[i, :, hc]
+        p_ref[rows24(z), hc] = total
+        pass_on(z, z + 2, 2)
+        pass_on(z, z - 2, 3)
+        pass_on(z, z + 1, 0)
+        pass_on(z, z - 1, 1)
+        yield
+        arrived(z - 2, 2)
+        pass_on(z + 6, z + 2, 6, quarters[0])
+        pass_on(z + 6, z + 1, 4)
+        arrived(z + 2, 3)
+        pass_on(z + 2, z - 2, 7, quarters[1])
+        pass_on(z + 2, z - 1, 5)
+        yield
+        arrived(z - 1, 0)
+        arrived(z + 1, 1)
+        arrived(z - 3, 4)
+        arrived(z + 3, 5)
+        arrived(z - 4, 6, quarters[0])
+        arrived(z - 4, 7, quarters[1])
+        yield
+
+    gathers = [planes(0), planes(1)]
+    gathers = run(gathers)
     back = run(back)
-    for i in reversed(order):
-        src = (z + 7 - i) % 8
-        wait_recv(p_ref.at[rows24(src)], rsem.at[ZP + 7 + i], tensor=zs[i])
+    gathers = run(gathers)
+    gathers = run(gathers)
     gbuf[...] = lax.dot_general(
         p_ref[:, pl.ds(pl.multiple_of(128 * (z // 2), 128), 128)], p_ref[...],
         (((0,), (0,)), ((), ())), precision=HI, preferred_element_type=F32,
@@ -489,8 +526,6 @@
         return pl.ds(pl.multiple_of(256 * who, 128), 256)
 
     sent.append(send(o_ref.at[:, half(1 - core)], osib, ssem.at[0], rsem.at[0], dp=sib))
-    for i in range(7):
-        sent.append(send(back_ref.at[zs[i] // 2, pl.ds(2 * (zs[i] % 2), 2)], ngbuf.at[i], ns.at[i], nr.at[i], tensor=zs[i]))
 
     def fill(v):
         top, low = split(v)
@@ -671,17 +706,30 @@
 
 
 def whole_kernel(*refs):
-    ins, refs = refs[:6], refs[6:]
-    buf, ortho, call, cown, csq, ig, gg = refs[:7]
-    refs = refs[7:]
+    ins, refs = list(refs[:6]), refs[6:]
+    buf_out, ortho, call, cown, csq, ig, gg = refs[:7]
+    buf, weight, moment, local, refs = refs[7], refs[8], refs[9], refs[10], refs[11:]
+    fetch = [
+        pltpu.make_async_copy(ins[3], weight, local.at[0]),
+        pltpu.make_async_copy(ins[4], moment, local.at[1]),
+    ]
+    for copy in fetch:
+        copy.start()
+    ins[3], ins[4] = weight, moment
+    store = pltpu.make_async_copy(buf, buf_out, local.at[2])
     front_scratch, refs = refs[:29], refs[29:]
     s_scr, w_scr, refs = refs[0], refs[1], refs[2:]
     p, gram, bt, btsib, backall, stdz, inv = front_scratch[:7]
     x, y, core, z = place()
     greet([{"tensor": (z + d) % 8} for d in range(1, 8)] + plane_peers(x, y, core))
     sent = []
-    front_steps(sent, *ins, p, gram, bt, btsib, buf, backall, stdz, inv, *front_scratch[7:])
+    front_steps(sent, fetch, store, *ins, p, gram, bt, btsib, buf, backall, stdz, inv, *front_scratch[7:])
+    ngbuf, ns, nr = refs[15], refs[-2], refs[-1]
+    for i in (3, 4, 2, 5, 1, 6, 0):
+        to = (z + 1 + i) % 8
+        sent.append(send(backall.at[to // 2, pl.ds(2 * (to % 2), 2)], ngbuf.at[i], ns.at[i], nr.at[i], tensor=to))
     chol_steps(gram, p, ortho, s_scr, w_scr)
+    store.wait()
     coeff_steps(sent, bt, btsib, ortho, backall, stdz, ins[1], inv, call, cown, csq, ig, gg, *refs)
     for copy in sent:
         copy.wait_send()
@@ -691,6 +739,7 @@
     vm = pl.BlockSpec(memory_space=pltpu.VMEM)
     rows, cols = moment.shape
     tokens = inputs.shape[0]
+    anywhere = pl.BlockSpec(memory_space=pl.ANY)
     block = (2, tokens, 384)
 
     def f32(*shape):
@@ -728,8 +777,8 @@
         f32(32, RANK),
         f32(3, 8, RANK),
         f32(4, 8, RANK),
-        dma((OTHER + 4,)),
-        dma((OTHER + 4,)),
+        dma((ZA + 16,)),
+        dma((ZA + 16,)),
     ]
     chol_scratch = [f32(RANK, 768), f32(128, 128)]
     coeff_scratch = [
@@ -771,9 +820,9 @@
             jax.ShapeDtypeStruct((tokens, 768), BF16),
             jax.ShapeDtypeStruct((8, 768), F32),
         ),
-        in_specs=[vm] * 6,
-        out_specs=(vm,) * 7,
-        scratch_shapes=front_scratch + chol_scratch + coeff_scratch,
+        in_specs=[vm, vm, vm, anywhere, anywhere, vm],
+        out_specs=(anywhere,) + (vm,) * 6,
+        scratch_shapes=[f32(rows, cols), bf16(rows, cols), f32(rows, cols), dma((3,))] + front_scratch + chol_scratch + coeff_scratch,
         compiler_params=pltpu.CompilerParams(
             collective_id=1, has_side_effects=True, vmem_limit_bytes=VMEM_LIMIT
         ),

time: 170 us -> 165 us (0.971)
  Pallas kernels: 169 us -> 164 us
    pallas_call x1, Pallas kernels: 163 us -> 158 us  [whole(): pl.pallas_call(whole_kernel, out_shape=(jax.ShapeDtypeStruct((rows, cols)...]
where the time goes in v6:
time: 165 us
  Pallas kernels  164 us (99%)
    pallas_call x1, Pallas kernels, whole(): pl.pallas_call(whole_kernel, out_shape=(jax.ShapeDtypeStruct((rows, cols)...  158 us
    pallas_call x1, Pallas kernels, final_products(): pl.pallas_call(lambda *refs: final_kernel(*scales, *refs), grid=(cols //...  6.42 us

profile of v6, /device:TPU:1, one launch (start us, length us, event | category | flops | bytes accessed | tf_op | source)
XLA Modules:
  0.0 165.0 jit_solution(8002836312066687018)
XLA Ops:
  0.6 157.9 %shard_map.101 = (f32[192,2688]{1,0:T(8,128)}, f32[192,512]{1,0:T(8,128)}, bf16[2688,512]{1,0:T(8,128)(2,1)}, f32[84,512]{1,0:T(8,128)}, f32[8,512]{1,0:T(8,128)...) custom-call(bf16[32,6144]{1,0:T(8,128)(2,1)} %refs_0_.1, f32[1,6144]{1,0:T(1,128)} %bitcast.1, bf16[32,2688]{1,0:T(8,128)(2,1)} %refs_2_.1, ...), custom_call_target="tpu_custom_call" | custom-call | tf_op jit(solution)/shard_map/pallas_call | solution.py:812
  158.6 6.4 %shard_map.102 = (f32[192,2688]{1,0:T(8,128)}, f32[192,2688]{1,0:T(8,128)}, f32[84,512]{1,0:T(8,128)}, bf16[32,768]{1,0:T(8,128)(2,1)}, f32[768]{0:T(1024)}) custom-call(f32[192,512]{1,0:T(8,128)} %get-tuple-element.17.refs_0_, f32[8,512]{1,0:T(8,128)} %get-tuple-element.18.refs_1_, bf16[2688,512]{1,0:T(8,128)(2,1)} %get-tuple-element.19.refs_2_, ...), custom_call_target="tpu_custom_call" | custom-call | tf_op jit(solution)/shard_map/pallas_call | solution.py:866

commit v7 on v6

--- a/solution.py
+++ b/solution.py
@@ -31,11 +31,15 @@
     return dp // 8, (dp // 2) % 4, dp % 2, lax.axis_index("tensor")
 
 
-def send(src, dst, send_sem, recv_sem, **peer):
-    copy = pltpu.make_async_remote_copy(
+def copy_to(src, dst, send_sem, recv_sem, **peer):
+    return pltpu.make_async_remote_copy(
         src_ref=src, dst_ref=dst, send_sem=send_sem, recv_sem=recv_sem,
         device_id=peer, device_id_type=MESH,
     )
+
+
+def send(src, dst, send_sem, recv_sem, **peer):
+    copy = copy_to(src, dst, send_sem, recv_sem, **peer)
     copy.start()
     return copy
 
@@ -197,6 +201,7 @@
 ZP = EX + 28
 OTHER = ZP + 35
 ZA = OTHER + 4
+GP = ZA + 16
 
 
 def front_steps(sent, fetch, store, in_ref, gain_ref, g_ref, w_ref, m_ref, r_ref,
@@ -427,26 +432,45 @@
     back = run(back)
     for i in reversed(order):
         wait_recv(gram_ref.at[(z + 7 - i) % 8, core, x], rsem.at[ZP + 21 + i], tensor=zs[i])
-    mine = gram_ref.at[:, core, x]
-    for i in range(3):
-        sent.append(send(mine, mine, ssem.at[ZP + 28 + i], rsem.at[ZP + 28 + i], dp=dp_of(xs[i], y, core)))
-    sent.append(send(mine, mine, ssem.at[ZP + 31], rsem.at[ZP + 31], dp=sib))
-    for i in range(3):
-        src = (x + 3 - i) % 4
-        there = gram_ref.at[:, core, src]
-        wait_recv(there, rsem.at[ZP + 28 + i], dp=sib)
-        sent.append(send(there, there, ssem.at[ZP + 32 + i], rsem.at[ZP + 32 + i], dp=sib))
-    wait_recv(gram_ref.at[:, 1 - core, x], rsem.at[ZP + 31], dp=sib)
-    for i in range(3):
-        wait_recv(gram_ref.at[:, 1 - core, (x + 3 - i) % 4], rsem.at[ZP + 32 + i], dp=sib)
-    wait_recv(btsib_ref, rsem.at[OTHER + 2], dp=sib)
-
-
-def chol_steps(g_ref, p_ref, o_ref, s_ref, w_ref):
+    cuts = (slice(0, 2), slice(2, 8))
+
+    def along(j, i):
+        mine = gram_ref.at[cuts[j], core, x]
+        slot = GP + 7 * j + i
+        return copy_to(mine, mine, ssem.at[slot], rsem.at[slot], dp=dp_of(xs[i], y, core))
+
+    def across(j, i):
+        there = gram_ref.at[cuts[j], core, x if i == 3 else (x + 3 - i) % 4]
+        slot = GP + 7 * j + 3 + i
+        return copy_to(there, there, ssem.at[slot], rsem.at[slot], dp=sib)
+
+    def pass_rows(j):
+        for i in range(3):
+            wait_recv(gram_ref.at[cuts[j], core, (x + 3 - i) % 4], rsem.at[GP + 7 * j + i], dp=sib)
+            across(j, i).start()
+
+    def end_rows(j):
+        for i in range(4):
+            there = gram_ref.at[cuts[j], 1 - core, x if i == 3 else (x + 3 - i) % 4]
+            wait_recv(there, rsem.at[GP + 7 * j + 3 + i], dp=sib)
+            across(j, i).wait_send()
+
+    for j in (0, 1):
+        for i in range(3):
+            copy = along(j, i)
+            copy.start()
+            sent.append(copy)
+        across(j, 3).start()
+    return pass_rows, end_rows
+
+
+def chol_steps(pass_rows, end_rows, g_ref, p_ref, o_ref, s_ref, w_ref):
     n_p = p_ref.shape[0]
-    s_ref[:, 0:512] = g_ref[...].reshape(512, 512)
     s_ref[:, 512:512 + n_p] = p_ref[...].T
     s_ref[:, 512 + n_p:] = jnp.zeros((512, s_ref.shape[1] - 512 - n_p), F32)
+    pass_rows(0)
+    end_rows(0)
+    s_ref[0:128, 0:512] = g_ref[0:2].reshape(128, 512)
     lane = lax.broadcasted_iota(jnp.int32, (8, 128), 1)
     sub = lax.broadcasted_iota(jnp.int32, (8, 128), 0)
 
@@ -460,6 +484,8 @@
         base = pl.multiple_of(kb * 128, 128)
         rest = s_ref[pl.ds(base, 128), pl.ds(base, 128)]
         for k in range(16):
+            if k == 12:
+                pl.when(kb == 0)(lambda: pass_rows(1))
             x = rest[0:8]
             below = rest[8:]
             inside = (lane >= 8 * k) & (lane < 8 * k + 8)
@@ -492,6 +518,11 @@
                         e[q] = e[q] - m * up[p][q]
                     below = below - m * rows[p]
                 rest = below
+        @pl.when(kb == 0)
+        def _():
+            end_rows(1)
+            s_ref[128:512, 0:512] = g_ref[2:8].reshape(384, 512)
+
         rows_k = pl.ds(base, 128)
         s_ref[rows_k, :] = jnp.dot(w_ref[...], s_ref[rows_k, :], precision=HI, preferred_element_type=F32)
         for rb in range(1, 4):
@@ -511,7 +542,7 @@
 SPLIT = ((0, 96), (96, 80), (0, 176))
 
 
-def coeff_steps(sent, bt_ref, btsib_ref, o_ref, back_ref, std_ref, gain_ref, inv_ref,
+def coeff_steps(sent, call_out, csem, bt_ref, btsib_ref, o_ref, back_ref, std_ref, gain_ref, inv_ref,
                 call_ref, cown_ref, csq_ref, ig_ref, gg_ref,
                 osib, rhs, c_ref, sbuf, rbuf, acc, s2, r2, fin, fsib, agb,
                 xsq, ysq, zsq, sqs, ngbuf, stat, gx, gy, gc, ssem, rsem, gs, gr, ns, nr):
@@ -526,6 +557,54 @@
         return pl.ds(pl.multiple_of(256 * who, 128), 256)
 
     sent.append(send(o_ref.at[:, half(1 - core)], osib, ssem.at[0], rsem.at[0], dp=sib))
+
+    def input_grad():
+        total = back_ref[z // 2, pl.ds(2 * (z % 2), 2)]
+        for i in range(7):
+            wait_recv(ngbuf.at[i], nr.at[i], tensor=zs[i])
+            total = total + ngbuf[i]
+        std = std_ref[...]
+        gain = gain_ref[:, pl.ds(pl.multiple_of(768 * z, 128), 768)]
+        scaled = total * jnp.stack([gain[:, 0:384], gain[:, 384:768]])
+        lane = lax.broadcasted_iota(jnp.int32, (32, 128), 1)
+
+        def per_token(v):
+            return jnp.sum(jnp.sum(v, axis=0), axis=1, keepdims=True)
+
+        stat[z] = jnp.where(lane < 64, per_token(scaled), per_token(scaled * std))
+        for i in range(7):
+            sent.append(send(stat.at[z], stat.at[z], ns.at[7 + i], nr.at[7 + i], tensor=zs[i]))
+        gx[x] = jnp.broadcast_to(jnp.sum(total * std, axis=1, keepdims=True), gx.shape[1:])
+        for i in range(3):
+            sent.append(send(gx.at[x], gx.at[x], ns.at[14 + i], nr.at[14 + i], dp=dp_of(xs[i], y, core)))
+        yield
+        for i in range(3):
+            wait_recv(gx.at[(x + 3 - i) % 4], nr.at[14 + i], dp=sib)
+        gy[y] = (gx[0] + gx[1]) + (gx[2] + gx[3])
+        for i in range(3):
+            sent.append(send(gy.at[y], gy.at[y], ns.at[17 + i], nr.at[17 + i], dp=dp_of(x, ys[i], core)))
+        for i in range(7):
+            wait_recv(stat.at[(z + 7 - i) % 8], nr.at[7 + i], tensor=zs[i])
+        sums = stat[0]
+        for i in range(1, 8):
+            sums = sums + stat[i]
+        sums = sums * (1.0 / (16 * 384))
+        full = inv_ref[...] * (scaled - sums[:, 0:1] - std * sums[:, 64:65])
+        ig_ref[:, 0:384] = full[0].astype(BF16)
+        ig_ref[:, 384:768] = full[1].astype(BF16)
+        yield
+        for i in range(3):
+            wait_recv(gy.at[(y + 3 - i) % 4], nr.at[17 + i], dp=sib)
+        gc[core] = (gy[0] + gy[1]) + (gy[2] + gy[3])
+        sent.append(send(gc.at[core], gc.at[core], ns.at[20], nr.at[20], dp=sib))
+        yield
+        wait_recv(gc.at[1 - core], nr.at[20], dp=sib)
+        gg_ref[:, 0:384] = gc[0, 0] + gc[1, 0]
+        gg_ref[:, 384:768] = gc[0, 1] + gc[1, 1]
+        yield
+
+    tokens_side = input_grad()
+    next(tokens_side)
 
     def fill(v):
         top, low = split(v)
@@ -603,26 +682,29 @@
         agb[x * 4 + y, :, cols_of(core, s)] = padded(total)
         yield
 
-    round_robin([reduce_direct(0), reduce_direct(1)])
+    round_robin([reduce_direct(0), reduce_direct(1), tokens_side])
 
     def norms():
-        sent.append(send(fin, fsib, ssem.at[24], rsem.at[24], dp=sib))
         v = fin[...]
         xsq[x] = jnp.broadcast_to(jnp.sum(v * v, axis=0, keepdims=True), (8, 256))
         for i in range(3):
             sent.append(send(xsq.at[x], xsq.at[x], ssem.at[25 + i], rsem.at[25 + i], dp=dp_of(xs[i], y, core)))
+        sent.append(send(fin, fsib, ssem.at[24], rsem.at[24], dp=sib))
+        yield
         yield
         for i in range(3):
             wait_recv(xsq.at[(x + 3 - i) % 4], rsem.at[25 + i], dp=sib)
         ysq[y] = (xsq[0] + xsq[1]) + (xsq[2] + xsq[3])
         for i in range(3):
             sent.append(send(ysq.at[y], ysq.at[y], ssem.at[28 + i], rsem.at[28 + i], dp=dp_of(x, ys[i], core)))
+        yield
         yield
         for i in range(3):
             wait_recv(ysq.at[(y + 3 - i) % 4], rsem.at[28 + i], dp=sib)
         zsq[z] = (ysq[0] + ysq[1]) + (ysq[2] + ysq[3])
         for i in range(7):
             sent.append(send(zsq.at[z], zsq.at[z], ssem.at[31 + i], rsem.at[31 + i], tensor=zs[i]))
+        yield
         yield
         for i in range(7):
             wait_recv(zsq.at[(z + 7 - i) % 8], rsem.at[31 + i], tensor=zs[i])
@@ -643,51 +725,6 @@
         csq_ref[:, 256:512] = sqs[1]
         yield
 
-    def input_grad():
-        total = back_ref[z // 2, pl.ds(2 * (z % 2), 2)]
-        for i in range(7):
-            wait_recv(ngbuf.at[i], nr.at[i], tensor=zs[i])
-            total = total + ngbuf[i]
-        std = std_ref[...]
-        gain = gain_ref[:, pl.ds(pl.multiple_of(768 * z, 128), 768)]
-        scaled = total * jnp.stack([gain[:, 0:384], gain[:, 384:768]])
-        lane = lax.broadcasted_iota(jnp.int32, (32, 128), 1)
-
-        def per_token(v):
-            return jnp.sum(jnp.sum(v, axis=0), axis=1, keepdims=True)
-
-        stat[z] = jnp.where(lane < 64, per_token(scaled), per_token(scaled * std))
-        for i in range(7):
-            sent.append(send(stat.at[z], stat.at[z], ns.at[7 + i], nr.at[7 + i], tensor=zs[i]))
-        gx[x] = jnp.broadcast_to(jnp.sum(total * std, axis=1, keepdims=True), gx.shape[1:])
-        for i in range(3):
-            sent.append(send(gx.at[x], gx.at[x], ns.at[14 + i], nr.at[14 + i], dp=dp_of(xs[i], y, core)))
-        yield
-        for i in range(3):
-            wait_recv(gx.at[(x + 3 - i) % 4], nr.at[14 + i], dp=sib)
-        gy[y] = (gx[0] + gx[1]) + (gx[2] + gx[3])
-        for i in range(3):
-            sent.append(send(gy.at[y], gy.at[y], ns.at[17 + i], nr.at[17 + i], dp=dp_of(x, ys[i], core)))
-        for i in range(7):
-            wait_recv(stat.at[(z + 7 - i) % 8], nr.at[7 + i], tensor=zs[i])
-        sums = stat[0]
-        for i in range(1, 8):
-            sums = sums + stat[i]
-        sums = sums * (1.0 / (16 * 384))
-        full = inv_ref[...] * (scaled - sums[:, 0:1] - std * sums[:, 64:65])
-        ig_ref[:, 0:384] = full[0].astype(BF16)
-        ig_ref[:, 384:768] = full[1].astype(BF16)
-        yield
-        for i in range(3):
-            wait_recv(gy.at[(y + 3 - i) % 4], nr.at[17 + i], dp=sib)
-        gc[core] = (gy[0] + gy[1]) + (gy[2] + gy[3])
-        sent.append(send(gc.at[core], gc.at[core], ns.at[20], nr.at[20], dp=sib))
-        yield
-        wait_recv(gc.at[1 - core], nr.at[20], dp=sib)
-        gg_ref[:, 0:384] = gc[0, 0] + gc[1, 0]
-        gg_ref[:, 384:768] = gc[0, 1] + gc[1, 1]
-        yield
-
     def loc(s):
         def at(who, bx, by, part):
             lo, rows = SPLIT[part]
@@ -695,20 +732,28 @@
         return at
 
     round_robin([
+        norms(),
         gather_stream(loc(0), first[0], gs, gr, 0, sent),
         gather_stream(loc(1), first[1], gs, gr, GATHER_SLOTS, sent),
-        norms(),
-        input_grad(),
     ])
+    outs = []
     for j in range(8):
         two = jnp.concatenate([agb[2 * j, 0:168].astype(F32), agb[2 * j + 1, 0:168].astype(F32)], axis=0)
         call_ref[336 * j:336 * j + 336, :] = two.astype(BF16)
+        out = pltpu.make_async_copy(
+            call_ref.at[336 * j:336 * j + 336], call_out.at[336 * j:336 * j + 336], csem.at[j]
+        )
+        out.start()
+        outs.append(out)
+    for out in outs:
+        out.wait()
 
 
 def whole_kernel(*refs):
     ins, refs = list(refs[:6]), refs[6:]
-    buf_out, ortho, call, cown, csq, ig, gg = refs[:7]
-    buf, weight, moment, local, refs = refs[7], refs[8], refs[9], refs[10], refs[11:]
+    buf_out, ortho, call_out, cown, csq, ig, gg = refs[:7]
+    buf, weight, moment, local, call, csem = refs[7:13]
+    refs = refs[13:]
     fetch = [
         pltpu.make_async_copy(ins[3], weight, local.at[0]),
         pltpu.make_async_copy(ins[4], moment, local.at[1]),
@@ -723,14 +768,15 @@
     x, y, core, z = place()
     greet([{"tensor": (z + d) % 8} for d in range(1, 8)] + plane_peers(x, y, core))
     sent = []
-    front_steps(sent, fetch, store, *ins, p, gram, bt, btsib, buf, backall, stdz, inv, *front_scratch[7:])
+    pass_rows, end_rows = front_steps(sent, fetch, store, *ins, p, gram, bt, btsib, buf, backall, stdz, inv, *front_scratch[7:])
     ngbuf, ns, nr = refs[15], refs[-2], refs[-1]
     for i in (3, 4, 2, 5, 1, 6, 0):
         to = (z + 1 + i) % 8
         sent.append(send(backall.at[to // 2, pl.ds(2 * (to % 2), 2)], ngbuf.at[i], ns.at[i], nr.at[i], tensor=to))
-    chol_steps(gram, p, ortho, s_scr, w_scr)
+    chol_steps(pass_rows, end_rows, gram, p, ortho, s_scr, w_scr)
+    wait_recv(btsib, front_scratch[-1].at[OTHER + 2], dp=dp_of(x, y, 1 - core))
     store.wait()
-    coeff_steps(sent, bt, btsib, ortho, backall, stdz, ins[1], inv, call, cown, csq, ig, gg, *refs)
+    coeff_steps(sent, call_out, csem, bt, btsib, ortho, backall, stdz, ins[1], inv, call, cown, csq, ig, gg, *refs)
     for copy in sent:
         copy.wait_send()
 
@@ -777,8 +823,8 @@
         f32(32, RANK),
         f32(3, 8, RANK),
         f32(4, 8, RANK),
-        dma((ZA + 16,)),
-        dma((ZA + 16,)),
+        dma((GP + 14,)),
+        dma((GP + 14,)),
     ]
     chol_scratch = [f32(RANK, 768), f32(128, 128)]
     coeff_scratch = [
@@ -821,8 +867,10 @@
             jax.ShapeDtypeStruct((8, 768), F32),
         ),
         in_specs=[vm, vm, vm, anywhere, anywhere, vm],
-        out_specs=(anywhere,) + (vm,) * 6,
-        scratch_shapes=[f32(rows, cols), bf16(rows, cols), f32(rows, cols), dma((3,))] + front_scratch + chol_scratch + coeff_scratch,
+        out_specs=(anywhere, vm, anywhere, vm, vm, vm, vm),
+        scratch_shapes=[
+            f32(rows, cols), bf16(rows, cols), f32(rows, cols), dma((3,)), bf16(cols, RANK), dma((8,)),
+        ] + front_scratch + chol_scratch + coeff_scratch,
         compiler_params=pltpu.CompilerParams(
             collective_id=1, has_side_effects=True, vmem_limit_bytes=VMEM_LIMIT
         ),

time: 165 us -> 167 us (1.012)
  Pallas kernels: 164 us -> 166 us
where the time goes in v7:
time: 167 us; the launch traced here: 166 us
  Pallas kernels  166 us (99%)
    pallas_call x1, Pallas kernels, whole(): pl.pallas_call(whole_kernel, out_shape=(jax.ShapeDtypeStruct((rows, cols)...  159 us
    pallas_call x1, Pallas kernels, final_products(): pl.pallas_call(lambda *refs: final_kernel(*scales, *refs), grid=(cols //...  6.44 us

profile of v7, /device:TPU:1, one launch (start us, length us, event | category | flops | bytes accessed | tf_op | source)
XLA Modules:
  0.0 166.4 jit_solution(7706764664338684657)
XLA Ops:
  0.6 159.3 %shard_map.101 = (f32[192,2688]{1,0:T(8,128)}, f32[192,512]{1,0:T(8,128)}, bf16[2688,512]{1,0:T(8,128)(2,1)}, f32[84,512]{1,0:T(8,128)}, f32[8,512]{1,0:T(8,128)...) custom-call(bf16[32,6144]{1,0:T(8,128)(2,1)} %refs_0_.1, f32[1,6144]{1,0:T(1,128)} %bitcast.1, bf16[32,2688]{1,0:T(8,128)(2,1)} %refs_2_.1, ...), custom_call_target="tpu_custom_call" | custom-call | tf_op jit(solution)/shard_map/pallas_call | solution.py:858
  160.0 6.4 %shard_map.102 = (f32[192,2688]{1,0:T(8,128)}, f32[192,2688]{1,0:T(8,128)}, f32[84,512]{1,0:T(8,128)}, bf16[32,768]{1,0:T(8,128)(2,1)}, f32[768]{0:T(1024)}) custom-call(f32[192,512]{1,0:T(8,128)} %get-tuple-element.17.refs_0_, f32[8,512]{1,0:T(8,128)} %get-tuple-element.18.refs_1_, bf16[2688,512]{1,0:T(8,128)(2,1)} %get-tuple-element.19.refs_2_, ...), custom_call_target="tpu_custom_call" | custom-call | tf_op jit(solution)/shard_map/pallas_call | solution.py:914

commit v8 on v7

--- a/solution.py
+++ b/solution.py
@@ -480,12 +480,12 @@
     def row_splat(v, i):
         return jnp.broadcast_to(v[i:i + 1, :], (8, 128))
 
-    def block(kb, carry):
-        base = pl.multiple_of(kb * 128, 128)
-        rest = s_ref[pl.ds(base, 128), pl.ds(base, 128)]
+    for kb in range(4):
+        base = 128 * kb
+        rest = s_ref[base:base + 128, base:base + 128]
         for k in range(16):
-            if k == 12:
-                pl.when(kb == 0)(lambda: pass_rows(1))
+            if kb == 0 and k == 12:
+                pass_rows(1)
             x = rest[0:8]
             below = rest[8:]
             inside = (lane >= 8 * k) & (lane < 8 * k + 8)
@@ -518,24 +518,17 @@
                         e[q] = e[q] - m * up[p][q]
                     below = below - m * rows[p]
                 rest = below
-        @pl.when(kb == 0)
-        def _():
+        if kb == 0:
             end_rows(1)
             s_ref[128:512, 0:512] = g_ref[2:8].reshape(384, 512)
-
-        rows_k = pl.ds(base, 128)
-        s_ref[rows_k, :] = jnp.dot(w_ref[...], s_ref[rows_k, :], precision=HI, preferred_element_type=F32)
-        for rb in range(1, 4):
-            @pl.when(rb > kb)
-            def _():
-                ub = s_ref[rows_k, 128 * rb:128 * rb + 128]
-                s_ref[128 * rb:128 * rb + 128, 128 * rb:] -= lax.dot_general(
-                    ub, s_ref[rows_k, 128 * rb:], (((0,), (0,)), ((), ())), precision=HI,
-                    preferred_element_type=F32,
-                )
-        return carry
-
-    lax.fori_loop(0, 4, block, 0)
+        s_ref[base:base + 128, base + 128:] = jnp.dot(
+            w_ref[...], s_ref[base:base + 128, base + 128:], precision=HI, preferred_element_type=F32
+        )
+        if kb < 3:
+            s_ref[base + 128:, base + 128:] -= lax.dot_general(
+                s_ref[base:base + 128, base + 128:512], s_ref[base:base + 128, base + 128:],
+                (((0,), (0,)), ((), ())), precision=HI, preferred_element_type=F32,
+            )
     o_ref[...] = s_ref[:, 512:512 + n_p].T
 
 
@@ -604,7 +597,12 @@
         yield
 
     tokens_side = input_grad()
-    next(tokens_side)
+
+    def begin_tokens():
+        for _ in range(2):
+            yield
+        next(tokens_side)
+        yield
 
     def fill(v):
         top, low = split(v)
@@ -682,7 +680,7 @@
         agb[x * 4 + y, :, cols_of(core, s)] = padded(total)
         yield
 
-    round_robin([reduce_direct(0), reduce_direct(1), tokens_side])
+    round_robin([reduce_direct(0), reduce_direct(1), begin_tokens()])
 
     def norms():
         v = fin[...]
@@ -732,9 +730,10 @@
         return at
 
     round_robin([
-        norms(),
         gather_stream(loc(0), first[0], gs, gr, 0, sent),
         gather_stream(loc(1), first[1], gs, gr, GATHER_SLOTS, sent),
+        norms(),
+        tokens_side,
     ])
     outs = []
     for j in range(8):

time: 167 us -> 163 us (0.976)
  Pallas kernels: 166 us -> 162 us
    pallas_call x1, Pallas kernels: 159 us -> 156 us  [whole(): pl.pallas_call(whole_kernel, out_shape=(jax.ShapeDtypeStruct((rows, cols)...]
where the time goes in v8:
time: 163 us
  Pallas kernels  162 us (99%)
    pallas_call x1, Pallas kernels, whole(): pl.pallas_call(whole_kernel, out_shape=(jax.ShapeDtypeStruct((rows, cols)...  156 us
    pallas_call x1, Pallas kernels, final_products(): pl.pallas_call(lambda *refs: final_kernel(*scales, *refs), grid=(cols //...  6.41 us

profile of v8, /device:TPU:1, one launch (start us, length us, event | category | flops | bytes accessed | tf_op | source)
XLA Modules:
  0.0 163.0 jit_solution(13885038950975704751)
XLA Ops:
  0.6 155.9 %shard_map.101 = (f32[192,2688]{1,0:T(8,128)}, f32[192,512]{1,0:T(8,128)}, bf16[2688,512]{1,0:T(8,128)(2,1)}, f32[84,512]{1,0:T(8,128)}, f32[8,512]{1,0:T(8,128)...) custom-call(bf16[32,6144]{1,0:T(8,128)(2,1)} %refs_0_.1, f32[1,6144]{1,0:T(1,128)} %bitcast.1, bf16[32,2688]{1,0:T(8,128)(2,1)} %refs_2_.1, ...), custom_call_target="tpu_custom_call" | custom-call | tf_op jit(solution)/shard_map/pallas_call | solution.py:857
  156.5 6.4 %shard_map.102 = (f32[192,2688]{1,0:T(8,128)}, f32[192,2688]{1,0:T(8,128)}, f32[84,512]{1,0:T(8,128)}, bf16[32,768]{1,0:T(8,128)(2,1)}, f32[768]{0:T(1024)}) custom-call(f32[192,512]{1,0:T(8,128)} %get-tuple-element.17.refs_0_, f32[8,512]{1,0:T(8,128)} %get-tuple-element.18.refs_1_, bf16[2688,512]{1,0:T(8,128)(2,1)} %get-tuple-element.19.refs_2_, ...), custom_call_target="tpu_custom_call" | custom-call | tf_op jit(solution)/shard_map/pallas_call | solution.py:913

commit v9 on v8

--- a/solution.py
+++ b/solution.py
@@ -309,13 +309,16 @@
     r_live, g_live, x_live = r_streams, g_streams, ex
     r_live = run(r_live)
     tail_live = [tail]
+    r_turns = 7
     while g_live or x_live or tail_live:
         g_live = run(g_live)
         if x_live:
             x_live = run(x_live)
         elif tail_live:
             tail_live = run(tail_live)
-        r_live = run(r_live)
+        if r_turns:
+            r_turns -= 1
+            r_live = run(r_live)
     work_live = [work]
     while r_live or work_live:
         r_live = run(r_live)
@@ -397,8 +400,8 @@
 
     gathers = [planes(0), planes(1)]
     gathers = run(gathers)
+    gathers = run(gathers)
     back = run(back)
-    gathers = run(gathers)
     gathers = run(gathers)
     gbuf[...] = lax.dot_general(
         p_ref[:, pl.ds(pl.multiple_of(128 * (z // 2), 128), 128)], p_ref[...],

time: 163 us -> 164 us (level)
  no operation moved by 1% of the time
where the time goes in v9:
time: 164 us; the launch traced here: 163 us
  Pallas kernels  163 us (99%)
    pallas_call x1, Pallas kernels, whole(): pl.pallas_call(whole_kernel, out_shape=(jax.ShapeDtypeStruct((rows, cols)...  156 us
    pallas_call x1, Pallas kernels, final_products(): pl.pallas_call(lambda *refs: final_kernel(*scales, *refs), grid=(cols //...  6.41 us

profile of v9, /device:TPU:1, one launch (start us, length us, event | category | flops | bytes accessed | tf_op | source)
XLA Modules:
  0.0 163.4 jit_solution(4983966535865128189)
XLA Ops:
  0.6 156.3 %shard_map.101 = (f32[192,2688]{1,0:T(8,128)}, f32[192,512]{1,0:T(8,128)}, bf16[2688,512]{1,0:T(8,128)(2,1)}, f32[84,512]{1,0:T(8,128)}, f32[8,512]{1,0:T(8,128)...) custom-call(bf16[32,6144]{1,0:T(8,128)(2,1)} %refs_0_.1, f32[1,6144]{1,0:T(1,128)} %bitcast.1, bf16[32,2688]{1,0:T(8,128)(2,1)} %refs_2_.1, ...), custom_call_target="tpu_custom_call" | custom-call | tf_op jit(solution)/shard_map/pallas_call | solution.py:860
  157.0 6.4 %shard_map.102 = (f32[192,2688]{1,0:T(8,128)}, f32[192,2688]{1,0:T(8,128)}, f32[84,512]{1,0:T(8,128)}, bf16[32,768]{1,0:T(8,128)(2,1)}, f32[768]{0:T(1024)}) custom-call(f32[192,512]{1,0:T(8,128)} %get-tuple-element.17.refs_0_, f32[8,512]{1,0:T(8,128)} %get-tuple-element.18.refs_1_, bf16[2688,512]{1,0:T(8,128)(2,1)} %get-tuple-element.19.refs_2_, ...), custom_call_target="tpu_custom_call" | custom-call | tf_op jit(solution)/shard_map/pallas_call | solution.py:916
